TPU v7x, 32 devices: a whole 2x2x4 slice. The times are simulated.
32 devices in a mesh: dp: 4 (over y, x), tensor: 8 (over z, core).
Axes of the slice: x: 2, y: 2, z: 4, core: 2. Of those that a mesh axis runs over, the one named last changes fastest.
Arguments:
- tokens: bfloat16 [4096, 2048], P(('dp', 'tensor')), may hold values from -6 to 6
- segment_ids: int32 [4, 1024], P('dp'), may hold values from 0 to 3, never falling along the last dimension, each value on 1 to 512 neighbouring positions
- w_query: bfloat16 [2048, 2048], P(None, 'tensor'), may hold values from -0.125 to 0.125
- w_key: bfloat16 [2048, 2048], P(None, 'tensor'), may hold values from -0.125 to 0.125
- w_value: bfloat16 [2048, 2048], P(None, 'tensor'), may hold values from -0.125 to 0.125
- w_out: bfloat16 [2048, 2048], P('tensor'), may hold values from -0.125 to 0.125
- w_gate: bfloat16 [2048, 8192], P(None, 'tensor'), may hold values from -0.125 to 0.125
- w_up: bfloat16 [2048, 8192], P(None, 'tensor'), may hold values from -0.125 to 0.125
- w_down: bfloat16 [8192, 2048], P('tensor'), may hold values from -0.0625 to 0.0625
- q_gain: float32 [2048], P('tensor'), may hold values from 0.5 to 2, as said below
- k_gain: float32 [2048], P('tensor'), may hold values from 0.5 to 2, as said below
- attn_gain: float32 [2048], replicated, may hold values from 0.5 to 1.5
- ffn_gain: float32 [2048], replicated, may hold values from 0.5 to 1.5
- cotangent: bfloat16 [4096, 2048], P(('dp', 'tensor')), may hold values from -6 to 6
Outputs:
- block_out: bfloat16 [4096, 2048], P(('dp', 'tensor'))
- grad_tokens: float32 [4096, 2048], P(('dp', 'tensor'))
- grad_w_query: float32 [2048, 2048], P(None, 'tensor')
- grad_w_key: float32 [2048, 2048], P(None, 'tensor')
- grad_w_value: float32 [2048, 2048], P(None, 'tensor')
- grad_w_out: float32 [2048, 2048], P('tensor')
- grad_w_gate: float32 [2048, 8192], P(None, 'tensor')
- grad_w_up: float32 [2048, 8192], P(None, 'tensor')
- grad_w_down: float32 [8192, 2048], P('tensor')
- grad_q_gain: float32 [2048], P('tensor')
- grad_k_gain: float32 [2048], P('tensor')
- grad_attn_gain: float32 [2048], replicated
- grad_ffn_gain: float32 [2048], replicated
Inputs may be any that keep to these rules, and one draw needn't show every extreme that they name: `segment_ids`: within each packed sequence the segment number never falls; a segment holds 1 to 512 tokens. `q_gain`: positive gains. `k_gain`: positive gains.
All inputs are finite; a program needn't handle non-finite values.
Results may differ from a plain program's by a relative error of at most 0.017.
Values may be sent and summed in bfloat16 or wider, within the bound.
A program may use at most 256 MiB of HBM per device.

v0:
```python
import jax
import jax.numpy as jnp
from jax import lax
from jax.sharding import PartitionSpec as P

HD = 128


EPS = 1e-06
THETA = 500000.0


def rounded(value):
    return lax.optimization_barrier(value.astype(jnp.bfloat16)).astype(jnp.float32)


def dot_last(left, right):
    return lax.dot_general(
        left, right, (((1,), (1,)), ((), ())), preferred_element_type=jnp.float32
    )


def dot_first(left, right):
    return lax.dot_general(
        left, right, (((0,), (0,)), ((), ())), preferred_element_type=jnp.float32
    )


def positions_of(segment_ids):
    length = segment_ids.shape[-1]
    places = jnp.arange(length, dtype=jnp.int32)
    earlier = jnp.concatenate([segment_ids[:, :1] - 1, segment_ids[:, :-1]], axis=1)
    starts = jnp.where(segment_ids != earlier, places[None, :], jnp.zeros_like(segment_ids))
    starts = lax.cummax(starts, axis=1)
    return places[None, :] - starts


def rotary_tables(positions):
    half = HD // 2
    freq = THETA ** (-(jnp.arange(half, dtype=jnp.float32) * 2.0 / HD))
    angle = positions.astype(jnp.float32)[:, None] * freq[None, :]
    cosine = jnp.concatenate([jnp.cos(angle), jnp.cos(angle)], axis=1)
    sine = jnp.concatenate([jnp.sin(angle), jnp.sin(angle)], axis=1)
    return (cosine, sine)


def rotate(value, cosine, sine):
    half = value.shape[-1] // 2
    turned = jnp.concatenate([-value[..., half:], value[..., :half]], axis=-1)
    return value * cosine[:, None, :] + turned * sine[:, None, :]


def rotate_back(grad, cosine, sine):
    half = grad.shape[-1] // 2
    scaled = grad * sine[:, None, :]
    unturned = jnp.concatenate([scaled[..., half:], -scaled[..., :half]], axis=-1)
    return grad * cosine[:, None, :] + unturned


def norm_back(grad_out, unit, inverse, gain):
    inner = grad_out * gain
    return inverse * (inner - unit * jnp.mean(inner * unit, axis=1, keepdims=True))


def on_device(
    tokens,
    segment_ids,
    w_query,
    w_key,
    w_value,
    w_out,
    w_gate,
    w_up,
    w_down,
    q_gain,
    k_gain,
    attn_gain,
    ffn_gain,
    cotangent,
):
    row_count, full_width = tokens.shape
    head_cols = w_query.shape[1]
    heads_here = head_cols // HD
    ff_cols = w_gate.shape[1]
    seqs_here, seq_len = segment_ids.shape
    token_count = seqs_here * seq_len
    att_scale = HD ** (-0.5)
    whole_x = lax.all_gather(tokens, "tensor", axis=0, tiled=True)
    w_qkv = jnp.concatenate([w_query, w_key, w_value], axis=1)
    projected = jnp.dot(whole_x, w_qkv, preferred_element_type=jnp.float32)
    q_raw = projected[:, :head_cols]
    k_raw = projected[:, head_cols : 2 * head_cols]
    values = projected[:, 2 * head_cols :].astype(jnp.bfloat16)
    q_total, k_total = lax.psum(
        (jnp.sum(q_raw * q_raw, axis=1), jnp.sum(k_raw * k_raw, axis=1)), "tensor"
    )
    q_inverse = lax.rsqrt(q_total / full_width + EPS)[:, None]
    k_inverse = lax.rsqrt(k_total / full_width + EPS)[:, None]
    q_unit = q_raw * q_inverse
    k_unit = k_raw * k_inverse
    cosine, sine = rotary_tables(positions_of(segment_ids).reshape(token_count))
    queries = rotate((q_unit * q_gain).reshape(token_count, heads_here, HD), cosine, sine).astype(
        jnp.bfloat16
    )
    keys = rotate((k_unit * k_gain).reshape(token_count, heads_here, HD), cosine, sine).astype(
        jnp.bfloat16
    )
    shaped = (seqs_here, seq_len, heads_here, HD)
    query_seqs = queries.reshape(shaped)
    key_seqs = keys.reshape(shaped)
    value_seqs = values.reshape(shaped)
    places = jnp.arange(seq_len, dtype=jnp.int32)
    causal = places[:, None] >= places[None, :]

    def scores_of(query_block, key_block, seg_row):
        raw = (
            jnp.einsum("qhd,khd->hqk", query_block, key_block, preferred_element_type=jnp.float32)
            * att_scale
        )
        allowed = causal & (seg_row[:, None] == seg_row[None, :])
        return jnp.where(allowed[None], raw, -1e30)

    def attend(pieces):
        query_block, key_block, value_block, seg_row = pieces
        scores = scores_of(query_block, key_block, seg_row)
        top = jnp.max(scores, axis=-1, keepdims=True)
        expo = jnp.exp(scores - top)
        total = jnp.sum(expo, axis=-1, keepdims=True)
        probs = (expo / total).astype(jnp.bfloat16)
        mixed_block = jnp.einsum(
            "hqk,khd->qhd", probs, value_block, preferred_element_type=jnp.float32
        )
        return (mixed_block.astype(jnp.bfloat16), (top + jnp.log(total))[..., 0])

    mixed, log_total = lax.map(attend, (query_seqs, key_seqs, value_seqs, segment_ids))
    mixed = mixed.reshape(token_count, head_cols)
    x_rows = tokens.astype(jnp.float32)
    branch = lax.psum_scatter(
        jnp.dot(mixed, w_out, preferred_element_type=jnp.float32),
        "tensor",
        scatter_dimension=0,
        tiled=True,
    )
    a_inverse = lax.rsqrt(jnp.mean(branch * branch, axis=1, keepdims=True) + EPS)
    hidden = x_rows + branch * a_inverse * attn_gain
    h_low = lax.all_gather(hidden.astype(jnp.bfloat16), "tensor", axis=0, tiled=True)
    a_unit = branch * a_inverse
    w_gate_up = jnp.concatenate([w_gate, w_up], axis=1)
    gate_up = jnp.dot(h_low, w_gate_up, preferred_element_type=jnp.float32)
    gate = gate_up[:, :ff_cols]
    up = gate_up[:, ff_cols:]
    sigma_gate = jax.nn.sigmoid(gate)
    silu_gate = gate * sigma_gate
    act = (silu_gate * up).astype(jnp.bfloat16)
    down = lax.psum_scatter(
        jnp.dot(act, w_down, preferred_element_type=jnp.float32),
        "tensor",
        scatter_dimension=0,
        tiled=True,
    )
    f_inverse = lax.rsqrt(jnp.mean(down * down, axis=1, keepdims=True) + EPS)
    f_unit = down * f_inverse
    block_out = (hidden + f_unit * ffn_gain).astype(jnp.bfloat16)
    grad_out = cotangent.astype(jnp.float32)
    grad_ffn_part = jnp.sum(grad_out * f_unit, axis=0)
    grad_down = norm_back(grad_out, f_unit, f_inverse, ffn_gain).astype(jnp.bfloat16)
    grad_down_all = lax.all_gather(grad_down, "tensor", axis=0, tiled=True)
    grad_act = dot_last(grad_down_all, w_down)
    grad_w_down = dot_first(act, grad_down_all)
    grad_gate = grad_act * up * sigma_gate * (1.0 + gate * (1.0 - sigma_gate))
    grad_up = grad_act * silu_gate
    grad_gate_up = jnp.concatenate([grad_gate, grad_up], axis=1).astype(jnp.bfloat16)
    grad_w_gate_up = dot_first(h_low, grad_gate_up)
    grad_hidden = grad_out + lax.psum_scatter(
        dot_last(grad_gate_up, w_gate_up), "tensor", scatter_dimension=0, tiled=True
    )
    grad_attn_part = jnp.sum(grad_hidden * a_unit, axis=0)
    grad_branch = norm_back(grad_hidden, a_unit, a_inverse, attn_gain).astype(jnp.bfloat16)
    grad_branch_all = lax.all_gather(grad_branch, "tensor", axis=0, tiled=True)
    grad_w_out = dot_first(mixed, grad_branch_all)
    grad_mixed = dot_last(grad_branch_all, w_out).astype(jnp.bfloat16).reshape(shaped)

    def attend_back(pieces):
        query_block, key_block, value_block, seg_row, log_block, grad_block = pieces
        scores = scores_of(query_block, key_block, seg_row)
        probs = jnp.exp(scores - log_block[..., None])
        grad_probs = jnp.einsum(
            "qhd,khd->hqk", grad_block, value_block, preferred_element_type=jnp.float32
        )
        grad_scores = (
            probs * (grad_probs - jnp.sum(probs * grad_probs, axis=-1, keepdims=True))
        ).astype(jnp.bfloat16)
        grad_query = (
            jnp.einsum("hqk,khd->qhd", grad_scores, key_block, preferred_element_type=jnp.float32)
            * att_scale
        )
        grad_key = (
            jnp.einsum("hqk,qhd->khd", grad_scores, query_block, preferred_element_type=jnp.float32)
            * att_scale
        )
        grad_value = jnp.einsum(
            "hqk,qhd->khd",
            probs.astype(jnp.bfloat16),
            grad_block,
            preferred_element_type=jnp.float32,
        )
        return (grad_query, grad_key, grad_value.astype(jnp.bfloat16))

    grad_query, grad_key, grad_value = lax.map(
        attend_back, (query_seqs, key_seqs, value_seqs, segment_ids, log_total, grad_mixed)
    )
    grad_q_normed = rotate_back(
        rounded(grad_query.reshape(token_count, heads_here, HD)), cosine, sine
    ).reshape(token_count, head_cols)
    grad_k_normed = rotate_back(
        rounded(grad_key.reshape(token_count, heads_here, HD)), cosine, sine
    ).reshape(token_count, head_cols)
    grad_q_gain = jnp.sum(grad_q_normed * q_unit, axis=0)
    grad_k_gain = jnp.sum(grad_k_normed * k_unit, axis=0)
    inner_q = grad_q_normed * q_gain
    inner_k = grad_k_normed * k_gain
    q_inner_sum, k_inner_sum = lax.psum(
        (jnp.sum(inner_q * q_unit, axis=1), jnp.sum(inner_k * k_unit, axis=1)), "tensor"
    )
    grad_q_raw = q_inverse * (inner_q - q_unit * (q_inner_sum / full_width)[:, None])
    grad_k_raw = k_inverse * (inner_k - k_unit * (k_inner_sum / full_width)[:, None])
    grad_qkv = jnp.concatenate(
        [
            grad_q_raw.astype(jnp.bfloat16),
            grad_k_raw.astype(jnp.bfloat16),
            grad_value.reshape(token_count, head_cols),
        ],
        axis=1,
    )
    grad_w_qkv = dot_first(whole_x, grad_qkv)
    grad_tokens = grad_hidden + lax.psum_scatter(
        dot_last(grad_qkv, w_qkv), "tensor", scatter_dimension=0, tiled=True
    )
    grad_w_qkv, grad_w_out, grad_w_gate_up, grad_w_down, grad_q_gain, grad_k_gain = lax.psum(
        (grad_w_qkv, grad_w_out, grad_w_gate_up, grad_w_down, grad_q_gain, grad_k_gain), "dp"
    )
    grad_attn_gain, grad_ffn_gain = lax.psum((grad_attn_part, grad_ffn_part), ("dp", "tensor"))
    return (
        block_out,
        grad_tokens,
        grad_w_qkv[:, :head_cols],
        grad_w_qkv[:, head_cols : 2 * head_cols],
        grad_w_qkv[:, 2 * head_cols :],
        grad_w_out,
        grad_w_gate_up[:, :ff_cols],
        grad_w_gate_up[:, ff_cols:],
        grad_w_down,
        grad_q_gain,
        grad_k_gain,
        grad_attn_gain,
        grad_ffn_gain,
    )


def solution(mesh):
    placed = (
        P(("dp", "tensor"), None),
        P("dp", None),
        P(None, "tensor"),
        P(None, "tensor"),
        P(None, "tensor"),
        P("tensor", None),
        P(None, "tensor"),
        P(None, "tensor"),
        P("tensor", None),
        P("tensor"),
        P("tensor"),
        P(),
        P(),
        P(("dp", "tensor"), None),
    )
    return jax.shard_map(
        on_device,
        mesh=mesh,
        in_specs=placed,
        out_specs=(
            P(("dp", "tensor"), None),
            P(("dp", "tensor"), None),
            P(None, "tensor"),
            P(None, "tensor"),
            P(None, "tensor"),
            P("tensor", None),
            P(None, "tensor"),
            P(None, "tensor"),
            P("tensor", None),
            P("tensor"),
            P("tensor"),
            P(),
            P(),
        ),
        check_vma=False,
    )
```

profile of v0, /device:TPU:0, one launch (start us, length us, event | category | flops | bytes accessed | tf_op | source)
XLA Modules:
  0.0 1320.7 jit_solution(9570834029763886558)
XLA Ops:
  12.5 1.7 constant_dynamic-update-slice_fusion.2
  14.4 1.6 copy-done.37
  17.6 41.9 %all-gather.5.cloned.1.call-done = bf16[1024,2048]{1,0:T(8,128)(2,1)} async-done(((bf16[128,2048]{1,0:T(8,128)(2,1)}), bf16[1024,2048]{1,0:T(8,128)(2,1)}) %all-gather.5.cloned.1.call-update) | async-done | bytes 4194320 | tf_op jit(solution)/shard_map/all_gather | solution.py:88
  59.5 6.2 convolution_bitcast_fusion.1
  67.5 14.8 %all-reduce.2 = (f32[1024]{0:T(1024)S(1)}, f32[1024]{0:T(1024)S(1)}) all-reduce(f32[1024]{0:T(1024)S(1)} %get-tuple-element.103, f32[1024]{0:T(1024)S(1)} %get-tuple-element.102), channel_id=1, replica_groups=mesh['dp'=4,'tensor'=8] {'tensor'}, use_global_device_ids=true, to_apply=%region_1.0 | all-reduce | flops 2048 | bytes 16384 | tf_op jit(solution)/shard_map/psum | solution.py:94
  82.4 1.8 fusion.33
  85.5 2.0 fusion.47
  88.7 2.1 copy-done.2
  93.3 4.7 fusion.48
  98.1 87.9 %reduce-scatter.5.cloned.1.call-done = f32[128,2048]{1,0:T(8,128)} async-done(((f32[1024,2048]{1,0:T(8,128)}), f32[128,2048]{1,0:T(8,128)}) %reduce-scatter.5.cloned.1.call-update) | async-done | bytes 1048592 | tf_op jit(solution)/shard_map/reduce_scatter | solution.py:138
  187.3 2.2 fusion.35
  190.1 4.8 constant_dynamic-update-slice_fusion.4
  195.0 2.5 constant_dynamic-update-slice_fusion.3
  197.4 37.9 %all-gather.7.cloned.1.call-done = bf16[1024,2048]{1,0:T(8,128)(2,1)} async-done(((bf16[128,2048]{1,0:T(8,128)(2,1)}), bf16[1024,2048]{1,0:T(8,128)(2,1)}) %all-gather.7.cloned.1.call-update) | async-done | bytes 4194320 | tf_op jit(solution)/shard_map/all_gather | solution.py:146
  235.3 12.5 fusion.49
  249.2 2.8 copy-done.10
  253.3 6.7 fusion.50
  260.1 88.4 %reduce-scatter.7.cloned.1.call-done = f32[128,2048]{1,0:T(8,128)} async-done(((f32[1024,2048]{1,0:T(8,128)}), f32[128,2048]{1,0:T(8,128)}) %reduce-scatter.7.cloned.1.call-update) | async-done | bytes 1048592 | tf_op jit(solution)/shard_map/reduce_scatter | solution.py:155
  351.6 2.3 fusion.22
  354.1 45.4 %all-gather.9.cloned.1.call-done = bf16[1024,2048]{1,0:T(8,128)(2,1)} async-done(((bf16[128,2048]{1,0:T(8,128)(2,1)}), bf16[1024,2048]{1,0:T(8,128)(2,1)}) %all-gather.9.cloned.1.call-update) | async-done | bytes 4194320 | tf_op jit(solution)/shard_map/all_gather | solution.py:167
  399.5 11.7 multiply_convert_fusion.2
  413.2 13.3 %fusion.9 = f32[1024,2048]{1,0:T(8,128)} fusion(bf16[2048,2048]{1,0:T(8,128)(2,1)} %constant_dynamic-update-slice_fusion.3, bf16[1024,1024]{1,0:T(8,128)(2,1)S(1)} %get-tuple-element.123, bf16[1024,1024]{1,0:T(8,128)(2,1)S(1)} %get-tuple-element.122), kind=kOutput, calls=%fused_computation.21 | convolution fusion | flops 8598323200 | bytes 20971520 | tf_op jit(solution)/shard_map/dot_general | solution.py:18
  426.6 88.4 %reduce-scatter.9.cloned.1.call-done = f32[128,2048]{1,0:T(8,128)} async-done(((f32[1024,2048]{1,0:T(8,128)}), f32[128,2048]{1,0:T(8,128)}) %reduce-scatter.9.cloned.1.call-update) | async-done | bytes 1048592 | tf_op jit(solution)/shard_map/reduce_scatter | solution.py:174
  515.0 1.7 multiply_reduce_fusion.1
  516.8 3.0 multiply_convert_fusion.6
  520.1 45.4 %all-gather.11.cloned.1.call-done = bf16[1024,2048]{1,0:T(8,128)(2,1)} async-done(((bf16[128,2048]{1,0:T(8,128)(2,1)}), bf16[1024,2048]{1,0:T(8,128)(2,1)}) %all-gather.11.cloned.1.call-update) | async-done | bytes 4194320 | tf_op jit(solution)/shard_map/all_gather | solution.py:179
  565.5 3.6 convolution_convert_fusion
  569.1 5.1 fusion.13
  574.3 1.9 multiply_reduce_fusion
  576.1 2.5 multiply_convert_fusion
  584.0 14.8 %all-reduce.1 = (f32[1024]{0:T(1024)S(1)}, f32[1024]{0:T(1024)S(1)}) all-reduce(f32[1024]{0:T(1024)S(1)} %get-tuple-element.97, f32[1024]{0:T(1024)S(1)} %get-tuple-element.100), channel_id=1, replica_groups=mesh['dp'=4,'tensor'=8] {'tensor'}, use_global_device_ids=true, to_apply=%region_19.20 | all-reduce | flops 2048 | bytes 16384 | tf_op jit(solution)/shard_map/psum | solution.py:222
  598.8 2.2 multiply_convert_fusion.5
  602.0 5.7 fusion.34
  609.3 9.2 fusion.52
  618.5 12.1 fusion.8
  630.6 2.6 fusion.51
  634.1 6.6 convolution_bitcast_fusion
  640.7 39.8 %all-reduce = (f32[2048]{0:T(1024)}, f32[2048]{0:T(1024)}) all-reduce(f32[2048]{0:T(1024)S(1)} %get-tuple-element.104, f32[2048]{0:T(1024)S(1)} %get-tuple-element.106), channel_id=1, replica_groups=mesh['dp'=4,'tensor'=8] {'dp','tensor'}, use_global_device_ids=true, to_apply=%region_30.31 | all-reduce | flops 4096 | bytes 32768 | tf_op jit(solution)/shard_map/psum | solution.py:242
  680.5 10.8 all-reduce.3
  691.3 5.4 reduce-scatter.11.cloned.1.call-done
  696.7 2.4 fusion.36
  699.1 583.0 %all-reduce.7.cloned.1.call-done = (f32[2048,768]{0,1:T(8,128)}, f32[256,2048]{1,0:T(8,128)}, f32[2048,2048]{1,0:T(8,128)}, f32[1024,2048]{1,0:T(8,128)}) async-done(((f32[2048,768]{0,1:T(8,128)}, f32[256,2048]{1,0:T(8,128)}, f32[2048,2048]{1,0:T(8,128)}, f32[1024,2048]{1,0:T(8,128)}), (f32[2048,768]{0,1:T(8,128)}, f32[256,2048]{1,0:T(8,128)}, f32[2048,2048]{1,0:T(8,128)}, ...) | async-done | bytes 33554448 | tf_op jit(solution)/shard_map/psum | solution.py:239
  1282.1 5.5 fusion.44
  1287.7 2.9 copy.52
  1290.6 2.9 copy.51
  1293.4 1.8 copy.50
  1295.2 13.4 %fusion.43 = (f32[2048,1024]{1,0:T(8,128)}, f32[2048,1024]{1,0:T(8,128)}) fusion(f32[2048,2048]{1,0:T(8,128)} %get-tuple-element.118), kind=kLoop, calls=%fused_computation.114 | loop fusion | bytes 33554432 | tf_op jit(solution)/shard_map/slice | solution.py:251
  1310.4 3.4 copy.70
  (170 shorter events, 33.8 us)
Async XLA Ops:
  7.2 86.1 %copy-start = (bf16[256,2048]{1,0:T(8,128)(2,1)S(1)}, bf16[256,2048]{1,0:T(8,128)(2,1)}, u32[]{:S(2)}) copy-start(bf16[256,2048]{1,0:T(8,128)(2,1)} %param.19) | copy-start | bytes 3145732
  7.2 7.0 copy-start.26
  7.2 52.3 %all-gather.5.cloned.1.call-start = ((), (), s32[]{:S(2)}) async-start(), calls=%async_computation.4 | async-start | bytes 4718592 | tf_op jit(solution)/shard_map/all_gather | solution.py:88
  7.9 178.0 %reduce-scatter.5.cloned.1.call-start = ((), (), s32[]{:S(2)}) async-start(), calls=%async_computation.5 | async-start | bytes 9437184 | tf_op jit(solution)/shard_map/reduce_scatter | solution.py:138
  11.3 3.0 copy-start.27
  11.4 4.6 copy-start.41
  12.5 71.9 %copy-start.11 = (f32[1024,128]{0,1:T(8,128)}, f32[1024,128]{0,1:T(8,128)S(1)}, u32[]{:S(2)}) copy-start(f32[1024,128]{0,1:T(8,128)S(1)} %get-tuple-element.156) | copy-start | bytes 1572868
  12.5 71.9 %copy-start.14 = (f32[1024,128]{0,1:T(8,128)}, f32[1024,128]{0,1:T(8,128)S(1)}, u32[]{:S(2)}) copy-start(f32[1024,128]{0,1:T(8,128)S(1)} %get-tuple-element.155) | copy-start | bytes 1572868
  17.6 64.7 %copy-start.42 = (f32[256]{0:T(256)S(1)}, f32[256]{0:T(256)}, u32[]{:S(2)}) copy-start(f32[256]{0:T(256)} %param.24) | copy-start | bytes 3076
  17.6 64.8 %copy-start.43 = (f32[256]{0:T(256)S(1)}, f32[256]{0:T(256)}, u32[]{:S(2)}) copy-start(f32[256]{0:T(256)} %param.23) | copy-start | bytes 3076
  67.5 21.2 %copy-start.23 = (bf16[1024,256]{0,1:T(8,128)(2,1)}, bf16[1024,256]{0,1:T(8,128)(2,1)S(1)}, u32[]{:S(2)}) copy-start(bf16[1024,256]{0,1:T(8,128)(2,1)S(1)} %slice.142) | copy-start | bytes 1572868
  87.5 3.3 copy-start.2
  98.0 89.3 %copy-start.13 = (bf16[128,2048]{1,0:T(8,128)(2,1)S(1)}, bf16[128,2048]{1,0:T(8,128)(2,1)}, u32[]{:S(2)}) copy-start(bf16[128,2048]{1,0:T(8,128)(2,1)} %param.14) | copy-start | bytes 1572868
  98.0 89.3 %copy-start.39 = (f32[2048]{0:T(1024)S(1)}, f32[2048]{0:T(1024)}, u32[]{:S(2)}) copy-start(f32[2048]{0:T(1024)} %param.25) | copy-start | bytes 24580
  98.0 137.2 %all-gather.7.cloned.1.call-start = ((), (), s32[]{:S(2)}) async-start(), calls=%async_computation.6 | async-start | bytes 4718592 | tf_op jit(solution)/shard_map/all_gather | solution.py:146
  189.6 158.9 %reduce-scatter.7.cloned.1.call-start = ((), (), s32[]{:S(2)}) async-start(), calls=%async_computation.7 | async-start | bytes 9437184 | tf_op jit(solution)/shard_map/reduce_scatter | solution.py:155
  190.1 4.8 copy-start.16
  247.7 4.3 copy-start.10
  247.8 5.6 copy-start.44
  260.0 89.9 %copy-start.7 = (bf16[128,2048]{1,0:T(8,128)(2,1)S(1)}, bf16[128,2048]{1,0:T(8,128)(2,1)}, u32[]{:S(2)}) copy-start(bf16[128,2048]{1,0:T(8,128)(2,1)} %param.27) | copy-start | bytes 1572868
  260.0 89.9 %copy-start.40 = (f32[2048]{0:T(1024)S(1)}, f32[2048]{0:T(1024)}, u32[]{:S(2)}) copy-start(f32[2048]{0:T(1024)} %param.26) | copy-start | bytes 24580
  260.0 139.5 %all-gather.9.cloned.1.call-start = ((), (), s32[]{:S(2)}) async-start(), calls=%async_computation.8 | async-start | bytes 4718592 | tf_op jit(solution)/shard_map/all_gather | solution.py:167
  353.9 161.1 %reduce-scatter.9.cloned.1.call-start = ((), (), s32[]{:S(2)}) async-start(), calls=%async_computation.9 | async-start | bytes 9437184 | tf_op jit(solution)/shard_map/reduce_scatter | solution.py:174
  426.5 88.5 %copy-start.5 = (f32[128,2048]{1,0:T(8,128)S(1)}, f32[128,2048]{1,0:T(8,128)}, u32[]{:S(2)}) copy-start(f32[128,2048]{1,0:T(8,128)} %reduce-scatter.5.cloned.1.call-done) | copy-start | bytes 3145732
  426.5 90.3 %copy-start.6 = (f32[128,2048]{1,0:T(8,128)S(1)}, f32[128,2048]{1,0:T(8,128)}, u32[]{:S(2)}) copy-start(f32[128,2048]{1,0:T(8,128)} %reduce-scatter.7.cloned.1.call-done) | copy-start | bytes 3145732
  426.5 138.9 %all-gather.11.cloned.1.call-start = ((), (), s32[]{:S(2)}) async-start(), calls=%async_computation.10 | async-start | bytes 4718592 | tf_op jit(solution)/shard_map/all_gather | solution.py:179
  519.8 176.9 %reduce-scatter.11.cloned.1.call-start = ((), (), s32[]{:S(2)}) async-start(), calls=%async_computation.11 | async-start | bytes 9437184 | tf_op jit(solution)/shard_map/reduce_scatter | solution.py:236
  565.5 8.7 slice-start
  569.1 5.1 slice-start.1
  569.1 5.1 copy-start.24
  574.2 26.8 %copy-start.35 = (bf16[2,128,1024]{2,1,0:T(8,128)(2,1)}, bf16[2,128,1024]{2,1,0:T(8,128)(2,1)S(1)}, u32[]{:S(2)}) copy-start(bf16[2,128,1024]{2,1,0:T(8,128)(2,1)S(1)} %fusion.13) | copy-start | bytes 1572868
  598.8 3.3 copy-start.38
  607.8 674.4 %all-reduce.7.cloned.1.call-start = ((), (), s32[]{:S(2)}) async-start(), calls=%async_computation.12 | async-start | bytes 67108864 | tf_op jit(solution)/shard_map/psum | solution.py:239
  609.3 9.2 copy-start.46
  609.3 9.2 copy-start.49
  609.3 9.2 copy-start.51
  618.5 12.1 copy-start.30
  618.5 12.1 copy-start.47
  630.6 2.6 copy-start.32
  630.6 2.6 copy-start.34
  630.6 2.6 copy-start.36
  630.6 3.5 copy-start.45
  640.7 56.0 %copy-start.8 = (bf16[128,2048]{1,0:T(8,128)(2,1)S(1)}, bf16[128,2048]{1,0:T(8,128)(2,1)}, u32[]{:S(2)}) copy-start(bf16[128,2048]{1,0:T(8,128)(2,1)} %param.27) | copy-start | bytes 1572868
  640.7 56.0 %copy-start.9 = (f32[128,2048]{1,0:T(8,128)S(1)}, f32[128,2048]{1,0:T(8,128)}, u32[]{:S(2)}) copy-start(f32[128,2048]{1,0:T(8,128)} %reduce-scatter.9.cloned.1.call-done) | copy-start | bytes 3145732
  1295.2 14.7 %slice-start.2 = ((s8[8388608]{0:T(1024)(128)(4,1)}), s8[4194304]{0:T(1024)(128)(4,1)S(1)}, s32[]{:S(2)}) async-start(s8[8388608]{0:T(1024)(128)(4,1)} %bitcast.85), calls=%async_computation.15 | async-start | bytes 8388608
  1295.2 13.4 %copy-start.25 = (f32[256,2048]{1,0:T(8,128)S(1)}, f32[256,2048]{1,0:T(8,128)}, u32[]{:S(2)}) copy-start(f32[256,2048]{1,0:T(8,128)} %get-tuple-element.162) | copy-start | bytes 6291460
  1295.2 15.1 %slice-start.3 = ((s8[8388608]{0:T(1024)(128)(4,1)}), s8[4194304]{0:T(1024)(128)(4,1)S(1)}, s32[]{:S(2)}) async-start(s8[8388608]{0:T(1024)(128)(4,1)} %bitcast.85), calls=%async_computation.16 | async-start | bytes 8388608
  1310.4 3.4 copy-start.1
  (17 other events, 27.6 us)
Sparse Core Ops, SparseCore 0:
  9.6 49.8 all-gather.4
  98.1 87.7 reduce-scatter.4
  189.7 45.4 all-gather.6
  260.2 88.3 reduce-scatter.6
  354.0 45.4 all-gather.8
  426.7 88.3 reduce-scatter.8
  519.9 45.4 all-gather.10
  607.9 88.7 reduce-scatter.10
  701.3 580.8 all-reduce.6
where the time goes:
time: 1330 us; the launch traced here: 1320 us
  waiting for transfers between devices  1020 us (77%)
  matrix products  108 us (8%)
  blocking collectives  80.2 us (6%)
  local copies, waits for them, and re-layouts  59.4 us (4%)
  other arithmetic  31.7 us (2%)
  between operations  15.7 us (1%)
    psum x1, waiting for transfers between devices, on_device(): lax.psum((grad_w_qkv, grad_w_out, grad_w_gate_up, grad_w_down, grad_q_gai...  583 us
    reduce_scatter x1, waiting for transfers between devices, on_device(): lax.psum_scatter(jnp.dot(act, w_down, preferred_element_type=jnp.float32)...  88.4 us
    reduce_scatter x1, waiting for transfers between devices, on_device(): lax.psum_scatter(dot_last(grad_gate_up, w_gate_up), 'tensor', scatter_dim...  88.4 us
    reduce_scatter x1, waiting for transfers between devices, on_device(): lax.psum_scatter(jnp.dot(mixed, w_out, preferred_element_type=jnp.float32...  87.9 us
    all_gather x1, waiting for transfers between devices, on_device(): grad_down_all = lax.all_gather(grad_down, 'tensor', axis=0, tiled=True)  45.4 us
    all_gather x1, waiting for transfers between devices, on_device(): grad_branch_all = lax.all_gather(grad_branch, 'tensor', axis=0, tiled=True)  45.4 us
    all_gather x1, waiting for transfers between devices, on_device(): whole_x = lax.all_gather(tokens, 'tensor', axis=0, tiled=True)  41.9 us
    psum x1, blocking collectives, on_device(): lax.psum((grad_attn_part, grad_ffn_part), ('dp', 'tensor'))  39.8 us
  transfers between devices with their start and end apart: 9, of which 9 were waited for; matrix products, arithmetic and copies ran while one was open for 4% of the time, Pallas kernels for 0%

commit v1 on v0

--- a/solution.py
+++ b/solution.py
@@ -29,10 +29,8 @@
 def positions_of(segment_ids):
     length = segment_ids.shape[-1]
     places = jnp.arange(length, dtype=jnp.int32)
-    earlier = jnp.concatenate([segment_ids[:, :1] - 1, segment_ids[:, :-1]], axis=1)
-    starts = jnp.where(segment_ids != earlier, places[None, :], jnp.zeros_like(segment_ids))
-    starts = lax.cummax(starts, axis=1)
-    return places[None, :] - starts
+    below = (segment_ids[:, None, :] < segment_ids[:, :, None]).astype(jnp.int32)
+    return places[None, :] - jnp.sum(below, axis=2)
 
 
 def rotary_tables(positions):
@@ -136,11 +134,11 @@
     mixed = mixed.reshape(token_count, head_cols)
     x_rows = tokens.astype(jnp.float32)
     branch = lax.psum_scatter(
-        jnp.dot(mixed, w_out, preferred_element_type=jnp.float32),
+        jnp.dot(mixed, w_out, preferred_element_type=jnp.float32).astype(jnp.bfloat16),
         "tensor",
         scatter_dimension=0,
         tiled=True,
-    )
+    ).astype(jnp.float32)
     a_inverse = lax.rsqrt(jnp.mean(branch * branch, axis=1, keepdims=True) + EPS)
     hidden = x_rows + branch * a_inverse * attn_gain
     h_low = lax.all_gather(hidden.astype(jnp.bfloat16), "tensor", axis=0, tiled=True)
@@ -153,11 +151,11 @@
     silu_gate = gate * sigma_gate
     act = (silu_gate * up).astype(jnp.bfloat16)
     down = lax.psum_scatter(
-        jnp.dot(act, w_down, preferred_element_type=jnp.float32),
+        jnp.dot(act, w_down, preferred_element_type=jnp.float32).astype(jnp.bfloat16),
         "tensor",
         scatter_dimension=0,
         tiled=True,
-    )
+    ).astype(jnp.float32)
     f_inverse = lax.rsqrt(jnp.mean(down * down, axis=1, keepdims=True) + EPS)
     f_unit = down * f_inverse
     block_out = (hidden + f_unit * ffn_gain).astype(jnp.bfloat16)
@@ -172,8 +170,8 @@
     grad_gate_up = jnp.concatenate([grad_gate, grad_up], axis=1).astype(jnp.bfloat16)
     grad_w_gate_up = dot_first(h_low, grad_gate_up)
     grad_hidden = grad_out + lax.psum_scatter(
-        dot_last(grad_gate_up, w_gate_up), "tensor", scatter_dimension=0, tiled=True
-    )
+        dot_last(grad_gate_up, w_gate_up).astype(jnp.bfloat16), "tensor", scatter_dimension=0, tiled=True
+    ).astype(jnp.float32)
     grad_attn_part = jnp.sum(grad_hidden * a_unit, axis=0)
     grad_branch = norm_back(grad_hidden, a_unit, a_inverse, attn_gain).astype(jnp.bfloat16)
     grad_branch_all = lax.all_gather(grad_branch, "tensor", axis=0, tiled=True)
@@ -234,11 +232,13 @@
     )
     grad_w_qkv = dot_first(whole_x, grad_qkv)
     grad_tokens = grad_hidden + lax.psum_scatter(
-        dot_last(grad_qkv, w_qkv), "tensor", scatter_dimension=0, tiled=True
-    )
-    grad_w_qkv, grad_w_out, grad_w_gate_up, grad_w_down, grad_q_gain, grad_k_gain = lax.psum(
-        (grad_w_qkv, grad_w_out, grad_w_gate_up, grad_w_down, grad_q_gain, grad_k_gain), "dp"
-    )
+        dot_last(grad_qkv, w_qkv).astype(jnp.bfloat16), "tensor", scatter_dimension=0, tiled=True
+    ).astype(jnp.float32)
+    grad_w_qkv, grad_w_out, grad_w_gate_up, grad_w_down = [
+        lax.psum(part.astype(jnp.bfloat16), "dp").astype(jnp.float32)
+        for part in (grad_w_qkv, grad_w_out, grad_w_gate_up, grad_w_down)
+    ]
+    grad_q_gain, grad_k_gain = lax.psum((grad_q_gain, grad_k_gain), "dp")
     grad_attn_gain, grad_ffn_gain = lax.psum((grad_attn_part, grad_ffn_part), ("dp", "tensor"))
     return (
         block_out,

time: 1330 us -> 899 us (0.68)
  waiting for transfers between devices: 1020 us -> 598 us
    psum x1, waiting for transfers between devices: 583 us -> 280 us  [on_device(): lax.psum(part.astype(jnp.bfloat16), 'dp').astype(jnp.float32)]
    reduce_scatter x2, waiting for transfers between devices: 93.9 us -> 48.8 us  [the longest x1 48.8 us: on_device(): lax.psum_scatter(dot_last(grad_gate_up, w_gate_up).astype(jnp.bfloat16),...]
    reduce_scatter x1, waiting for transfers between devices: 87.9 us -> 48 us  [on_device(): lax.psum_scatter(jnp.dot(mixed, w_out, preferred_element_type=jnp.float32...]
    reduce_scatter x1, waiting for transfers between devices: 88.4 us -> 48.8 us  [on_device(): lax.psum_scatter(jnp.dot(act, w_down, preferred_element_type=jnp.float32)...]
    unnamed x120 -> x96, local copies, waits for them, and re-layouts: 36.5 us -> 31.2 us
  transfers between devices with their start and end apart: 9 -> 9, of which waited for: 9 -> 8; matrix products, arithmetic and copies ran while one was open for 4% -> 5% of each run, Pallas kernels for 0% -> 0%
where the time goes in v1:
time: 899 us; the launch traced here: 890 us
  waiting for transfers between devices  598 us (67%)
  matrix products  107 us (12%)
  blocking collectives  79.3 us (9%)
  local copies, waits for them, and re-layouts  49.7 us (6%)
  other arithmetic  39.9 us (4%)
  between operations  14.9 us (2%)
    psum x1, waiting for transfers between devices, on_device(): lax.psum(part.astype(jnp.bfloat16), 'dp').astype(jnp.float32)  280 us
    reduce_scatter x1, waiting for transfers between devices, on_device(): lax.psum_scatter(jnp.dot(act, w_down, preferred_element_type=jnp.float32)...  48.8 us
    reduce_scatter x1, waiting for transfers between devices, on_device(): lax.psum_scatter(dot_last(grad_gate_up, w_gate_up).astype(jnp.bfloat16),...  48.8 us
    reduce_scatter x1, waiting for transfers between devices, on_device(): lax.psum_scatter(jnp.dot(mixed, w_out, preferred_element_type=jnp.float32...  48 us
    all_gather x1, waiting for transfers between devices, on_device(): grad_branch_all = lax.all_gather(grad_branch, 'tensor', axis=0, tiled=True)  45.2 us
    all_gather x1, waiting for transfers between devices, on_device(): grad_down_all = lax.all_gather(grad_down, 'tensor', axis=0, tiled=True)  45 us
    all_gather x1, waiting for transfers between devices, on_device(): whole_x = lax.all_gather(tokens, 'tensor', axis=0, tiled=True)  42.6 us
    psum x1, blocking collectives, on_device(): lax.psum((grad_attn_part, grad_ffn_part), ('dp', 'tensor'))  38.3 us
  transfers between devices with their start and end apart: 9, of which 8 were waited for; matrix products, arithmetic and copies ran while one was open for 5% of the time, Pallas kernels for 0%

profile of v1, /device:TPU:0, one launch (start us, length us, event | category | flops | bytes accessed | tf_op | source)
XLA Modules:
  0.0 889.5 jit_solution(1835168054110939800)
XLA Ops:
  10.5 2.6 constant_dynamic-update-slice_fusion.2
  15.3 1.6 fusion.6
  16.9 42.6 %all-gather.5.cloned.1.call-done = bf16[1024,2048]{1,0:T(8,128)(2,1)} async-done(((bf16[128,2048]{1,0:T(8,128)(2,1)}), bf16[1024,2048]{1,0:T(8,128)(2,1)}) %all-gather.5.cloned.1.call-update) | async-done | bytes 4194320 | tf_op jit(solution)/shard_map/all_gather | solution.py:86
  59.5 6.2 convolution_bitcast_fusion
  67.5 14.8 %all-reduce.2 = (f32[1024]{0:T(1024)S(1)}, f32[1024]{0:T(1024)S(1)}) all-reduce(f32[1024]{0:T(1024)S(1)} %get-tuple-element.103, f32[1024]{0:T(1024)S(1)} %get-tuple-element.102), channel_id=1, replica_groups=mesh['dp'=4,'tensor'=8] {'tensor'}, use_global_device_ids=true, to_apply=%region_1.0 | all-reduce | flops 2048 | bytes 16384 | tf_op jit(solution)/shard_map/psum | solution.py:92
  82.3 1.8 fusion.49
  85.5 2.0 fusion.58
  88.7 2.2 copy-done.2
  90.9 1.6 fusion.16
  93.3 3.3 convolution_convert_fusion.2
  96.9 48.0 %reduce-scatter.5.cloned.1.call-done = bf16[128,2048]{1,0:T(8,128)(2,1)} async-done(((bf16[1024,2048]{1,0:T(8,128)(2,1)}), bf16[128,2048]{1,0:T(8,128)(2,1)}) %reduce-scatter.5.cloned.1.call-update) | async-done | bytes 524304 | tf_op jit(solution)/shard_map/reduce_scatter | solution.py:136
  146.2 2.1 fusion.47
  148.4 4.8 constant_dynamic-update-slice_fusion.4
  153.2 2.5 constant_dynamic-update-slice_fusion.3
  155.7 38.1 %all-gather.7.cloned.1.call-done = bf16[1024,2048]{1,0:T(8,128)(2,1)} async-done(((bf16[128,2048]{1,0:T(8,128)(2,1)}), bf16[1024,2048]{1,0:T(8,128)(2,1)}) %all-gather.7.cloned.1.call-update) | async-done | bytes 4194320 | tf_op jit(solution)/shard_map/all_gather | solution.py:144
  193.8 12.5 %fusion.59 = f32[1024,2048]{1,0:T(8,128)S(1)} fusion(bf16[1024,2048]{1,0:T(8,128)(2,1)} %all-gather.7.cloned.1.call-done, bf16[2048,2048]{1,0:T(8,128)(2,1)} %constant_dynamic-update-slice_fusion.3), kind=kOutput, calls=%fused_computation.133 | convolution fusion | flops 8589934592 | bytes 20971520 | tf_op jit(solution)/shard_map/dot_general | solution.py:147
  207.7 2.8 copy-done.7
  211.9 6.1 convolution_convert_fusion.5
  218.0 48.8 %reduce-scatter.7.cloned.1.call-done = bf16[128,2048]{1,0:T(8,128)(2,1)} async-done(((bf16[1024,2048]{1,0:T(8,128)(2,1)}), bf16[128,2048]{1,0:T(8,128)(2,1)}) %reduce-scatter.7.cloned.1.call-update) | async-done | bytes 524304 | tf_op jit(solution)/shard_map/reduce_scatter | solution.py:153
  269.6 2.2 fusion.26
  272.3 45.0 %all-gather.9.cloned.1.call-done = bf16[1024,2048]{1,0:T(8,128)(2,1)} async-done(((bf16[128,2048]{1,0:T(8,128)(2,1)}), bf16[1024,2048]{1,0:T(8,128)(2,1)}) %all-gather.9.cloned.1.call-update) | async-done | bytes 4194320 | tf_op jit(solution)/shard_map/all_gather | solution.py:165
  317.3 11.7 %multiply_convert_fusion.2 = (bf16[1024,1024]{1,0:T(8,128)(2,1)S(1)}, bf16[1024,1024]{1,0:T(8,128)(2,1)S(1)}) fusion(f32[1024,2048]{1,0:T(8,128)} %copy-done.7, bf16[1024,2048]{1,0:T(8,128)(2,1)} %all-gather.9.cloned.1.call-done, bf16[1024,2048]{1,0:T(8,128)(2,1)} %param.22), kind=kOutput, calls=%fused_computation.13 | convolution fusion | flops 4308598784 | bytes 20971520 | tf_op jit(solution)/shard_map/dot_general | solution.py:18
  330.9 12.6 %convolution_convert_fusion.1 = bf16[1024,2048]{1,0:T(8,128)(2,1)} fusion(bf16[2048,2048]{1,0:T(8,128)(2,1)} %constant_dynamic-update-slice_fusion.3, bf16[1024,1024]{1,0:T(8,128)(2,1)S(1)} %get-tuple-element.121, bf16[1024,1024]{1,0:T(8,128)(2,1)S(1)} %get-tuple-element.120), kind=kOutput, calls=%fused_computation.21 | convolution fusion | flops 8600420352 | bytes 16777216 | tf_op jit(solution)/shard_map/dot_general | solution.py:18
  343.6 48.8 %reduce-scatter.9.cloned.1.call-done = bf16[128,2048]{1,0:T(8,128)(2,1)} async-done(((bf16[1024,2048]{1,0:T(8,128)(2,1)}), bf16[128,2048]{1,0:T(8,128)(2,1)}) %reduce-scatter.9.cloned.1.call-update) | async-done | bytes 524304 | tf_op jit(solution)/shard_map/reduce_scatter | solution.py:172
  393.9 2.8 fusion.31
  397.0 45.2 %all-gather.11.cloned.1.call-done = bf16[1024,2048]{1,0:T(8,128)(2,1)} async-done(((bf16[128,2048]{1,0:T(8,128)(2,1)}), bf16[1024,2048]{1,0:T(8,128)(2,1)}) %all-gather.11.cloned.1.call-update) | async-done | bytes 4194320 | tf_op jit(solution)/shard_map/all_gather | solution.py:177
  442.2 3.6 convolution_convert_fusion.8
  445.8 5.9 fusion.19
  451.8 1.9 multiply_reduce_fusion
  453.6 2.5 multiply_convert_fusion
  461.4 14.8 %all-reduce.1 = (f32[1024]{0:T(1024)S(1)}, f32[1024]{0:T(1024)S(1)}) all-reduce(f32[1024]{0:T(1024)S(1)} %get-tuple-element.97, f32[1024]{0:T(1024)S(1)} %get-tuple-element.100), channel_id=1, replica_groups=mesh['dp'=4,'tensor'=8] {'tensor'}, use_global_device_ids=true, to_apply=%region_18.19 | all-reduce | flops 2048 | bytes 16384 | tf_op jit(solution)/shard_map/psum | solution.py:220
  476.2 2.1 multiply_convert_fusion.5
  479.1 7.5 convolution_convert_fusion.3
  487.0 9.6 %convolution_convert_fusion.4 = bf16[1024,2048]{1,0:T(8,128)(2,1)} fusion(bf16[1024,1024]{1,0:T(8,128)(2,1)} %copy-done.15, bf16[1024,2048]{1,0:T(8,128)(2,1)} %all-gather.9.cloned.1.call-done), kind=kOutput, calls=%fused_computation.24 | convolution fusion | flops 4297064448 | bytes 10485760 | tf_op jit(solution)/shard_map/dot_general | solution.py:24
  496.6 11.6 %convolution_convert_fusion = bf16[2048,2048]{1,0:T(8,128)(2,1)} fusion(bf16[1024,2048]{1,0:T(8,128)(2,1)S(1)} %copy-done.37, bf16[1024,1024]{1,0:T(8,128)(2,1)S(1)} %copy-done.42, bf16[1024,1024]{1,0:T(8,128)(2,1)S(1)} %copy-done.40), kind=kOutput, calls=%fused_computation.6 | convolution fusion | flops 8602517504 | bytes 16777216 | tf_op jit(solution)/shard_map/dot_general | solution.py:24
  508.2 2.3 convolution_convert_fusion.7
  511.2 6.2 fusion.8
  517.4 38.3 %all-reduce = (f32[2048]{0:T(1024)}, f32[2048]{0:T(1024)}) all-reduce(f32[2048]{0:T(1024)S(1)} %get-tuple-element.104, f32[2048]{0:T(1024)S(1)} %get-tuple-element.106), channel_id=1, replica_groups=mesh['dp'=4,'tensor'=8] {'dp','tensor'}, use_global_device_ids=true, to_apply=%region_29.30 | all-reduce | flops 4096 | bytes 32768 | tf_op jit(solution)/shard_map/psum | solution.py:242
  555.7 11.3 %all-reduce.3 = (f32[256]{0:T(256)}, f32[256]{0:T(256)}) all-reduce(f32[256]{0:T(256)S(1)} %get-tuple-element.101, f32[256]{0:T(256)S(1)} %get-tuple-element.96), channel_id=1, replica_groups=mesh['dp'=4,'tensor'=8] {'dp'}, use_global_device_ids=true, to_apply=%region_25.26 | all-reduce | flops 512 | bytes 4096 | tf_op jit(solution)/shard_map/psum | solution.py:241
  567.0 2.3 convert_add_fusion.1
  569.3 280.2 %all-reduce.7.cloned.1.call-done = (bf16[2048,768]{0,1:T(8,128)(2,1)}, bf16[2048,2048]{1,0:T(8,128)(2,1)}, bf16[256,2048]{1,0:T(8,128)(2,1)}, bf16[1024,2048]{1,0:T(8,128)(2,1)}) async-done(((bf16[2048,768]{0,1:T(8,128)(2,1)}, bf16[2048,2048]{1,0:T(8,128)(2,1)}, bf16[256,2048]{1,0:T(8,128)(2,1)}, bf16[1024,2048]{1,0:T(8,128)(2,1)}), (bf16[2048,768]{0,1:T(8,128)(2,1)}, bf16[2048,2048]{1,0:T(8,128)(2,1)}, ...) | async-done | bytes 16777232 | tf_op jit(solution)/shard_map/psum | solution.py:238
  849.5 2.9 convert_element_type.190
  852.5 2.9 fusion.55
  855.4 2.9 copy.52
  858.3 2.9 copy.51
  861.2 2.9 copy.50
  864.1 6.7 convert_element_type.194
  870.7 11.8 %fusion.54 = (f32[2048,1024]{1,0:T(8,128)}, f32[2048,1024]{1,0:T(8,128)}) fusion(bf16[2048,2048]{1,0:T(8,128)(2,1)} %get-tuple-element.117), kind=kLoop, calls=%fused_computation.128 | loop fusion | bytes 33554432 | tf_op jit(solution)/shard_map/slice | solution.py:251
  (141 shorter events, 28.8 us)
Async XLA Ops:
  7.2 86.2 %copy-start = (bf16[256,2048]{1,0:T(8,128)(2,1)S(1)}, bf16[256,2048]{1,0:T(8,128)(2,1)}, u32[]{:S(2)}) copy-start(bf16[256,2048]{1,0:T(8,128)(2,1)} %param.19) | copy-start | bytes 3145732
  7.2 5.9 copy-start.24
  7.2 52.3 %all-gather.5.cloned.1.call-start = ((), (), s32[]{:S(2)}) async-start(), calls=%async_computation.4 | async-start | bytes 4718592 | tf_op jit(solution)/shard_map/all_gather | solution.py:86
  7.9 137.0 %reduce-scatter.5.cloned.1.call-start = ((), (), s32[]{:S(2)}) async-start(), calls=%async_computation.5 | async-start | bytes 4718592 | tf_op jit(solution)/shard_map/reduce_scatter | solution.py:136
  8.0 6.2 copy-start.25
  9.4 6.0 copy-start.32
  10.5 73.9 %copy-start.11 = (f32[1024,128]{0,1:T(8,128)}, f32[1024,128]{0,1:T(8,128)S(1)}, u32[]{:S(2)}) copy-start(f32[1024,128]{0,1:T(8,128)S(1)} %get-tuple-element.155) | copy-start | bytes 1572868
  16.9 65.4 %copy-start.33 = (f32[256]{0:T(256)S(1)}, f32[256]{0:T(256)}, u32[]{:S(2)}) copy-start(f32[256]{0:T(256)} %param.24) | copy-start | bytes 3076
  16.9 65.4 %copy-start.34 = (f32[256]{0:T(256)S(1)}, f32[256]{0:T(256)}, u32[]{:S(2)}) copy-start(f32[256]{0:T(256)} %param.23) | copy-start | bytes 3076
  65.7 1.6 copy-start.3
  67.5 21.2 %copy-start.20 = (bf16[1024,256]{0,1:T(8,128)(2,1)}, bf16[1024,256]{0,1:T(8,128)(2,1)S(1)}, u32[]{:S(2)}) copy-start(bf16[1024,256]{0,1:T(8,128)(2,1)S(1)} %slice.124) | copy-start | bytes 1572868
  85.0 2.5 copy-start.16
  85.0 2.5 copy-start.18
  87.5 3.4 copy-start.2
  96.6 49.6 %copy-start.10 = (bf16[128,2048]{1,0:T(8,128)(2,1)S(1)}, bf16[128,2048]{1,0:T(8,128)(2,1)}, u32[]{:S(2)}) copy-start(bf16[128,2048]{1,0:T(8,128)(2,1)} %param.14) | copy-start | bytes 1572868
  96.6 49.6 %copy-start.30 = (f32[2048]{0:T(1024)S(1)}, f32[2048]{0:T(1024)}, u32[]{:S(2)}) copy-start(f32[2048]{0:T(1024)} %param.25) | copy-start | bytes 24580
  96.7 97.1 %all-gather.7.cloned.1.call-start = ((), (), s32[]{:S(2)}) async-start(), calls=%async_computation.6 | async-start | bytes 4718592 | tf_op jit(solution)/shard_map/all_gather | solution.py:144
  148.3 118.5 %reduce-scatter.7.cloned.1.call-start = ((), (), s32[]{:S(2)}) async-start(), calls=%async_computation.7 | async-start | bytes 4718592 | tf_op jit(solution)/shard_map/reduce_scatter | solution.py:153
  148.4 4.8 copy-start.14
  206.3 4.3 copy-start.7
  206.3 5.6 copy-start.35
  217.9 50.1 %copy-start.5 = (bf16[128,2048]{1,0:T(8,128)(2,1)S(1)}, bf16[128,2048]{1,0:T(8,128)(2,1)}, u32[]{:S(2)}) copy-start(bf16[128,2048]{1,0:T(8,128)(2,1)} %param.27) | copy-start | bytes 1572868
  217.9 50.2 %copy-start.31 = (f32[2048]{0:T(1024)S(1)}, f32[2048]{0:T(1024)}, u32[]{:S(2)}) copy-start(f32[2048]{0:T(1024)} %param.26) | copy-start | bytes 24580
  218.0 99.3 %all-gather.9.cloned.1.call-start = ((), (), s32[]{:S(2)}) async-start(), calls=%async_computation.8 | async-start | bytes 4718592 | tf_op jit(solution)/shard_map/all_gather | solution.py:165
  271.8 120.6 %reduce-scatter.9.cloned.1.call-start = ((), (), s32[]{:S(2)}) async-start(), calls=%async_computation.9 | async-start | bytes 4718592 | tf_op jit(solution)/shard_map/reduce_scatter | solution.py:172
  328.9 2.0 copy-start.41
  343.5 48.9 %copy-start.8 = (bf16[128,2048]{1,0:T(8,128)(2,1)S(1)}, bf16[128,2048]{1,0:T(8,128)(2,1)}, u32[]{:S(2)}) copy-start(bf16[128,2048]{1,0:T(8,128)(2,1)} %reduce-scatter.5.cloned.1.call-done) | copy-start | bytes 1572868
  343.5 50.4 %copy-start.9 = (bf16[128,2048]{1,0:T(8,128)(2,1)S(1)}, bf16[128,2048]{1,0:T(8,128)(2,1)}, u32[]{:S(2)}) copy-start(bf16[128,2048]{1,0:T(8,128)(2,1)} %reduce-scatter.7.cloned.1.call-done) | copy-start | bytes 1572868
  343.5 98.7 %all-gather.11.cloned.1.call-start = ((), (), s32[]{:S(2)}) async-start(), calls=%async_computation.10 | async-start | bytes 4718592 | tf_op jit(solution)/shard_map/all_gather | solution.py:177
  396.8 170.3 %reduce-scatter.11.cloned.1.call-start = ((), (), s32[]{:S(2)}) async-start(), calls=%async_computation.11 | async-start | bytes 4718592 | tf_op jit(solution)/shard_map/reduce_scatter | solution.py:234
  442.2 9.5 %slice-start = ((s8[8388608]{0:T(1024)(128)(4,1)}), s8[4194304]{0:T(1024)(128)(4,1)S(1)}, s32[]{:S(2)}) async-start(s8[8388608]{0:T(1024)(128)(4,1)} %bitcast.67), calls=%async_computation.13 | async-start | bytes 8388608
  445.8 5.9 slice-start.1
  445.8 5.9 copy-start.21
  453.6 2.5 copy-start.19
  456.2 1.5 copy-start.17
  458.8 1.9 copy-start.4
  486.7 362.8 %all-reduce.7.cloned.1.call-start = ((), (), s32[]{:S(2)}) async-start(), calls=%async_computation.12 | async-start | bytes 33554432 | tf_op jit(solution)/shard_map/psum | solution.py:238
  486.9 9.6 %copy-start.37 = (bf16[1024,2048]{1,0:T(8,128)(2,1)S(1)}, bf16[1024,2048]{1,0:T(8,128)(2,1)}, u32[]{:S(2)}) copy-start(bf16[1024,2048]{1,0:T(8,128)(2,1)} %all-gather.7.cloned.1.call-done) | copy-start | bytes 12582916
  487.0 9.6 %copy-start.40 = (bf16[1024,1024]{1,0:T(8,128)(2,1)S(1)}, bf16[1024,1024]{1,0:T(8,128)(2,1)}, u32[]{:S(2)}) copy-start(bf16[1024,1024]{1,0:T(8,128)(2,1)} %copy-done.39) | copy-start | bytes 6291460
  487.0 9.6 %copy-start.42 = (bf16[1024,1024]{1,0:T(8,128)(2,1)S(1)}, bf16[1024,1024]{1,0:T(8,128)(2,1)}, u32[]{:S(2)}) copy-start(bf16[1024,1024]{1,0:T(8,128)(2,1)} %copy-done.41) | copy-start | bytes 6291460
  496.6 11.7 %copy-start.23 = (bf16[2,128,1024]{2,1,0:T(8,128)(2,1)S(1)}, bf16[2,128,1024]{2,1,0:T(8,128)(2,1)}, u32[]{:S(2)}) copy-start(bf16[2,128,1024]{2,1,0:T(8,128)(2,1)} %copy-done.22) | copy-start | bytes 1572868
  496.6 11.7 %copy-start.38 = (bf16[1024,2048]{1,0:T(8,128)(2,1)S(1)}, bf16[1024,2048]{1,0:T(8,128)(2,1)}, u32[]{:S(2)}) copy-start(bf16[1024,2048]{1,0:T(8,128)(2,1)} %all-gather.11.cloned.1.call-done) | copy-start | bytes 12582916
  508.2 2.3 copy-start.28
  508.2 2.3 copy-start.29
  508.2 2.9 copy-start.36
  517.4 49.6 %copy-start.13 = (bf16[128,2048]{1,0:T(8,128)(2,1)S(1)}, bf16[128,2048]{1,0:T(8,128)(2,1)}, u32[]{:S(2)}) copy-start(bf16[128,2048]{1,0:T(8,128)(2,1)} %reduce-scatter.9.cloned.1.call-done) | copy-start | bytes 1572868
  849.5 2.9 copy-start.6
  870.7 11.9 %copy-start.1 = (bf16[256,2048]{1,0:T(8,128)(2,1)S(1)}, bf16[256,2048]{1,0:T(8,128)(2,1)}, u32[]{:S(2)}) copy-start(bf16[256,2048]{1,0:T(8,128)(2,1)} %param.19) | copy-start | bytes 3145732
  (6 other events, 6.5 us)
Sparse Core Ops, SparseCore 0:
  9.6 49.8 all-gather.4
  96.8 48.1 reduce-scatter.4
  148.5 45.2 all-gather.6
  218.1 48.7 reduce-scatter.6
  271.9 45.2 all-gather.8
  343.7 48.7 reduce-scatter.8
  396.9 45.2 all-gather.10
  486.8 48.1 reduce-scatter.10
  540.1 309.3 all-reduce.6

commit v2 on v1

--- a/solution.py
+++ b/solution.py
@@ -1,6 +1,8 @@
 import jax
 import jax.numpy as jnp
 from jax import lax
+from jax.experimental import pallas as pl
+from jax.experimental.pallas import tpu as pltpu
 from jax.sharding import PartitionSpec as P
 
 HD = 128
@@ -257,6 +259,597 @@
     )
 
 
+MESH = pl.DeviceIdType.MESH
+LANES = 2
+
+
+def places_of():
+    d = lax.axis_index("dp")
+    t = lax.axis_index("tensor")
+    z, c = lax.div(t, 2), lax.rem(t, 2)
+    dx = d + 1 - 2 * lax.rem(d, 2)
+    dy = lax.rem(d + 2, 4)
+    zs = (z, z + 1 - 2 * lax.rem(z, 2), lax.rem(z + 2, 4), 3 - z)
+    inner = lax.rem(z + 1, 4) >= 2
+    return d, dx, dy, zs, c, inner
+
+
+def remote(src, dst, send, recv, dp, tensor):
+    return pltpu.make_async_remote_copy(
+        src_ref=src, dst_ref=dst, send_sem=send, recv_sem=recv, device_id=(dp, tensor), device_id_type=MESH
+    )
+
+
+def enter(d, zs, c, dx=None, dy=None):
+    barrier = pltpu.get_barrier_semaphore()
+    peers = [(d, 2 * zs[r] + c) for r in (1, 2, 3)] + [(d, 2 * zs[0] + 1 - c)]
+    if dx is not None:
+        peers += [(dx, 2 * zs[0] + c), (dy, 2 * zs[0] + c)]
+    for peer in peers:
+        pl.semaphore_signal(barrier, inc=1, device_id=peer, device_id_type=MESH)
+    pl.semaphore_wait(barrier, len(peers))
+
+
+class Gather:
+    def __init__(self, full, send, recv, place):
+        self.full, self.send, self.recv = full, send, recv
+        self.d, _, _, self.zs, self.c, self.inner = place
+        self.t = 2 * self.zs[0] + self.c
+
+    def lane(self, r):
+        return self.full.at[2 * self.zs[r] + self.c]
+
+    def other(self, r):
+        return self.full.at[2 * self.zs[r] + 1 - self.c]
+
+    def to_z(self, r, k, via):
+        return remote(self.lane(r), self.lane(r), self.send.at[via if r == 0 else 7], self.recv.at[k], self.d, 2 * self.zs[via] + self.c)
+
+    def to_core(self, r):
+        return remote(self.lane(r), self.lane(r), self.send.at[0 if r == 0 else 3 + r], self.recv.at[4 + r], self.d, 2 * self.zs[0] + 1 - self.c)
+
+    def start(self):
+        self.to_z(0, 2, 2).start()
+        self.to_z(0, 1, 1).start()
+        self.to_core(0).start()
+
+    def start_inner(self):
+        @pl.when(self.inner)
+        def _():
+            self.to_z(0, 2, 2).wait_send()
+            self.to_z(0, 3, 3).start()
+
+    def arrive(self, r):
+        self.to_z(r, r, r).wait_recv()
+        if r == 2:
+            @pl.when(self.inner)
+            def _():
+                self.to_z(2, 3, 1).start()
+        self.to_core(r).start()
+
+    def ready(self, r):
+        remote(self.other(r), self.other(r), self.send.at[0], self.recv.at[4 + r], self.d, self.t).wait_recv()
+
+    def finish(self):
+        @pl.when(jnp.logical_not(self.inner))
+        def _():
+            self.to_z(0, 2, 2).wait_send()
+
+        @pl.when(self.inner)
+        def _():
+            self.to_z(0, 3, 3).wait_send()
+            self.to_z(2, 3, 1).wait_send()
+
+        self.to_z(0, 1, 1).wait_send()
+        for r in range(4):
+            self.to_core(r).wait_send()
+
+
+class Scatter:
+    def __init__(self, parts, pair, land, send, recv, place):
+        self.parts, self.pair, self.land, self.send, self.recv = parts, pair, land, send, recv
+        self.d, _, _, self.zs, self.c, self.inner = place
+        self.t = 2 * self.zs[0] + self.c
+
+    def mine(self, r):
+        return self.parts.at[2 * self.zs[r] + self.c]
+
+    def to_core(self, r):
+        src = self.parts.at[2 * self.zs[r] + 1 - self.c]
+        return remote(src, self.pair.at[r], self.send.at[r], self.recv.at[r], self.d, 2 * self.zs[0] + 1 - self.c)
+
+    def to_z(self, r, k, via):
+        return remote(self.mine(r), self.land.at[k], self.send.at[4 + r], self.recv.at[4 + k], self.d, 2 * self.zs[via] + self.c)
+
+    def add_pair(self, r):
+        self.to_core(r).wait_recv()
+        add_into(self.mine(r), self.pair.at[r])
+
+    def pass_on(self, r):
+        if r == 1:
+            self.to_z(1, 1, 1).start()
+        if r == 2:
+            @pl.when(jnp.logical_not(self.inner))
+            def _():
+                self.to_z(2, 2, 2).start()
+        if r == 3:
+            @pl.when(self.inner)
+            def _():
+                self.to_z(3, 3, 3).start()
+
+            @pl.when(jnp.logical_not(self.inner))
+            def _():
+                self.to_z(3, 0, 1).start()
+
+    def relay(self):
+        @pl.when(self.inner)
+        def _():
+            self.to_z(3, 0, 1).wait_recv()
+            add_into(self.mine(2), self.land.at[0])
+            self.to_z(2, 2, 2).start()
+
+    def arrived(self):
+        self.to_z(1, 1, 1).wait_recv()
+        self.to_z(2, 2, 2).wait_recv()
+
+        @pl.when(self.inner)
+        def _():
+            self.to_z(3, 3, 3).wait_recv()
+
+        @pl.when(jnp.logical_not(self.inner))
+        def _():
+            self.land[3] = jnp.zeros(self.land.shape[1:], self.land.dtype)
+
+    def total(self, rows):
+        own = self.parts[2 * self.zs[0] + self.c, rows, :].astype(jnp.float32)
+        return own + self.land[1, rows, :].astype(jnp.float32) + self.land[2, rows, :].astype(jnp.float32) + self.land[3, rows, :].astype(jnp.float32)
+
+    def finish(self):
+        for r in range(4):
+            self.to_core(r).wait_send()
+        for r in (1, 2, 3):
+            self.to_z(r, 1, 1).wait_send()
+
+
+def add_into(into, other):
+    rows = into.shape[0]
+
+    def step(i, carry):
+        at = pl.ds(pl.multiple_of(i * 32, 32), 32)
+        into[at, :] = (into[at, :].astype(jnp.float32) + other[at, :].astype(jnp.float32)).astype(into.dtype)
+        return carry
+
+    lax.fori_loop(0, rows // 32, step, 0)
+
+
+class Spread:
+    def __init__(self, full, whole, send, recv, own_sem, place):
+        self.full, self.whole, self.send, self.recv, self.own_sem = full, whole, send, recv, own_sem
+        self.d, self.dx, self.dy, self.zs, self.c, _ = place
+        self.t = 2 * self.zs[0] + self.c
+        self.dd = 3 - self.d
+
+    def slot(self, g, r):
+        return self.whole.at[g, 2 * self.zs[r] + self.c]
+
+    def own(self, r, k):
+        src = self.full.at[2 * self.zs[r] + self.c]
+        return remote(src, self.slot(self.d, r), self.send.at[k * 4 + r], self.recv.at[k * 4 + r], (self.dx, self.dy)[k], self.t)
+
+    def start(self, r):
+        self.own(r, 0).start()
+        self.own(r, 1).start()
+
+    def hop(self, r):
+        group, target = (self.dx, self.dy) if r in (0, 3) else (self.dy, self.dx)
+        return remote(self.slot(group, r), self.slot(group, r), self.send.at[8 + r], self.recv.at[8 + r], target, self.t)
+
+    def to_core(self, r, k):
+        group = (self.dx, self.dy, self.dd)[k]
+        return remote(self.slot(group, r), self.slot(group, r), self.send.at[12 + k * 4 + r], self.recv.at[12 + k * 4 + r], self.d, 2 * self.zs[0] + 1 - self.c)
+
+    def pass_on(self, r):
+        remote(self.slot(self.dx, r), self.slot(self.dx, r), self.send.at[0], self.recv.at[r], self.dx, self.t).wait_recv()
+        remote(self.slot(self.dy, r), self.slot(self.dy, r), self.send.at[0], self.recv.at[4 + r], self.dy, self.t).wait_recv()
+        self.hop(r).start()
+        self.to_core(r, 0).start()
+        self.to_core(r, 1).start()
+
+    def last(self, r):
+        remote(self.slot(self.dd, r), self.slot(self.dd, r), self.send.at[0], self.recv.at[8 + r], self.dx, self.t).wait_recv()
+        self.to_core(r, 2).start()
+
+    def keep(self):
+        return pltpu.make_async_copy(self.full, self.whole.at[self.d], self.own_sem)
+
+    def finish(self):
+        for r in range(4):
+            self.own(r, 0).wait_send()
+            self.own(r, 1).wait_send()
+            self.hop(r).wait_send()
+            for k in range(3):
+                self.to_core(r, k).wait()
+        self.keep().wait()
+
+
+def dot_nt(left, right):
+    return lax.dot_general(left, right, (((1,), (1,)), ((), ())), preferred_element_type=jnp.float32)
+
+
+def ffn_kernel(
+    h_ref, hid_ref, cot_ref, gain_ref, wg_ref, wu_ref, wd_ref,
+    bo_ref, gh_ref, fg_ref, hall_ref, gdall_ref,
+    hfull, gfull, gate, up, act, gg, gu, parts, pair, land,
+    ag_send, ag_recv, rs_send, rs_recv, xy_send, xy_recv, own_sem,
+):
+    place = places_of()
+    d, dx, dy, zs, c, inner = place
+    t = 2 * zs[0] + c
+    width = wg_ref.shape[1]
+    wide = h_ref.shape[1]
+    rows = h_ref.shape[0]
+    ft, dt = 512, 1024
+    hfull[t] = h_ref[...]
+    enter(d, zs, c, dx, dy)
+
+    def unit_forward(zz):
+        both = pl.ds(2 * zz, 2)
+        at = pl.ds(pl.multiple_of(zz * 2 * rows, 2 * rows), 2 * rows)
+
+        def mid(j, carry):
+            cols = pl.ds(pl.multiple_of(j * ft, ft), ft)
+            block = hfull[both].reshape(2 * rows, wide)
+            g = jnp.dot(block, wg_ref[:, cols], preferred_element_type=jnp.float32)
+            u = jnp.dot(block, wu_ref[:, cols], preferred_element_type=jnp.float32)
+            gate[at, cols] = g
+            up[at, cols] = u
+            act[:, cols] = (g * jax.nn.sigmoid(g) * u).astype(jnp.bfloat16)
+            return carry
+
+        lax.fori_loop(0, width // ft, mid, 0)
+
+        def out(j, carry):
+            cols = pl.ds(pl.multiple_of(j * dt, dt), dt)
+            p = jnp.dot(act[...], wd_ref[:, cols], preferred_element_type=jnp.float32)
+            parts[both, :, cols] = p.astype(jnp.bfloat16).reshape(2, rows, dt)
+            return carry
+
+        lax.fori_loop(0, wide // dt, out, 0)
+
+    def unit_backward(zz):
+        both = pl.ds(2 * zz, 2)
+        at = pl.ds(pl.multiple_of(zz * 2 * rows, 2 * rows), 2 * rows)
+
+        def mid(j, carry):
+            cols = pl.ds(pl.multiple_of(j * ft, ft), ft)
+            block = gfull[both].reshape(2 * rows, wide)
+            ga = dot_nt(block, wd_ref[cols, :])
+            g, u = gate[at, cols], up[at, cols]
+            s = jax.nn.sigmoid(g)
+            gg[:, cols] = (ga * u * s * (1.0 + g * (1.0 - s))).astype(jnp.bfloat16)
+            gu[:, cols] = (ga * (g * s)).astype(jnp.bfloat16)
+            return carry
+
+        lax.fori_loop(0, width // ft, mid, 0)
+
+        def out(j, carry):
+            cols = pl.ds(pl.multiple_of(j * dt, dt), dt)
+            p = dot_nt(gg[...], wg_ref[cols, :]) + dot_nt(gu[...], wu_ref[cols, :])
+            parts[both, :, cols] = p.astype(jnp.bfloat16).reshape(2, rows, dt)
+            return carry
+
+        lax.fori_loop(0, wide // dt, out, 0)
+
+    def phase(p, full, whole, unit):
+        ag = Gather(full, ag_send.at[p], ag_recv.at[p], place)
+        rs = Scatter(parts, pair.at[p], land.at[p], rs_send.at[p], rs_recv.at[p], place)
+        xy = Spread(full, whole, xy_send.at[p], xy_recv.at[p], own_sem.at[p], place)
+        ag.start()
+        xy.start(0)
+        ag.ready(0)
+        unit(zs[0])
+        rs.to_core(0).start()
+        ag.start_inner()
+        ag.arrive(2)
+        xy.start(2)
+        ag.arrive(1)
+        xy.start(1)
+        ag.ready(2)
+        unit(zs[2])
+        rs.to_core(2).start()
+        ag.ready(1)
+        unit(zs[1])
+        rs.to_core(1).start()
+        rs.add_pair(2)
+        rs.pass_on(2)
+        rs.add_pair(1)
+        rs.pass_on(1)
+        ag.arrive(3)
+        xy.start(3)
+        ag.ready(3)
+        unit(zs[3])
+        rs.to_core(3).start()
+        xy.keep().start()
+        rs.add_pair(3)
+        rs.pass_on(3)
+        rs.add_pair(0)
+        xy.pass_on(0)
+        xy.pass_on(2)
+        xy.pass_on(1)
+        rs.relay()
+        rs.arrived()
+        return ag, rs, xy
+
+    ag, rs, xy_h = phase(0, hfull, hall_ref, unit_forward)
+    gain = gain_ref[...]
+    fg_ref[...] = jnp.zeros_like(fg_ref)
+    step_rows = 32
+
+    def middle(i, carry):
+        at = pl.ds(pl.multiple_of(i * step_rows, step_rows), step_rows)
+        down = rs.total(at)
+        inverse = lax.rsqrt(jnp.mean(down * down, axis=1, keepdims=True) + EPS)
+        unit = down * inverse
+        bo_ref[at, :] = (hid_ref[at, :] + unit * gain).astype(jnp.bfloat16)
+        grad = cot_ref[at, :].astype(jnp.float32)
+        fg_ref[...] += jnp.sum(grad * unit, axis=0, keepdims=True)
+        inner_grad = grad * gain
+        gfull[t, at, :] = (inverse * (inner_grad - unit * jnp.mean(inner_grad * unit, axis=1, keepdims=True))).astype(jnp.bfloat16)
+        return carry
+
+    lax.fori_loop(0, rows // step_rows, middle, 0)
+    ag.finish()
+    rs.finish()
+    xy_h.pass_on(3)
+    for r in range(4):
+        xy_h.last(r)
+    ag, rs, xy = phase(1, gfull, gdall_ref, unit_backward)
+
+    def ending(i, carry):
+        at = pl.ds(pl.multiple_of(i * step_rows, step_rows), step_rows)
+        gh_ref[at, :] = cot_ref[at, :].astype(jnp.float32) + rs.total(at)
+        return carry
+
+    lax.fori_loop(0, rows // step_rows, ending, 0)
+    ag.finish()
+    rs.finish()
+    xy.pass_on(3)
+    for r in range(4):
+        xy.last(r)
+    xy_h.finish()
+    xy.finish()
+
+
+def ffn(h_own, hidden, cot, gain, w_gate, w_up, w_down):
+    rows, wide = h_own.shape
+    width = w_gate.shape[1]
+    groups, world = 4, 8
+    vmem = pl.BlockSpec(memory_space=pltpu.VMEM)
+    anywhere = pl.BlockSpec(memory_space=pl.ANY)
+    bf, f32 = jnp.bfloat16, jnp.float32
+    whole = jax.ShapeDtypeStruct((groups, world, rows, wide), bf)
+    dma = pltpu.SemaphoreType.DMA
+    return pl.pallas_call(
+        ffn_kernel,
+        out_shape=(
+            jax.ShapeDtypeStruct((rows, wide), bf),
+            jax.ShapeDtypeStruct((rows, wide), f32),
+            jax.ShapeDtypeStruct((1, wide), f32),
+            whole,
+            whole,
+        ),
+        in_specs=[vmem] * 7,
+        out_specs=(vmem, vmem, vmem, anywhere, anywhere),
+        scratch_shapes=[
+            pltpu.VMEM((world, rows, wide), bf),
+            pltpu.VMEM((world, rows, wide), bf),
+            pltpu.VMEM((world * rows, width), f32),
+            pltpu.VMEM((world * rows, width), f32),
+            pltpu.VMEM((2 * rows, width), bf),
+            pltpu.VMEM((2 * rows, width), bf),
+            pltpu.VMEM((2 * rows, width), bf),
+            pltpu.VMEM((world, rows, wide), bf),
+            pltpu.VMEM((2, 4, rows, wide), bf),
+            pltpu.VMEM((2, 4, rows, wide), bf),
+            dma((2, 8)),
+            dma((2, 8)),
+            dma((2, 8)),
+            dma((2, 8)),
+            dma((2, 24)),
+            dma((2, 24)),
+            dma((2,)),
+        ],
+        compiler_params=pltpu.CompilerParams(
+            collective_id=2, has_side_effects=True, vmem_limit_bytes=60 * 2**20
+        ),
+        name="ffn",
+    )(h_own, hidden, cot, gain.reshape(1, wide), w_gate, w_up, w_down)
+
+
+def on_device_fused(
+    tokens,
+    segment_ids,
+    w_query,
+    w_key,
+    w_value,
+    w_out,
+    w_gate,
+    w_up,
+    w_down,
+    q_gain,
+    k_gain,
+    attn_gain,
+    ffn_gain,
+    cotangent,
+):
+    row_count, full_width = tokens.shape
+    head_cols = w_query.shape[1]
+    heads_here = head_cols // HD
+    ff_cols = w_gate.shape[1]
+    seqs_here, seq_len = segment_ids.shape
+    token_count = seqs_here * seq_len
+    att_scale = HD ** (-0.5)
+    whole_x = lax.all_gather(tokens, "tensor", axis=0, tiled=True)
+    w_qkv = jnp.concatenate([w_query, w_key, w_value], axis=1)
+    projected = jnp.dot(whole_x, w_qkv, preferred_element_type=jnp.float32)
+    q_raw = projected[:, :head_cols]
+    k_raw = projected[:, head_cols : 2 * head_cols]
+    values = projected[:, 2 * head_cols :].astype(jnp.bfloat16)
+    q_total, k_total = lax.psum(
+        (jnp.sum(q_raw * q_raw, axis=1), jnp.sum(k_raw * k_raw, axis=1)), "tensor"
+    )
+    q_inverse = lax.rsqrt(q_total / full_width + EPS)[:, None]
+    k_inverse = lax.rsqrt(k_total / full_width + EPS)[:, None]
+    q_unit = q_raw * q_inverse
+    k_unit = k_raw * k_inverse
+    cosine, sine = rotary_tables(positions_of(segment_ids).reshape(token_count))
+    queries = rotate((q_unit * q_gain).reshape(token_count, heads_here, HD), cosine, sine).astype(
+        jnp.bfloat16
+    )
+    keys = rotate((k_unit * k_gain).reshape(token_count, heads_here, HD), cosine, sine).astype(
+        jnp.bfloat16
+    )
+    shaped = (seqs_here, seq_len, heads_here, HD)
+    query_seqs = queries.reshape(shaped)
+    key_seqs = keys.reshape(shaped)
+    value_seqs = values.reshape(shaped)
+    places = jnp.arange(seq_len, dtype=jnp.int32)
+    causal = places[:, None] >= places[None, :]
+
+    def scores_of(query_block, key_block, seg_row):
+        raw = (
+            jnp.einsum("qhd,khd->hqk", query_block, key_block, preferred_element_type=jnp.float32)
+            * att_scale
+        )
+        allowed = causal & (seg_row[:, None] == seg_row[None, :])
+        return jnp.where(allowed[None], raw, -1e30)
+
+    def attend(pieces):
+        query_block, key_block, value_block, seg_row = pieces
+        scores = scores_of(query_block, key_block, seg_row)
+        top = jnp.max(scores, axis=-1, keepdims=True)
+        expo = jnp.exp(scores - top)
+        total = jnp.sum(expo, axis=-1, keepdims=True)
+        probs = (expo / total).astype(jnp.bfloat16)
+        mixed_block = jnp.einsum(
+            "hqk,khd->qhd", probs, value_block, preferred_element_type=jnp.float32
+        )
+        return (mixed_block.astype(jnp.bfloat16), (top + jnp.log(total))[..., 0])
+
+    mixed, log_total = lax.map(attend, (query_seqs, key_seqs, value_seqs, segment_ids))
+    mixed = mixed.reshape(token_count, head_cols)
+    x_rows = tokens.astype(jnp.float32)
+    branch = lax.psum_scatter(
+        jnp.dot(mixed, w_out, preferred_element_type=jnp.float32).astype(jnp.bfloat16),
+        "tensor",
+        scatter_dimension=0,
+        tiled=True,
+    ).astype(jnp.float32)
+    a_inverse = lax.rsqrt(jnp.mean(branch * branch, axis=1, keepdims=True) + EPS)
+    hidden = x_rows + branch * a_inverse * attn_gain
+    a_unit = branch * a_inverse
+    block_out, grad_hidden, grad_ffn_part, h_all, grad_down_all = ffn(
+        hidden.astype(jnp.bfloat16), hidden, cotangent, ffn_gain, w_gate, w_up, w_down
+    )
+    grad_ffn_part = grad_ffn_part[0]
+    h_all = h_all.reshape(-1, full_width)
+    grad_down_all = grad_down_all.reshape(-1, full_width)
+    gate = jnp.dot(h_all, w_gate, preferred_element_type=jnp.float32)
+    up = jnp.dot(h_all, w_up, preferred_element_type=jnp.float32)
+    sigma_gate = jax.nn.sigmoid(gate)
+    silu_gate = gate * sigma_gate
+    act = (silu_gate * up).astype(jnp.bfloat16)
+    grad_act = dot_last(grad_down_all, w_down)
+    grad_w_down = dot_first(act, grad_down_all)
+    grad_gate = grad_act * up * sigma_gate * (1.0 + gate * (1.0 - sigma_gate))
+    grad_up = grad_act * silu_gate
+    grad_w_gate = dot_first(h_all, grad_gate.astype(jnp.bfloat16))
+    grad_w_up = dot_first(h_all, grad_up.astype(jnp.bfloat16))
+    grad_attn_part = jnp.sum(grad_hidden * a_unit, axis=0)
+    grad_branch = norm_back(grad_hidden, a_unit, a_inverse, attn_gain).astype(jnp.bfloat16)
+    grad_branch_all = lax.all_gather(grad_branch, "tensor", axis=0, tiled=True)
+    grad_w_out = dot_first(mixed, grad_branch_all)
+    grad_mixed = dot_last(grad_branch_all, w_out).astype(jnp.bfloat16).reshape(shaped)
+
+    def attend_back(pieces):
+        query_block, key_block, value_block, seg_row, log_block, grad_block = pieces
+        scores = scores_of(query_block, key_block, seg_row)
+        probs = jnp.exp(scores - log_block[..., None])
+        grad_probs = jnp.einsum(
+            "qhd,khd->hqk", grad_block, value_block, preferred_element_type=jnp.float32
+        )
+        grad_scores = (
+            probs * (grad_probs - jnp.sum(probs * grad_probs, axis=-1, keepdims=True))
+        ).astype(jnp.bfloat16)
+        grad_query = (
+            jnp.einsum("hqk,khd->qhd", grad_scores, key_block, preferred_element_type=jnp.float32)
+            * att_scale
+        )
+        grad_key = (
+            jnp.einsum("hqk,qhd->khd", grad_scores, query_block, preferred_element_type=jnp.float32)
+            * att_scale
+        )
+        grad_value = jnp.einsum(
+            "hqk,qhd->khd",
+            probs.astype(jnp.bfloat16),
+            grad_block,
+            preferred_element_type=jnp.float32,
+        )
+        return (grad_query, grad_key, grad_value.astype(jnp.bfloat16))
+
+    grad_query, grad_key, grad_value = lax.map(
+        attend_back, (query_seqs, key_seqs, value_seqs, segment_ids, log_total, grad_mixed)
+    )
+    grad_q_normed = rotate_back(
+        rounded(grad_query.reshape(token_count, heads_here, HD)), cosine, sine
+    ).reshape(token_count, head_cols)
+    grad_k_normed = rotate_back(
+        rounded(grad_key.reshape(token_count, heads_here, HD)), cosine, sine
+    ).reshape(token_count, head_cols)
+    grad_q_gain = jnp.sum(grad_q_normed * q_unit, axis=0)
+    grad_k_gain = jnp.sum(grad_k_normed * k_unit, axis=0)
+    inner_q = grad_q_normed * q_gain
+    inner_k = grad_k_normed * k_gain
+    q_inner_sum, k_inner_sum = lax.psum(
+        (jnp.sum(inner_q * q_unit, axis=1), jnp.sum(inner_k * k_unit, axis=1)), "tensor"
+    )
+    grad_q_raw = q_inverse * (inner_q - q_unit * (q_inner_sum / full_width)[:, None])
+    grad_k_raw = k_inverse * (inner_k - k_unit * (k_inner_sum / full_width)[:, None])
+    grad_qkv = jnp.concatenate(
+        [
+            grad_q_raw.astype(jnp.bfloat16),
+            grad_k_raw.astype(jnp.bfloat16),
+            grad_value.reshape(token_count, head_cols),
+        ],
+        axis=1,
+    )
+    grad_w_qkv = dot_first(whole_x, grad_qkv)
+    grad_tokens = grad_hidden + lax.psum_scatter(
+        dot_last(grad_qkv, w_qkv).astype(jnp.bfloat16), "tensor", scatter_dimension=0, tiled=True
+    ).astype(jnp.float32)
+    grad_w_qkv, grad_w_out = [
+        lax.psum(part.astype(jnp.bfloat16), "dp").astype(jnp.float32)
+        for part in (grad_w_qkv, grad_w_out)
+    ]
+    grad_q_gain, grad_k_gain = lax.psum((grad_q_gain, grad_k_gain), "dp")
+    grad_attn_gain, grad_ffn_gain = lax.psum((grad_attn_part, grad_ffn_part), ("dp", "tensor"))
+    return (
+        block_out,
+        grad_tokens,
+        grad_w_qkv[:, :head_cols],
+        grad_w_qkv[:, head_cols : 2 * head_cols],
+        grad_w_qkv[:, 2 * head_cols :],
+        grad_w_out,
+        grad_w_gate,
+        grad_w_up,
+        grad_w_down,
+        grad_q_gain,
+        grad_k_gain,
+        grad_attn_gain,
+        grad_ffn_gain,
+    )
+
+
 def solution(mesh):
     placed = (
         P(("dp", "tensor"), None),
@@ -275,7 +868,7 @@
         P(("dp", "tensor"), None),
     )
     return jax.shard_map(
-        on_device,
+        on_device_fused if dict(mesh.shape) == {"dp": 4, "tensor": 8} else on_device,
         mesh=mesh,
         in_specs=placed,
         out_specs=(

time: 899 us -> 657 us (0.73)
  waiting for transfers between devices: 598 us -> 89.5 us
  Pallas kernels: 0 us -> 202 us
  matrix products: 107 us -> 208 us
  local copies, waits for them, and re-layouts: 49.7 us -> 25.4 us
  other arithmetic: 39.9 us -> 27.8 us
    psum x1, waiting for transfers between devices: 280 us -> 0.01 us  [on_device_fused(): lax.psum(part.astype(jnp.bfloat16), 'dp').astype(jnp.float32)]
    pallas_call x0 -> x1, Pallas kernels: none -> 202 us  [ffn(): pl.pallas_call(ffn_kernel, out_shape=(jax.ShapeDtypeStruct((rows, wide),...]
    all_gather x4 -> x2, waiting for transfers between devices: 171 us -> 40.7 us  [the longest x1 40.7 us: on_device_fused(): whole_x = lax.all_gather(tokens, 'tensor', axis=0, tiled=True)]
    reduce_scatter x4 -> x2, waiting for transfers between devices: 146 us -> 48 us  [the longest x1 48 us: on_device_fused(): lax.psum_scatter(jnp.dot(mixed, w_out, preferred_element_type=jnp.float32...]
    dot_general x4 -> x5, matrix products: 29.7 us -> 103 us  [dot_first(): lax.dot_general(left, right, (((0,), (0,)), ((), ())), preferred_element_...]
    dot_general x4, matrix products: 28.1 us -> 56.8 us  [the longest x1 23.8 us: on_device_fused(): up = jnp.dot(h_all, w_up, preferred_element_type=jnp.float32)]
    unnamed x96 -> x68, local copies, waits for them, and re-layouts: 31.2 us -> 17.3 us
    convert_element_type x8 -> x5, other arithmetic: 20.8 us -> 10.7 us  [the longest x1 2.79 us: on_device_fused(): lax.psum(part.astype(jnp.bfloat16), 'dp').astype(jnp.float32)]
  transfers between devices with their start and end apart: 9 -> 5, of which waited for: 8 -> 2; matrix products, arithmetic and copies ran while one was open for 5% -> 30% of each run, Pallas kernels for 0% -> 0%
where the time goes in v2:
time: 657 us; the launch traced here: 648 us
  matrix products  208 us (32%)
  Pallas kernels  202 us (31%)
  waiting for transfers between devices  89.5 us (14%)
  blocking collectives  80 us (12%)
  other arithmetic  27.8 us (4%)
  local copies, waits for them, and re-layouts  25.4 us (4%)
  between operations  14.8 us (2%)
    pallas_call x1, Pallas kernels, ffn(): pl.pallas_call(ffn_kernel, out_shape=(jax.ShapeDtypeStruct((rows, wide),...  202 us
    dot_general x5, matrix products, dot_first(): lax.dot_general(left, right, (((0,), (0,)), ((), ())), preferred_element_...  103 us
    reduce_scatter x1, waiting for transfers between devices, on_device_fused(): lax.psum_scatter(jnp.dot(mixed, w_out, preferred_element_type=jnp.float32...  48 us
    all_gather x1, waiting for transfers between devices, on_device_fused(): whole_x = lax.all_gather(tokens, 'tensor', axis=0, tiled=True)  40.7 us
    psum x1, blocking collectives, on_device_fused(): lax.psum((grad_attn_part, grad_ffn_part), ('dp', 'tensor'))  38.5 us
    dot_general x3, matrix products, dot_last(): lax.dot_general(left, right, (((1,), (1,)), ((), ())), preferred_element_...  33 us
    dot_general x1, matrix products, on_device_fused(): up = jnp.dot(h_all, w_up, preferred_element_type=jnp.float32)  23.8 us
    dot_general x1, matrix products, on_device_fused(): gate = jnp.dot(h_all, w_gate, preferred_element_type=jnp.float32)  23.5 us
  transfers between devices with their start and end apart: 5, of which 2 were waited for; matrix products, arithmetic and copies ran while one was open for 30% of the time, Pallas kernels for 0%

profile of v2, /device:TPU:0, one launch (start us, length us, event | category | flops | bytes accessed | tf_op | source)
XLA Modules:
  0.0 648.2 jit_solution(9087587702407489625)
XLA Ops:
  8.0 1.3 convert_reduce_fusion
  9.3 1.0 multiply_cosine_fusion
  10.4 2.3 constant_dynamic-update-slice_fusion.2
  12.7 2.3 constant_dynamic-update-slice_fusion.1
  15.0 2.3 constant_dynamic-update-slice_fusion
  17.2 1.6 fusion.9
  18.8 40.7 %all-gather.3.cloned.1.call-done = bf16[1024,2048]{1,0:T(8,128)(2,1)} async-done(((bf16[128,2048]{1,0:T(8,128)(2,1)}), bf16[1024,2048]{1,0:T(8,128)(2,1)}) %all-gather.3.cloned.1.call-update) | async-done | bytes 4194320 | tf_op jit(solution)/shard_map/all_gather | solution.py:692
  59.5 6.2 convolution_bitcast_fusion
  66.0 1.4 copy-done.3
  67.4 0.9 slice.96
  68.2 14.8 %all-reduce.2 = (f32[1024]{0:T(1024)S(1)}, f32[1024]{0:T(1024)S(1)}) all-reduce(f32[1024]{0:T(1024)S(1)} %get-tuple-element.113, f32[1024]{0:T(1024)S(1)} %get-tuple-element.112), channel_id=1, replica_groups=mesh['dp'=4,'tensor'=8] {'tensor'}, use_global_device_ids=true, to_apply=%region_1.0 | all-reduce | flops 2048 | bytes 16384 | tf_op jit(solution)/shard_map/psum | solution.py:698
  83.1 1.8 fusion.42
  85.8 3.2 fusion.53
  89.1 1.2 fusion.4
  90.2 1.6 fusion.18
  92.4 0.8 copy-done.10
  93.2 3.3 convolution_convert_fusion
  96.9 48.0 %reduce-scatter.3.cloned.1.call-done = bf16[128,2048]{1,0:T(8,128)(2,1)} async-done(((bf16[1024,2048]{1,0:T(8,128)(2,1)}), bf16[128,2048]{1,0:T(8,128)(2,1)}) %reduce-scatter.3.cloned.1.call-update) | async-done | bytes 524304 | tf_op jit(solution)/shard_map/reduce_scatter | solution.py:742
  144.9 1.2 fusion.32
  146.1 2.7 fusion.48
  148.8 202.3 %ffn.1 = (bf16[128,2048]{1,0:T(8,128)(2,1)}, f32[128,2048]{1,0:T(8,128)}, f32[1,2048]{1,0:T(1,128)}, bf16[4,8,128,2048]{3,2,1,0:T(8,128)(2,1)}, bf16[4,8,128,2048]{3,2,1,0:T(8,128)(2,1)}) custom-call(bf16[128,2048]{1,0:T(8,128)(2,1)} %get-tuple-element.126.h_ref, f32[128,2048]{1,0:T(8,128)} %get-tuple-element.127.hid_ref, bf16[128,2048]{1,0:T(8,128)(2,1)} %cot_ref.1, ...), custom_call_target="tpu_custom_call" | custom-call | tf_op jit(solution)/shard_map/ffn/pallas_call | solution.py:632
  351.2 2.2 fusion.31
  353.4 2.4 fusion.30
  356.2 23.5 %fusion.56 = f32[4096,1024]{1,0:T(8,128)} fusion(bf16[4096,2048]{1,0:T(8,128)(2,1)} %bitcast.88, bf16[2048,1024]{1,0:T(8,128)(2,1)} %wg_ref.1), kind=kOutput, calls=%fused_computation.113 | convolution fusion | flops 17179869184 | bytes 37748736 | tf_op jit(solution)/shard_map/dot_general | solution.py:757
  379.7 22.3 %fusion.54 = f32[4096,1024]{1,0:T(8,128)} fusion(bf16[4096,2048]{1,0:T(8,128)(2,1)} %bitcast.92, bf16[1024,2048]{1,0:T(8,128)(2,1)S(1)} %copy-done.7), kind=kOutput, calls=%fused_computation.111 | convolution fusion | flops 17179869184 | bytes 37748736 | tf_op jit(solution)/shard_map/dot_general | solution.py:20
  402.1 30.4 %fusion.1 = f32[2048,1024]{1,0:T(8,128)} fusion(bf16[4096,2048]{1,0:T(8,128)(2,1)} %bitcast.89, f32[4096,1024]{1,0:T(8,128)} %fusion.54, f32[4096,1024]{1,0:T(8,128)} %fusion.56), kind=kOutput, calls=%fused_computation.5 | convolution fusion | flops 17205035008 | bytes 58720256 | tf_op jit(solution)/shard_map/dot_general | solution.py:26
  432.5 3.6 convolution_convert_fusion.4
  436.1 5.9 fusion.21
  442.0 1.9 multiply_reduce_fusion
  443.9 2.7 multiply_convert_fusion.5
  446.6 1.5 fusion.24
  450.7 15.8 %all-reduce.1 = (f32[1024]{0:T(1024)S(1)}, f32[1024]{0:T(1024)S(1)}) all-reduce(f32[1024]{0:T(1024)S(1)} %get-tuple-element.107, f32[1024]{0:T(1024)S(1)} %get-tuple-element.110), channel_id=1, replica_groups=mesh['dp'=4,'tensor'=8] {'tensor'}, use_global_device_ids=true, to_apply=%region_14.15 | all-reduce | flops 2048 | bytes 16384 | tf_op jit(solution)/shard_map/psum | solution.py:813
  466.6 2.2 multiply_convert_fusion.8
  468.8 4.6 convolution_convert_fusion.3
  473.4 5.9 fusion.11
  479.5 23.8 %fusion.55 = f32[4096,1024]{1,0:T(8,128)} fusion(bf16[4096,2048]{1,0:T(8,128)(2,1)} %bitcast.90, bf16[2048,1024]{1,0:T(8,128)(2,1)} %wu_ref.1), kind=kOutput, calls=%fused_computation.112 | convolution fusion | flops 17179869184 | bytes 37748736 | tf_op jit(solution)/shard_map/dot_general | solution.py:758
  503.3 7.0 %convolution_convert_fusion.1 = bf16[1024,2048]{1,0:T(8,128)(2,1)} fusion(bf16[2048,768]{1,0:T(8,128)(2,1)} %constant_dynamic-update-slice_fusion, bf16[1024,256]{0,1:T(8,128)(2,1)S(1)} %bitcast.83, bf16[1024,256]{0,1:T(8,128)(2,1)S(1)} %copy-done.13, bf16[1024,256]{0,1:T(8,128)(2,1)S(1)} %get-tuple-element.131), kind=kOutput, calls=%fused_computation.23 | convolution fusion | flops 3228041216 | bytes 8912896 | tf_op jit(solution)/shard_map/dot_general | solution.py:20
  510.3 28.6 %fusion.2 = f32[1024,2048]{1,0:T(8,128)} fusion(bf16[4096,2048]{1,0:T(8,128)(2,1)} %bitcast.93, f32[4096,1024]{1,0:T(8,128)} %fusion.55, f32[4096,1024]{1,0:T(8,128)} %fusion.56), kind=kOutput, calls=%fused_computation.6 | convolution fusion | flops 17205035008 | bytes 58720256 | tf_op jit(solution)/shard_map/dot_general | solution.py:26
  538.9 38.5 %all-reduce = (f32[2048]{0:T(1024)}, f32[2048]{0:T(1024)}) all-reduce(f32[2048]{0:T(1024)S(1)} %copy-done.22, f32[2048]{0:T(1024)S(1)} %bitcast.87), channel_id=1, replica_groups=mesh['dp'=4,'tensor'=8] {'dp','tensor'}, use_global_device_ids=true, to_apply=%region_23.24 | all-reduce | flops 4096 | bytes 32768 | tf_op jit(solution)/shard_map/psum | solution.py:835
  577.4 33.5 %fusion.3 = f32[2048,1024]{1,0:T(8,128)} fusion(bf16[4096,2048]{1,0:T(8,128)(2,1)} %bitcast.91, f32[4096,1024]{1,0:T(8,128)} %fusion.56, f32[4096,1024]{1,0:T(8,128)} %fusion.54, f32[4096,1024]{1,0:T(8,128)} %fusion.55), kind=kOutput, calls=%fused_computation.13 | convolution fusion | flops 17221812224 | bytes 75497472 | tf_op jit(solution)/shard_map/dot_general | solution.py:26
  610.9 10.9 %all-reduce.3 = (f32[256]{0:T(256)}, f32[256]{0:T(256)}) all-reduce(f32[256]{0:T(256)S(1)} %get-tuple-element.111, f32[256]{0:T(256)S(1)} %get-tuple-element.106), channel_id=1, replica_groups=mesh['dp'=4,'tensor'=8] {'dp'}, use_global_device_ids=true, to_apply=%region_19.20 | all-reduce | flops 512 | bytes 4096 | tf_op jit(solution)/shard_map/psum | solution.py:834
  621.8 2.8 convert_element_type.154
  624.6 5.0 fusion.50
  629.5 3.0 copy.48
  632.5 2.9 copy.47
  635.4 2.9 copy.46
  638.3 2.1 convert_add_fusion
  640.4 0.8 copy.62
  (93 shorter events, 5.9 us)
Async XLA Ops:
  7.2 86.1 %copy-start = (bf16[256,2048]{1,0:T(8,128)(2,1)S(1)}, bf16[256,2048]{1,0:T(8,128)(2,1)}, u32[]{:S(2)}) copy-start(bf16[256,2048]{1,0:T(8,128)(2,1)} %param.19) | copy-start | bytes 3145732
  7.2 10.0 %copy-start.17 = (s32[1,1024]{1,0:T(1,128)S(1)}, s32[1,1024]{1,0:T(1,128)}, u32[]{:S(2)}) copy-start(s32[1,1024]{1,0:T(1,128)} %param.15) | copy-start | bytes 12292
  7.2 52.3 %all-gather.3.cloned.1.call-start = ((), (), s32[]{:S(2)}) async-start(), calls=%async_computation.2 | async-start | bytes 4718592 | tf_op jit(solution)/shard_map/all_gather | solution.py:692
  7.9 136.9 %reduce-scatter.3.cloned.1.call-start = ((), (), s32[]{:S(2)}) async-start(), calls=%async_computation.3 | async-start | bytes 4718592 | tf_op jit(solution)/shard_map/reduce_scatter | solution.py:742
  18.8 64.3 %copy-start.23 = (f32[256]{0:T(256)S(1)}, f32[256]{0:T(256)}, u32[]{:S(2)}) copy-start(f32[256]{0:T(256)} %param.24) | copy-start | bytes 3076
  18.8 64.3 %copy-start.25 = (f32[256]{0:T(256)S(1)}, f32[256]{0:T(256)}, u32[]{:S(2)}) copy-start(f32[256]{0:T(256)} %param.23) | copy-start | bytes 3076
  65.8 1.6 copy-start.3
  83.1 2.1 copy-start.18
  83.1 2.1 copy-start.20
  85.8 4.4 copy-start.8
  89.0 3.4 copy-start.2
  92.4 0.8 copy-start.10
  92.4 53.7 %copy-start.16 = (f32[2048]{0:T(1024)S(1)}, f32[2048]{0:T(1024)}, u32[]{:S(2)}) copy-start(f32[2048]{0:T(1024)} %param.25) | copy-start | bytes 24580
  96.6 335.9 %all-gather.5.cloned.1.call-start = ((), (), s32[]{:S(2)}) async-start(), calls=%async_computation.4 | async-start | bytes 4718592 | tf_op jit(solution)/shard_map/all_gather | solution.py:770
  146.1 205.0 %copy-start.6 = (bf16[128,2048]{1,0:T(8,128)(2,1)S(1)}, bf16[128,2048]{1,0:T(8,128)(2,1)}, u32[]{:S(2)}) copy-start(bf16[128,2048]{1,0:T(8,128)(2,1)} %reduce-scatter.3.cloned.1.call-done) | copy-start | bytes 1572868
  355.7 266.0 %all-reduce.7.cloned.1.call-start = ((), (), s32[]{:S(2)}) async-start(), calls=%async_computation.6 | async-start | bytes 8388608 | tf_op jit(solution)/shard_map/psum | solution.py:831
  356.2 23.5 %copy-start.7 = (bf16[1024,2048]{1,0:T(8,128)(2,1)S(1)}, bf16[1024,2048]{1,0:T(8,128)(2,1)}, u32[]{:S(2)}) copy-start(bf16[1024,2048]{1,0:T(8,128)(2,1)} %wd_ref.1) | copy-start | bytes 12582916
  432.5 9.5 %slice-start = ((s8[8388608]{0:T(1024)(128)(4,1)}), s8[4194304]{0:T(1024)(128)(4,1)S(1)}, s32[]{:S(2)}) async-start(s8[8388608]{0:T(1024)(128)(4,1)} %bitcast.70), calls=%async_computation.7 | async-start | bytes 8388608
  432.5 9.5 %copy-start.9 = (bf16[1024,256]{0,1:T(8,128)(2,1)S(1)}, bf16[1024,256]{0,1:T(8,128)(2,1)}, u32[]{:S(2)}) copy-start(bf16[1024,256]{0,1:T(8,128)(2,1)} %slice.96) | copy-start | bytes 1572868
  436.1 5.9 slice-start.1
  448.1 1.9 copy-start.4
  448.2 1.9 copy-start.19
  448.2 1.9 copy-start.21
  448.2 1.9 copy-start.24
  448.2 1.9 copy-start.26
  449.3 19.5 %copy-start.11 = (bf16[2,128,1024]{2,1,0:T(8,128)(2,1)S(1)}, bf16[2,128,1024]{2,1,0:T(8,128)(2,1)}, u32[]{:S(2)}) copy-start(bf16[2,128,1024]{2,1,0:T(8,128)(2,1)} %copy-done.10) | copy-start | bytes 1572868
  466.5 6.9 %copy-start.28 = (bf16[1024,2048]{1,0:T(8,128)(2,1)S(1)}, bf16[1024,2048]{1,0:T(8,128)(2,1)}, u32[]{:S(2)}) copy-start(bf16[1024,2048]{1,0:T(8,128)(2,1)} %all-gather.3.cloned.1.call-done) | copy-start | bytes 12582916
  468.8 4.6 copy-start.12
  479.4 23.9 %copy-start.13 = (bf16[1024,256]{0,1:T(8,128)(2,1)S(1)}, bf16[1024,256]{0,1:T(8,128)(2,1)}, u32[]{:S(2)}) copy-start(bf16[1024,256]{0,1:T(8,128)(2,1)} %copy-done.12) | copy-start | bytes 1572868
  479.4 23.9 %copy-start.15 = (bf16[2,128,1024]{2,1,0:T(8,128)(2,1)S(1)}, bf16[2,128,1024]{2,1,0:T(8,128)(2,1)}, u32[]{:S(2)}) copy-start(bf16[2,128,1024]{2,1,0:T(8,128)(2,1)} %fusion.21) | copy-start | bytes 1572868
  479.4 158.9 %reduce-scatter.5.cloned.1.call-start = ((), (), s32[]{:S(2)}) async-start(), calls=%async_computation.5 | async-start | bytes 4718592 | tf_op jit(solution)/shard_map/reduce_scatter | solution.py:827
  510.3 28.6 %copy-start.22 = (f32[2048]{0:T(1024)S(1)}, f32[2048]{0:T(1024)}, u32[]{:S(2)}) copy-start(f32[2048]{0:T(1024)} %get-tuple-element.114) | copy-start | bytes 24580
  510.3 28.6 %copy-start.27 = (f32[1,2048]{1,0:T(1,128)S(1)}, f32[1,2048]{1,0:T(1,128)}, u32[]{:S(2)}) copy-start(f32[1,2048]{1,0:T(1,128)} %get-tuple-element.79) | copy-start | bytes 24580
  624.6 16.6 %copy-start.1 = (bf16[256,2048]{1,0:T(8,128)(2,1)S(1)}, bf16[256,2048]{1,0:T(8,128)(2,1)}, u32[]{:S(2)}) copy-start(bf16[256,2048]{1,0:T(8,128)(2,1)} %param.19) | copy-start | bytes 3145732
  629.5 8.8 %copy-start.5 = (f32[128,2048]{1,0:T(8,128)S(1)}, f32[128,2048]{1,0:T(8,128)}, u32[]{:S(2)}) copy-start(f32[128,2048]{1,0:T(8,128)} %get-tuple-element.76) | copy-start | bytes 3145732
  629.5 10.9 %copy-start.14 = (bf16[128,2048]{1,0:T(8,128)(2,1)S(1)}, bf16[128,2048]{1,0:T(8,128)(2,1)}, u32[]{:S(2)}) copy-start(bf16[128,2048]{1,0:T(8,128)(2,1)} %get-tuple-element.172) | copy-start | bytes 1572868
Sparse Core Ops, SparseCore 0:
  9.6 49.8 all-gather.2
  96.7 48.1 reduce-scatter.2
  355.9 46.8 all-gather.4
  479.5 103.7 all-reduce.6
  585.5 49.9 reduce-scatter.4

commit v3 on v2

--- a/solution.py
+++ b/solution.py
@@ -427,40 +427,38 @@
         self.full, self.whole, self.send, self.recv, self.own_sem = full, whole, send, recv, own_sem
         self.d, self.dx, self.dy, self.zs, self.c, _ = place
         self.t = 2 * self.zs[0] + self.c
-        self.dd = 3 - self.d
 
     def slot(self, g, r):
         return self.whole.at[g, 2 * self.zs[r] + self.c]
 
     def own(self, r, k):
         src = self.full.at[2 * self.zs[r] + self.c]
-        return remote(src, self.slot(self.d, r), self.send.at[k * 4 + r], self.recv.at[k * 4 + r], (self.dx, self.dy)[k], self.t)
+        return remote(src, self.slot(1 + k, r), self.send.at[k * 4 + r], self.recv.at[k * 4 + r], (self.dx, self.dy)[k], self.t)
 
     def start(self, r):
         self.own(r, 0).start()
         self.own(r, 1).start()
 
     def hop(self, r):
-        group, target = (self.dx, self.dy) if r in (0, 3) else (self.dy, self.dx)
-        return remote(self.slot(group, r), self.slot(group, r), self.send.at[8 + r], self.recv.at[8 + r], target, self.t)
+        group, target = (1, self.dy) if r in (0, 3) else (2, self.dx)
+        return remote(self.slot(group, r), self.slot(3, r), self.send.at[8 + r], self.recv.at[8 + r], target, self.t)
 
     def to_core(self, r, k):
-        group = (self.dx, self.dy, self.dd)[k]
-        return remote(self.slot(group, r), self.slot(group, r), self.send.at[12 + k * 4 + r], self.recv.at[12 + k * 4 + r], self.d, 2 * self.zs[0] + 1 - self.c)
+        return remote(self.slot(1 + k, r), self.slot(1 + k, r), self.send.at[12 + k * 4 + r], self.recv.at[12 + k * 4 + r], self.d, 2 * self.zs[0] + 1 - self.c)
 
     def pass_on(self, r):
-        remote(self.slot(self.dx, r), self.slot(self.dx, r), self.send.at[0], self.recv.at[r], self.dx, self.t).wait_recv()
-        remote(self.slot(self.dy, r), self.slot(self.dy, r), self.send.at[0], self.recv.at[4 + r], self.dy, self.t).wait_recv()
+        self.own(r, 0).wait_recv()
+        self.own(r, 1).wait_recv()
         self.hop(r).start()
         self.to_core(r, 0).start()
         self.to_core(r, 1).start()
 
     def last(self, r):
-        remote(self.slot(self.dd, r), self.slot(self.dd, r), self.send.at[0], self.recv.at[8 + r], self.dx, self.t).wait_recv()
+        self.hop(r).wait_recv()
         self.to_core(r, 2).start()
 
     def keep(self):
-        return pltpu.make_async_copy(self.full, self.whole.at[self.d], self.own_sem)
+        return pltpu.make_async_copy(self.full, self.whole.at[0], self.own_sem)
 
     def finish(self):
         for r in range(4):
@@ -477,19 +475,30 @@
 
 
 def ffn_kernel(
-    h_ref, hid_ref, cot_ref, gain_ref, wg_ref, wu_ref, wd_ref,
-    bo_ref, gh_ref, fg_ref, hall_ref, gdall_ref,
-    hfull, gfull, gate, up, act, gg, gu, parts, pair, land,
+    x_ref, br_ref, cot_ref, again_ref, gain_ref, wg_ref, wu_ref, wd_ref,
+    bo_ref, gh_ref, gb_ref, gains_ref, act, gg, gu, hall_ref, gdall_ref,
+    hfull, gfull, hid_ref, sums, gate, up, parts, pair, land,
     ag_send, ag_recv, rs_send, rs_recv, xy_send, xy_recv, own_sem,
 ):
     place = places_of()
     d, dx, dy, zs, c, inner = place
     t = 2 * zs[0] + c
     width = wg_ref.shape[1]
-    wide = h_ref.shape[1]
-    rows = h_ref.shape[0]
+    rows, wide = x_ref.shape
     ft, dt = 512, 1024
-    hfull[t] = h_ref[...]
+    step_rows = 32
+    a_gain, gain = again_ref[...], gain_ref[...]
+
+    def opening(i, carry):
+        at = pl.ds(pl.multiple_of(i * step_rows, step_rows), step_rows)
+        branch = br_ref[at, :]
+        inverse = lax.rsqrt(jnp.mean(branch * branch, axis=1, keepdims=True) + EPS)
+        hidden = x_ref[at, :].astype(jnp.float32) + branch * inverse * a_gain
+        hid_ref[at, :] = hidden
+        hfull[t, at, :] = hidden.astype(jnp.bfloat16)
+        return carry
+
+    lax.fori_loop(0, rows // step_rows, opening, 0)
     enter(d, zs, c, dx, dy)
 
     def unit_forward(zz):
@@ -503,14 +512,14 @@
             u = jnp.dot(block, wu_ref[:, cols], preferred_element_type=jnp.float32)
             gate[at, cols] = g
             up[at, cols] = u
-            act[:, cols] = (g * jax.nn.sigmoid(g) * u).astype(jnp.bfloat16)
+            act[at, cols] = (g * jax.nn.sigmoid(g) * u).astype(jnp.bfloat16)
             return carry
 
         lax.fori_loop(0, width // ft, mid, 0)
 
         def out(j, carry):
             cols = pl.ds(pl.multiple_of(j * dt, dt), dt)
-            p = jnp.dot(act[...], wd_ref[:, cols], preferred_element_type=jnp.float32)
+            p = jnp.dot(act[at, :], wd_ref[:, cols], preferred_element_type=jnp.float32)
             parts[both, :, cols] = p.astype(jnp.bfloat16).reshape(2, rows, dt)
             return carry
 
@@ -526,15 +535,15 @@
             ga = dot_nt(block, wd_ref[cols, :])
             g, u = gate[at, cols], up[at, cols]
             s = jax.nn.sigmoid(g)
-            gg[:, cols] = (ga * u * s * (1.0 + g * (1.0 - s))).astype(jnp.bfloat16)
-            gu[:, cols] = (ga * (g * s)).astype(jnp.bfloat16)
+            gg[at, cols] = (ga * u * s * (1.0 + g * (1.0 - s))).astype(jnp.bfloat16)
+            gu[at, cols] = (ga * (g * s)).astype(jnp.bfloat16)
             return carry
 
         lax.fori_loop(0, width // ft, mid, 0)
 
         def out(j, carry):
             cols = pl.ds(pl.multiple_of(j * dt, dt), dt)
-            p = dot_nt(gg[...], wg_ref[cols, :]) + dot_nt(gu[...], wu_ref[cols, :])
+            p = dot_nt(gg[at, :], wg_ref[cols, :]) + dot_nt(gu[at, :], wu_ref[cols, :])
             parts[both, :, cols] = p.astype(jnp.bfloat16).reshape(2, rows, dt)
             return carry
 
@@ -581,9 +590,7 @@
         return ag, rs, xy
 
     ag, rs, xy_h = phase(0, hfull, hall_ref, unit_forward)
-    gain = gain_ref[...]
-    fg_ref[...] = jnp.zeros_like(fg_ref)
-    step_rows = 32
+    sums[...] = jnp.zeros_like(sums)
 
     def middle(i, carry):
         at = pl.ds(pl.multiple_of(i * step_rows, step_rows), step_rows)
@@ -592,7 +599,7 @@
         unit = down * inverse
         bo_ref[at, :] = (hid_ref[at, :] + unit * gain).astype(jnp.bfloat16)
         grad = cot_ref[at, :].astype(jnp.float32)
-        fg_ref[...] += jnp.sum(grad * unit, axis=0, keepdims=True)
+        sums[0:1, :] += jnp.sum(grad * unit, axis=0, keepdims=True)
         inner_grad = grad * gain
         gfull[t, at, :] = (inverse * (inner_grad - unit * jnp.mean(inner_grad * unit, axis=1, keepdims=True))).astype(jnp.bfloat16)
         return carry
@@ -607,10 +614,20 @@
 
     def ending(i, carry):
         at = pl.ds(pl.multiple_of(i * step_rows, step_rows), step_rows)
-        gh_ref[at, :] = cot_ref[at, :].astype(jnp.float32) + rs.total(at)
+        grad = cot_ref[at, :].astype(jnp.float32) + rs.total(at)
+        gh_ref[at, :] = grad
+        branch = br_ref[at, :]
+        inverse = lax.rsqrt(jnp.mean(branch * branch, axis=1, keepdims=True) + EPS)
+        unit = branch * inverse
+        sums[1:2, :] += jnp.sum(grad * unit, axis=0, keepdims=True)
+        inner_grad = grad * a_gain
+        gb_ref[at, :] = (inverse * (inner_grad - unit * jnp.mean(inner_grad * unit, axis=1, keepdims=True))).astype(jnp.bfloat16)
         return carry
 
     lax.fori_loop(0, rows // step_rows, ending, 0)
+    for i in range(wide // HD):
+        gains_ref[i : i + 1, :] = sums[0:1, i * HD : (i + 1) * HD]
+        gains_ref[wide // HD + i : wide // HD + i + 1, :] = sums[1:2, i * HD : (i + 1) * HD]
     ag.finish()
     rs.finish()
     xy.pass_on(3)
@@ -620,34 +637,36 @@
     xy.finish()
 
 
-def ffn(h_own, hidden, cot, gain, w_gate, w_up, w_down):
-    rows, wide = h_own.shape
+def ffn(x_own, branch, cot, attn_gain, ffn_gain, w_gate, w_up, w_down):
+    rows, wide = x_own.shape
     width = w_gate.shape[1]
     groups, world = 4, 8
     vmem = pl.BlockSpec(memory_space=pltpu.VMEM)
     anywhere = pl.BlockSpec(memory_space=pl.ANY)
     bf, f32 = jnp.bfloat16, jnp.float32
     whole = jax.ShapeDtypeStruct((groups, world, rows, wide), bf)
+    units = jax.ShapeDtypeStruct((world * rows, width), bf)
     dma = pltpu.SemaphoreType.DMA
     return pl.pallas_call(
         ffn_kernel,
         out_shape=(
             jax.ShapeDtypeStruct((rows, wide), bf),
             jax.ShapeDtypeStruct((rows, wide), f32),
-            jax.ShapeDtypeStruct((1, wide), f32),
+            jax.ShapeDtypeStruct((rows, wide), bf),
+            jax.ShapeDtypeStruct((2 * wide // HD, HD), f32),
+            units, units, units,
             whole,
             whole,
         ),
-        in_specs=[vmem] * 7,
-        out_specs=(vmem, vmem, vmem, anywhere, anywhere),
+        in_specs=[vmem] * 8,
+        out_specs=(vmem,) * 7 + (anywhere, anywhere),
         scratch_shapes=[
             pltpu.VMEM((world, rows, wide), bf),
             pltpu.VMEM((world, rows, wide), bf),
+            pltpu.VMEM((rows, wide), f32),
+            pltpu.VMEM((8, wide), f32),
             pltpu.VMEM((world * rows, width), f32),
             pltpu.VMEM((world * rows, width), f32),
-            pltpu.VMEM((2 * rows, width), bf),
-            pltpu.VMEM((2 * rows, width), bf),
-            pltpu.VMEM((2 * rows, width), bf),
             pltpu.VMEM((world, rows, wide), bf),
             pltpu.VMEM((2, 4, rows, wide), bf),
             pltpu.VMEM((2, 4, rows, wide), bf),
@@ -663,7 +682,695 @@
             collective_id=2, has_side_effects=True, vmem_limit_bytes=60 * 2**20
         ),
         name="ffn",
-    )(h_own, hidden, cot, gain.reshape(1, wide), w_gate, w_up, w_down)
+    )(x_own, branch, cot, attn_gain.reshape(1, wide), ffn_gain.reshape(1, wide), w_gate, w_up, w_down)
+
+
+WINDOW = 3
+
+
+class Exchange:
+    def __init__(self, block, land, send, recv, place):
+        self.block, self.land, self.send, self.recv = block, land, send, recv
+        self.d, _, _, self.zs, self.c, _ = place
+        self.t = 2 * self.zs[0] + self.c
+
+    def copies(self):
+        out = []
+        for r in range(4):
+            for k in range(2):
+                if r == 0 and k == 0:
+                    continue
+                at = 4 * k + r
+                core = self.c if k == 0 else 1 - self.c
+                out.append((2 * self.zs[r] + core, at))
+        return out
+
+    def start(self):
+        for peer, at in self.copies():
+            remote(self.block, self.land.at[self.t], self.send.at[at], self.recv.at[at], self.d, peer).start()
+
+    def wait(self):
+        for peer, at in self.copies():
+            remote(self.block, self.land.at[peer], self.send.at[at], self.recv.at[at], self.d, peer).wait()
+
+
+def enter_all(d, zs, c, dx, dy):
+    barrier = pltpu.get_barrier_semaphore()
+    peers = [(d, 2 * zs[r] + c) for r in (1, 2, 3)] + [(d, 2 * zs[r] + 1 - c) for r in range(4)]
+    peers += [(dx, 2 * zs[0] + c), (dy, 2 * zs[0] + c)]
+    for peer in peers:
+        pl.semaphore_signal(barrier, inc=1, device_id=peer, device_id_type=MESH)
+    pl.semaphore_wait(barrier, len(peers))
+
+
+def put_column(stat, base, zz, square):
+    rows = square.shape[0]
+    folded = square[:, :HD]
+    for h in range(1, square.shape[1] // HD):
+        folded = folded + square[:, h * HD : (h + 1) * HD]
+    line = jnp.sum(folded.T, axis=0, keepdims=True)
+    for i in range(rows // HD):
+        stat[pl.ds(base + 2 * zz + i, 1), :] = line[:, i * HD : (i + 1) * HD]
+
+
+def get_column(stat_row, count):
+    return jnp.broadcast_to(stat_row, (count, HD)).T
+
+
+def attn_kernel(
+    x_ref, wq_ref, wk_ref, wv_ref, wo_ref, qg_ref, kg_ref, cos_ref, sin_ref, first_ref,
+    br_ref, q_out, k_out, v_out, qu_out, ku_out, rq_out, rk_out, mixed_out, xall_ref,
+    xfull, parts, pair, land, stat, stats,
+    ag_send, ag_recv, rs_send, rs_recv, xy_send, xy_recv, st_send, st_recv, own_sem,
+):
+    place = places_of()
+    d, dx, dy, zs, c, inner = place
+    t = 2 * zs[0] + c
+    rows, wide = x_ref.shape
+    span = 2 * rows
+    heads = wq_ref.shape[1] // HD
+    xfull[t] = x_ref[...]
+    enter_all(d, zs, c, dx, dy)
+    ag = Gather(xfull, ag_send, ag_recv, place)
+    rs = Scatter(parts, pair, land, rs_send, rs_recv, place)
+    xy = Spread(xfull, xall_ref, xy_send, xy_recv, own_sem, place)
+    ex = Exchange(stat, stats, st_send, st_recv, place)
+
+    def at_of(zz):
+        return pl.ds(pl.multiple_of(zz * span, span), span)
+
+    def project_qk(zz):
+        block = xfull[pl.ds(2 * zz, 2)].reshape(span, wide)
+        for w_ref, out, base in ((wq_ref, qu_out, 0), (wk_ref, ku_out, 8)):
+            raw = jnp.dot(block, w_ref[...], preferred_element_type=jnp.float32)
+            out[at_of(zz), :] = raw
+            put_column(stat, base, zz, raw * raw)
+
+    def project_v(zz):
+        block = xfull[pl.ds(2 * zz, 2)].reshape(span, wide)
+        v_out[at_of(zz), :] = jnp.dot(block, wv_ref[...], preferred_element_type=jnp.float32).astype(jnp.bfloat16)
+
+    ag.start()
+    xy.start(0)
+    ag.ready(0)
+    project_qk(zs[0])
+    project_v(zs[0])
+    ag.start_inner()
+    ag.arrive(2)
+    xy.start(2)
+    ag.arrive(1)
+    xy.start(1)
+    ag.ready(2)
+    project_qk(zs[2])
+    ag.ready(1)
+    project_qk(zs[1])
+    project_v(zs[2])
+    ag.arrive(3)
+    xy.start(3)
+    ag.ready(3)
+    project_qk(zs[3])
+    ex.start()
+    project_v(zs[1])
+    project_v(zs[3])
+    xy.keep().start()
+    ex.wait()
+    total = stat[...]
+    for r in range(4):
+        for k in range(2):
+            if r or k:
+                total = total + stats[2 * zs[r] + (c if k == 0 else 1 - c)]
+    inverse = lax.rsqrt(total / (8 * wq_ref.shape[1]) + EPS)
+    rq_out[...] = inverse[:8]
+    rk_out[...] = inverse[8:]
+
+    def norm_rope(i, carry):
+        at = pl.ds(pl.multiple_of(i * HD, HD), HD)
+        cosine, sine = cos_ref[at, :], sin_ref[at, :]
+        for line, raw, out, gain in ((rq_out, qu_out, q_out, qg_ref), (rk_out, ku_out, k_out, kg_ref)):
+            scale = get_column(line[pl.ds(i, 1), :], HD)
+            for h in range(heads):
+                cols = slice(h * HD, (h + 1) * HD)
+                unit = raw[at, cols] * scale
+                raw[at, cols] = unit
+                normed = unit * gain[:, cols]
+                out[at, cols] = (normed * cosine + pltpu.roll(normed, HD // 2, 1) * sine).astype(jnp.bfloat16)
+        return carry
+
+    lax.fori_loop(0, 8, norm_rope, 0)
+
+    def attend(zz):
+        at = at_of(zz)
+        low = jnp.maximum(zz - (WINDOW - 1), 0) * span
+        keys_at = pl.ds(pl.multiple_of(low, span), WINDOW * span)
+        key_place = low + lax.broadcasted_iota(jnp.int32, (span, WINDOW * span), 1)
+        query_place = zz * span + lax.broadcasted_iota(jnp.int32, (span, WINDOW * span), 0)
+        allowed = (key_place <= query_place) & (key_place >= first_ref[at, :])
+        for h in range(heads):
+            cols = slice(h * HD, (h + 1) * HD)
+            scores = dot_nt(q_out[at, cols], k_out[keys_at, cols]) * HD**-0.5
+            scores = jnp.where(allowed, scores, -1e30)
+            top = jnp.max(scores, axis=1, keepdims=True)
+            expo = jnp.exp(scores - top)
+            probs = expo * (1.0 / jnp.sum(expo, axis=1, keepdims=True))
+            mixed_out[at, cols] = jnp.dot(probs.astype(jnp.bfloat16), v_out[keys_at, cols], preferred_element_type=jnp.float32).astype(jnp.bfloat16)
+        dt = 1024
+
+        def out(j, carry):
+            to = pl.ds(pl.multiple_of(j * dt, dt), dt)
+            p = jnp.dot(mixed_out[at, :], wo_ref[:, to], preferred_element_type=jnp.float32)
+            parts[pl.ds(2 * zz, 2), :, to] = p.astype(jnp.bfloat16).reshape(2, rows, dt)
+            return carry
+
+        lax.fori_loop(0, wide // dt, out, 0)
+
+    attend(zs[3])
+    rs.to_core(3).start()
+    attend(zs[2])
+    rs.to_core(2).start()
+    rs.add_pair(3)
+    rs.pass_on(3)
+    attend(zs[1])
+    rs.to_core(1).start()
+    rs.add_pair(2)
+    rs.pass_on(2)
+    rs.add_pair(1)
+    rs.pass_on(1)
+    attend(zs[0])
+    rs.to_core(0).start()
+    rs.add_pair(0)
+    xy.pass_on(0)
+    xy.pass_on(2)
+    xy.pass_on(1)
+    rs.relay()
+    xy.pass_on(3)
+    for r in range(4):
+        xy.last(r)
+    rs.arrived()
+
+    def ending(i, carry):
+        at = pl.ds(pl.multiple_of(i * 32, 32), 32)
+        br_ref[at, :] = rs.total(at)
+        return carry
+
+    lax.fori_loop(0, rows // 32, ending, 0)
+    ag.finish()
+    rs.finish()
+    xy.finish()
+
+
+def attention(x_own, w_query, w_key, w_value, w_out, q_gain, k_gain, cosine, sine, first):
+    rows, wide = x_own.shape
+    head_cols = w_query.shape[1]
+    groups, world = 4, 8
+    count = world * rows
+    vmem = pl.BlockSpec(memory_space=pltpu.VMEM)
+    bf, f32 = jnp.bfloat16, jnp.float32
+    dma = pltpu.SemaphoreType.DMA
+    cols = jax.ShapeDtypeStruct((count, head_cols), bf)
+    wide_cols = jax.ShapeDtypeStruct((count, head_cols), f32)
+    line = jax.ShapeDtypeStruct((8, HD), f32)
+    return pl.pallas_call(
+        attn_kernel,
+        out_shape=(
+            jax.ShapeDtypeStruct((rows, wide), f32),
+            cols, cols, cols, wide_cols, wide_cols, line, line, cols,
+            jax.ShapeDtypeStruct((groups, world, rows, wide), bf),
+        ),
+        in_specs=[vmem] * 10,
+        out_specs=(vmem,) * 9 + (pl.BlockSpec(memory_space=pl.ANY),),
+        scratch_shapes=[
+            pltpu.VMEM((world, rows, wide), bf),
+            pltpu.VMEM((world, rows, wide), bf),
+            pltpu.VMEM((4, rows, wide), bf),
+            pltpu.VMEM((4, rows, wide), bf),
+            pltpu.VMEM((16, HD), f32),
+            pltpu.VMEM((world, 16, HD), f32),
+            dma((8,)), dma((8,)), dma((8,)), dma((8,)), dma((24,)), dma((24,)), dma((8,)), dma((8,)),
+            pltpu.SemaphoreType.DMA,
+        ],
+        compiler_params=pltpu.CompilerParams(
+            collective_id=1, has_side_effects=True, vmem_limit_bytes=60 * 2**20
+        ),
+        name="attn",
+    )(x_own, w_query, w_key, w_value, w_out, q_gain.reshape(1, -1), k_gain.reshape(1, -1), cosine, sine, first)
+
+
+def dot_tn(left, right):
+    return lax.dot_general(left, right, (((0,), (0,)), ((), ())), preferred_element_type=jnp.float32)
+
+
+class Background:
+    tokens, units = 512, 512
+
+    def __init__(self, hall, gdall, weights, outs, hbuf, gbuf, tiles, sums, mids, load_sem, tile_sem, out_sem):
+        self.hall, self.gdall, self.weights, self.outs = hall, gdall, weights, outs
+        self.hbuf, self.gbuf, self.tiles, self.sums, self.mids = hbuf, gbuf, tiles, sums, mids
+        self.load_sem, self.tile_sem, self.out_sem = load_sem, tile_sem, out_sem
+        self.blocks = self.tokens // hall.shape[2]
+        self.per_group = hall.shape[1] // self.blocks
+        self.per_tile = 3 * self.per_group
+        self.tile_count = weights[0].shape[1] // self.units
+        self.count = self.tile_count * self.per_tile
+
+    def loads(self, n):
+        slot, m = n % 2, n % self.per_tile
+        group, part = 1 + m // self.per_group, m % self.per_group
+        blocks = pl.ds(part * self.blocks, self.blocks)
+        return (
+            pltpu.make_async_copy(self.hall.at[group, blocks], self.hbuf.at[slot], self.load_sem.at[0, slot]),
+            pltpu.make_async_copy(self.gdall.at[group, blocks], self.gbuf.at[slot], self.load_sem.at[1, slot]),
+        )
+
+    def tile_loads(self, tile):
+        at = pl.ds(tile * self.units, self.units)
+        wg, wu, wd = self.weights
+        return (
+            pltpu.make_async_copy(wg.at[:, at], self.tiles[0], self.tile_sem.at[0]),
+            pltpu.make_async_copy(wu.at[:, at], self.tiles[1], self.tile_sem.at[1]),
+            pltpu.make_async_copy(wd.at[at, :], self.tiles[2], self.tile_sem.at[2]),
+        )
+
+    def stores(self, tile):
+        at = pl.ds(tile * self.units, self.units)
+        og, ou, od = self.outs
+        return (
+            pltpu.make_async_copy(self.sums[0], og.at[:, at], self.out_sem.at[0]),
+            pltpu.make_async_copy(self.sums[1], ou.at[:, at], self.out_sem.at[1]),
+            pltpu.make_async_copy(self.sums[2], od.at[at, :], self.out_sem.at[2]),
+        )
+
+    def begin(self):
+        for copy in self.tile_loads(0) + self.loads(0):
+            copy.start()
+
+    def step(self, n):
+        slot, tile, m = n % 2, n // self.per_tile, n % self.per_tile
+        if n + 1 < self.count:
+            for copy in self.loads(n + 1):
+                copy.start()
+        if m == 0:
+            for copy in self.tile_loads(tile):
+                copy.wait()
+            if tile:
+                for copy in self.stores(tile - 1):
+                    copy.wait()
+        for copy in self.loads(n):
+            copy.wait()
+        hbuf, gbuf = self.hbuf.at[slot], self.gbuf.at[slot]
+        wg, wu, wd = self.tiles
+        act, gg, gu = self.mids
+        rows, wide = hbuf.shape[1:]
+        half = self.tokens // 2
+
+        def mid(i, carry):
+            blocks = pl.ds(i * (self.blocks // 2), self.blocks // 2)
+            at = pl.ds(pl.multiple_of(i * half, half), half)
+            h = hbuf[blocks].reshape(half, wide)
+            g = jnp.dot(h, wg[...], preferred_element_type=jnp.float32)
+            u = jnp.dot(h, wu[...], preferred_element_type=jnp.float32)
+            ga = dot_nt(gbuf[blocks].reshape(half, wide), wd[...])
+            s = jax.nn.sigmoid(g)
+            gs = g * s
+            act[at, :] = (gs * u).astype(jnp.bfloat16)
+            gg[at, :] = (ga * u * s * (1.0 + g * (1.0 - s))).astype(jnp.bfloat16)
+            gu[at, :] = (ga * gs).astype(jnp.bfloat16)
+            return carry
+
+        lax.fori_loop(0, 2, mid, 0)
+        span = 512
+
+        def into(i, carry):
+            at = pl.ds(pl.multiple_of(i * span, span), span)
+            h = hbuf[:, :, at].reshape(self.tokens, span)
+            pg = dot_tn(h, gg[...])
+            pu = dot_tn(h, gu[...])
+            pd = dot_tn(act[...], gbuf[:, :, at].reshape(self.tokens, span))
+            if m == 0:
+                self.sums[0][at, :], self.sums[1][at, :], self.sums[2][:, at] = pg, pu, pd
+            else:
+                self.sums[0][at, :] += pg
+                self.sums[1][at, :] += pu
+                self.sums[2][:, at] += pd
+            return carry
+
+        lax.fori_loop(0, wide // span, into, 0)
+        if m == self.per_tile - 1:
+            for copy in self.stores(tile):
+                copy.start()
+            if tile + 1 < self.tile_count:
+                for copy in self.tile_loads(tile + 1):
+                    copy.start()
+
+    def finish(self):
+        for copy in self.stores(self.tile_count - 1):
+            copy.wait()
+
+
+class SpreadColumns:
+    def __init__(self, own, whole, send, recv, own_sem, place):
+        self.src, self.whole, self.send, self.recv, self.own_sem = own, whole, send, recv, own_sem
+        self.d, self.dx, self.dy, self.zs, self.c, _ = place
+        self.t = 2 * self.zs[0] + self.c
+
+    def own(self, p, k):
+        return remote(self.src.at[p], self.whole.at[1 + k, p], self.send.at[k * 3 + p], self.recv.at[k * 3 + p], (self.dx, self.dy)[k], self.t)
+
+    def hop(self, p, b):
+        half = self.src.shape[1] // 2
+        at = pl.ds(b * half, half)
+        return remote(self.whole.at[1 + b, p, at], self.whole.at[3, p, at], self.send.at[6 + 2 * p + b], self.recv.at[6 + 2 * p + b], (self.dy, self.dx)[b], self.t)
+
+    def start(self, p):
+        self.own(p, 0).start()
+        self.own(p, 1).start()
+
+    def pass_on(self, p):
+        for b in range(2):
+            self.own(p, b).wait_recv()
+            self.hop(p, b).start()
+
+    def keep(self):
+        return pltpu.make_async_copy(self.src, self.whole.at[0], self.own_sem)
+
+    def finish(self):
+        for p in range(3):
+            for b in range(2):
+                self.own(p, b).wait_send()
+                self.hop(p, b).wait()
+        self.keep().wait()
+
+
+class SumHalves:
+    def __init__(self, buf, once, twice, send, recv, place):
+        self.buf, self.land, self.send, self.recv = buf, (once, twice), send, recv
+        self.d, self.dx, self.dy, self.zs, self.c, _ = place
+        self.t = 2 * self.zs[0] + self.c
+
+    def move(self, stage, b):
+        at = 2 * stage + b
+        return remote(self.buf.at[b], self.land[stage].at[b], self.send.at[at], self.recv.at[at], (self.dx, self.dy)[(stage + b) % 2], self.t)
+
+    def start(self, stage):
+        for b in range(2):
+            self.move(stage, b).start()
+
+    def add(self, stage):
+        for b in range(2):
+            self.move(stage, b).wait()
+            add_into(self.buf.at[b], self.land[stage].at[b])
+
+
+class ExchangeGroups:
+    def __init__(self, block, land, send, recv, place):
+        self.block, self.land, self.send, self.recv = block, land, send, recv
+        d, dx, dy, zs, c, _ = place
+        self.peers, self.t = (dx, dy, 3 - d), 2 * zs[0] + c
+
+    def copies(self):
+        return [remote(self.block, self.land.at[k], self.send.at[k], self.recv.at[k], peer, self.t) for k, peer in enumerate(self.peers)]
+
+    def start(self):
+        for copy in self.copies():
+            copy.start()
+
+    def wait(self):
+        for copy in self.copies():
+            copy.wait()
+
+
+def back_kernel(
+    gb_ref, gh_ref, q_ref, k_ref, v_ref, mixed_ref, qu_ref, ku_ref, rq_ref, rk_ref, first_ref, cos_ref, sin_ref,
+    qg_ref, kg_ref, wq_ref, wk_ref, wv_ref, wo_ref, gains_ref, hall, gdall, wg, wu, wd,
+    gt_ref, gains_out, dwo_ref, gall_ref, dwg, dwu, dwd,
+    full, pair, land, gm, dq, dk, dv, own, wo_once, wo_twice, stat, stats, gland, block, blocks, gacc,
+    hbuf, gbuf, tg, tu, td, sg, su, sd, act, gg, gu,
+    ag_send, ag_recv, rs_send, rs_recv, st_send, st_recv, ga_send, ga_recv, gr_send, gr_recv,
+    co_send, co_recv, wo_send, wo_recv, own_sem, load_sem, tile_sem, out_sem,
+):
+    place = places_of()
+    d, dx, dy, zs, c, inner = place
+    t = 2 * zs[0] + c
+    rows, wide = gb_ref.shape
+    span = 2 * rows
+    heads = wq_ref.shape[1] // HD
+    count = q_ref.shape[0]
+    scale = HD**-0.5
+    full[t] = gb_ref[...]
+    barrier = pltpu.get_barrier_semaphore()
+    peers = [(d, 2 * zs[r] + c) for r in (1, 2, 3)] + [(d, 2 * zs[r] + 1 - c) for r in range(4)]
+    peers += [(dx, t), (dy, t), (3 - d, t)]
+    for peer in peers:
+        pl.semaphore_signal(barrier, inc=1, device_id=peer, device_id_type=MESH)
+    pl.semaphore_wait(barrier, len(peers))
+    ag = Gather(full, ag_send, ag_recv, place)
+    rs = Scatter(full, pair, land, rs_send, rs_recv, place)
+    ex = Exchange(stat, stats, st_send, st_recv, place)
+    gains = Exchange(gains_ref, gland, ga_send, ga_recv, place)
+    groups = ExchangeGroups(block, blocks, gr_send, gr_recv, place)
+    cols_all = SpreadColumns(own, gall_ref, co_send, co_recv, own_sem, place)
+    wo_sum = SumHalves(dwo_ref, wo_once, wo_twice, wo_send, wo_recv, place)
+    work = Background(hall, gdall, (wg, wu, wd), (dwg, dwu, dwd), hbuf, gbuf, (tg, tu, td), (sg, su, sd), (act, gg, gu), load_sem, tile_sem, out_sem)
+
+    def at_of(zz):
+        return pl.ds(pl.multiple_of(zz * span, span), span)
+
+    ag.start()
+    gains.start()
+    work.begin()
+    work.step(0)
+    work.step(1)
+    ag.ready(0)
+    ag.start_inner()
+    ag.arrive(2)
+    ag.arrive(1)
+    work.step(2)
+    work.step(3)
+    ag.ready(2)
+    ag.ready(1)
+    ag.arrive(3)
+    work.step(4)
+    work.step(5)
+    ag.ready(3)
+
+    def mixed_back(zz, carry):
+        part = full[pl.ds(2 * zz, 2)].reshape(span, wide)
+        gm[at_of(zz), :] = dot_nt(part, wo_ref[...]).astype(jnp.bfloat16)
+        return carry
+
+    lax.fori_loop(0, 4, mixed_back, 0)
+
+    def out_back(j, carry):
+        to = pl.ds(pl.multiple_of(j * 512, 512), 512)
+        p = dot_tn(mixed_ref[...], full[:, :, to].reshape(count, 512))
+        dwo_ref[:, :, to] = p.astype(jnp.bfloat16).reshape(2, p.shape[0] // 2, 512)
+        return carry
+
+    lax.fori_loop(0, wide // 512, out_back, 0)
+    wo_sum.start(0)
+    ag.finish()
+    dk[...] = jnp.zeros_like(dk)
+    dv[...] = jnp.zeros_like(dv)
+
+    def attend_back(zz, carry):
+        at = at_of(zz)
+        low = jnp.maximum(zz - (WINDOW - 1), 0) * span
+        keys_at = pl.ds(pl.multiple_of(low, span), WINDOW * span)
+        key_place = low + lax.broadcasted_iota(jnp.int32, (span, WINDOW * span), 1)
+        query_place = zz * span + lax.broadcasted_iota(jnp.int32, (span, WINDOW * span), 0)
+        allowed = (key_place <= query_place) & (key_place >= first_ref[at, :])
+        for h in range(heads):
+            cols = slice(h * HD, (h + 1) * HD)
+            scores = dot_nt(q_ref[at, cols], k_ref[keys_at, cols]) * scale
+            scores = jnp.where(allowed, scores, -1e30)
+            top = jnp.max(scores, axis=1, keepdims=True)
+            expo = jnp.exp(scores - top)
+            probs = expo * (1.0 / jnp.sum(expo, axis=1, keepdims=True))
+            grad = gm[at, cols]
+            gp = dot_nt(grad, v_ref[keys_at, cols])
+            gs = (probs * (gp - jnp.sum(probs * gp, axis=1, keepdims=True))).astype(jnp.bfloat16)
+            dq[at, cols] = jnp.dot(gs, k_ref[keys_at, cols], preferred_element_type=jnp.float32) * scale
+            dk[keys_at, cols] += dot_tn(gs, q_ref[at, cols]) * scale
+            dv[keys_at, cols] += dot_tn(probs.astype(jnp.bfloat16), grad)
+        return carry
+
+    lax.fori_loop(0, 4, attend_back, 0)
+    own[2] = dv[...].astype(jnp.bfloat16)
+    cols_all.start(2)
+    wo_sum.add(0)
+    wo_sum.start(1)
+    gacc[...] = jnp.zeros_like(gacc)
+
+    def unrope(i, carry):
+        at = pl.ds(pl.multiple_of(i * HD, HD), HD)
+        cosine, sine = cos_ref[at, :], sin_ref[at, :]
+        for n, (grad, unit_ref, gain) in enumerate(((dq, qu_ref, qg_ref), (dk, ku_ref, kg_ref))):
+            total = jnp.zeros((HD, HD), jnp.float32)
+            for h in range(heads):
+                cols = slice(h * HD, (h + 1) * HD)
+                value = grad[at, cols].astype(jnp.bfloat16).astype(jnp.float32)
+                value = value * cosine - pltpu.roll(value, HD // 2, 1) * sine
+                unit = unit_ref[at, cols]
+                row = n * heads + h
+                gacc[row : row + 1, :] += jnp.sum(value * unit, axis=0, keepdims=True)
+                value = value * gain[:, cols]
+                grad[at, cols] = value
+                total = total + value * unit
+            stat[pl.ds(8 * n + i, 1), :] = jnp.sum(total.T, axis=0, keepdims=True)
+        return carry
+
+    lax.fori_loop(0, count // HD, unrope, 0)
+    ex.start()
+    gains.wait()
+    total = gains_ref[...]
+    for r in range(4):
+        for k in range(2):
+            if r or k:
+                total = total + gland[2 * zs[r] + (c if k == 0 else 1 - c)]
+    lines = gains_ref.shape[0]
+    block[:lines, :] = total
+    block[lines:, :] = gacc[...]
+    groups.start()
+    work.step(6)
+    ex.wait()
+    total = stat[...]
+    for r in range(4):
+        for k in range(2):
+            if r or k:
+                total = total + stats[2 * zs[r] + (c if k == 0 else 1 - c)]
+    stat[...] = total * (1.0 / (8 * wq_ref.shape[1]))
+
+    def norm_back_rows(i, carry):
+        at = pl.ds(pl.multiple_of(i * HD, HD), HD)
+        for n, (grad, unit_ref, inv_ref) in enumerate(((dq, qu_ref, rq_ref), (dk, ku_ref, rk_ref))):
+            mean = get_column(stat[pl.ds(8 * n + i, 1), :], HD)
+            inverse = get_column(inv_ref[pl.ds(i, 1), :], HD)
+            for h in range(heads):
+                cols = slice(h * HD, (h + 1) * HD)
+                own[n, at, cols] = (inverse * (grad[at, cols] - unit_ref[at, cols] * mean)).astype(jnp.bfloat16)
+        return carry
+
+    lax.fori_loop(0, count // HD, norm_back_rows, 0)
+    cols_all.start(0)
+    cols_all.start(1)
+    cols_all.keep().start()
+
+    def tokens_back(zz):
+        at = at_of(zz)
+        dt = 1024
+
+        def out(j, carry):
+            to = pl.ds(pl.multiple_of(j * dt, dt), dt)
+            p = dot_nt(own[0, at, :], wq_ref[to, :]) + dot_nt(own[1, at, :], wk_ref[to, :]) + dot_nt(own[2, at, :], wv_ref[to, :])
+            full[pl.ds(2 * zz, 2), :, to] = p.astype(jnp.bfloat16).reshape(2, rows, dt)
+            return carry
+
+        lax.fori_loop(0, wide // dt, out, 0)
+
+    tokens_back(zs[3])
+    rs.to_core(3).start()
+    tokens_back(zs[2])
+    rs.to_core(2).start()
+    rs.add_pair(3)
+    rs.pass_on(3)
+    tokens_back(zs[1])
+    rs.to_core(1).start()
+    rs.add_pair(2)
+    rs.pass_on(2)
+    rs.add_pair(1)
+    rs.pass_on(1)
+    tokens_back(zs[0])
+    rs.to_core(0).start()
+    rs.add_pair(0)
+    cols_all.pass_on(2)
+    wo_sum.add(1)
+    work.step(7)
+    rs.relay()
+    work.step(8)
+    work.step(9)
+    cols_all.pass_on(0)
+    cols_all.pass_on(1)
+    work.step(10)
+    work.step(11)
+    rs.arrived()
+
+    def ending(i, carry):
+        at = pl.ds(pl.multiple_of(i * 32, 32), 32)
+        gt_ref[at, :] = gh_ref[at, :] + rs.total(at)
+        return carry
+
+    lax.fori_loop(0, rows // 32, ending, 0)
+    groups.wait()
+    gains_out[...] = block[...] + blocks[0] + blocks[1] + blocks[2]
+    rs.finish()
+    cols_all.finish()
+    work.finish()
+
+
+def backward(grad_branch, grad_hidden, kept, first, cosine, signed, q_gain, k_gain, weights, gains, h_all, gd_all, ffn_weights):
+    queries, keys, values, mixed, q_unit, k_unit, q_inverse, k_inverse = kept
+    rows, wide = grad_branch.shape
+    count, head_cols = queries.shape
+    heads = head_cols // HD
+    world = 8
+    width = ffn_weights[0].shape[1]
+    lines = gains.shape[0]
+    vmem = pl.BlockSpec(memory_space=pltpu.VMEM)
+    anywhere = pl.BlockSpec(memory_space=pl.ANY)
+    bf, f32 = jnp.bfloat16, jnp.float32
+    dma = pltpu.SemaphoreType.DMA
+    tok, unit = Background.tokens, Background.units
+    return pl.pallas_call(
+        back_kernel,
+        out_shape=(
+            jax.ShapeDtypeStruct((rows, wide), f32),
+            jax.ShapeDtypeStruct((lines + 8, HD), f32),
+            jax.ShapeDtypeStruct((2, head_cols // 2, wide), bf),
+            jax.ShapeDtypeStruct((4, 3, count, head_cols), bf),
+            jax.ShapeDtypeStruct((wide, width), f32),
+            jax.ShapeDtypeStruct((wide, width), f32),
+            jax.ShapeDtypeStruct((width, wide), f32),
+        ),
+        in_specs=[vmem] * 20 + [anywhere] * 5,
+        out_specs=(vmem, vmem, vmem) + (anywhere,) * 4,
+        scratch_shapes=[
+            pltpu.VMEM((world, rows, wide), bf),
+            pltpu.VMEM((4, rows, wide), bf),
+            pltpu.VMEM((4, rows, wide), bf),
+            pltpu.VMEM((count, head_cols), bf),
+            pltpu.VMEM((count, head_cols), f32),
+            pltpu.VMEM((count, head_cols), f32),
+            pltpu.VMEM((count, head_cols), f32),
+            pltpu.VMEM((3, count, head_cols), bf),
+            pltpu.VMEM((2, head_cols // 2, wide), bf),
+            pltpu.VMEM((2, head_cols // 2, wide), bf),
+            pltpu.VMEM((16, HD), f32),
+            pltpu.VMEM((world, 16, HD), f32),
+            pltpu.VMEM((world, lines, HD), f32),
+            pltpu.VMEM((lines + 8, HD), f32),
+            pltpu.VMEM((3, lines + 8, HD), f32),
+            pltpu.VMEM((8, HD), f32),
+            pltpu.VMEM((2, tok // rows, rows, wide), bf),
+            pltpu.VMEM((2, tok // rows, rows, wide), bf),
+            pltpu.VMEM((wide, unit), bf),
+            pltpu.VMEM((wide, unit), bf),
+            pltpu.VMEM((unit, wide), bf),
+            pltpu.VMEM((wide, unit), f32),
+            pltpu.VMEM((wide, unit), f32),
+            pltpu.VMEM((unit, wide), f32),
+            pltpu.VMEM((tok, unit), bf),
+            pltpu.VMEM((tok, unit), bf),
+            pltpu.VMEM((tok, unit), bf),
+            dma((8,)), dma((8,)), dma((8,)), dma((8,)), dma((8,)), dma((8,)), dma((8,)), dma((8,)), dma((3,)), dma((3,)),
+            dma((12,)), dma((12,)), dma((4,)), dma((4,)), pltpu.SemaphoreType.DMA, dma((2, 2)), dma((3,)), dma((3,)),
+        ],
+        compiler_params=pltpu.CompilerParams(
+            collective_id=3, has_side_effects=True, vmem_limit_bytes=62 * 2**20
+        ),
+        name="back",
+    )(
+        grad_branch, grad_hidden, queries, keys, values, mixed, q_unit, k_unit, q_inverse, k_inverse, first, cosine, signed,
+        q_gain.reshape(1, -1), k_gain.reshape(1, -1), *weights, gains, h_all, gd_all, *ffn_weights,
+    )
 
 
 def on_device_fused(
@@ -682,171 +1389,49 @@
     ffn_gain,
     cotangent,
 ):
-    row_count, full_width = tokens.shape
+    wide = tokens.shape[1]
+    token_count = segment_ids.shape[0] * segment_ids.shape[1]
     head_cols = w_query.shape[1]
-    heads_here = head_cols // HD
-    ff_cols = w_gate.shape[1]
-    seqs_here, seq_len = segment_ids.shape
-    token_count = seqs_here * seq_len
-    att_scale = HD ** (-0.5)
-    whole_x = lax.all_gather(tokens, "tensor", axis=0, tiled=True)
-    w_qkv = jnp.concatenate([w_query, w_key, w_value], axis=1)
-    projected = jnp.dot(whole_x, w_qkv, preferred_element_type=jnp.float32)
-    q_raw = projected[:, :head_cols]
-    k_raw = projected[:, head_cols : 2 * head_cols]
-    values = projected[:, 2 * head_cols :].astype(jnp.bfloat16)
-    q_total, k_total = lax.psum(
-        (jnp.sum(q_raw * q_raw, axis=1), jnp.sum(k_raw * k_raw, axis=1)), "tensor"
-    )
-    q_inverse = lax.rsqrt(q_total / full_width + EPS)[:, None]
-    k_inverse = lax.rsqrt(k_total / full_width + EPS)[:, None]
-    q_unit = q_raw * q_inverse
-    k_unit = k_raw * k_inverse
-    cosine, sine = rotary_tables(positions_of(segment_ids).reshape(token_count))
-    queries = rotate((q_unit * q_gain).reshape(token_count, heads_here, HD), cosine, sine).astype(
-        jnp.bfloat16
-    )
-    keys = rotate((k_unit * k_gain).reshape(token_count, heads_here, HD), cosine, sine).astype(
-        jnp.bfloat16
-    )
-    shaped = (seqs_here, seq_len, heads_here, HD)
-    query_seqs = queries.reshape(shaped)
-    key_seqs = keys.reshape(shaped)
-    value_seqs = values.reshape(shaped)
-    places = jnp.arange(seq_len, dtype=jnp.int32)
-    causal = places[:, None] >= places[None, :]
-
-    def scores_of(query_block, key_block, seg_row):
-        raw = (
-            jnp.einsum("qhd,khd->hqk", query_block, key_block, preferred_element_type=jnp.float32)
-            * att_scale
-        )
-        allowed = causal & (seg_row[:, None] == seg_row[None, :])
-        return jnp.where(allowed[None], raw, -1e30)
-
-    def attend(pieces):
-        query_block, key_block, value_block, seg_row = pieces
-        scores = scores_of(query_block, key_block, seg_row)
-        top = jnp.max(scores, axis=-1, keepdims=True)
-        expo = jnp.exp(scores - top)
-        total = jnp.sum(expo, axis=-1, keepdims=True)
-        probs = (expo / total).astype(jnp.bfloat16)
-        mixed_block = jnp.einsum(
-            "hqk,khd->qhd", probs, value_block, preferred_element_type=jnp.float32
-        )
-        return (mixed_block.astype(jnp.bfloat16), (top + jnp.log(total))[..., 0])
-
-    mixed, log_total = lax.map(attend, (query_seqs, key_seqs, value_seqs, segment_ids))
-    mixed = mixed.reshape(token_count, head_cols)
-    x_rows = tokens.astype(jnp.float32)
-    branch = lax.psum_scatter(
-        jnp.dot(mixed, w_out, preferred_element_type=jnp.float32).astype(jnp.bfloat16),
-        "tensor",
-        scatter_dimension=0,
-        tiled=True,
-    ).astype(jnp.float32)
-    a_inverse = lax.rsqrt(jnp.mean(branch * branch, axis=1, keepdims=True) + EPS)
-    hidden = x_rows + branch * a_inverse * attn_gain
-    a_unit = branch * a_inverse
-    block_out, grad_hidden, grad_ffn_part, h_all, grad_down_all = ffn(
-        hidden.astype(jnp.bfloat16), hidden, cotangent, ffn_gain, w_gate, w_up, w_down
-    )
-    grad_ffn_part = grad_ffn_part[0]
-    h_all = h_all.reshape(-1, full_width)
-    grad_down_all = grad_down_all.reshape(-1, full_width)
-    gate = jnp.dot(h_all, w_gate, preferred_element_type=jnp.float32)
-    up = jnp.dot(h_all, w_up, preferred_element_type=jnp.float32)
-    sigma_gate = jax.nn.sigmoid(gate)
-    silu_gate = gate * sigma_gate
-    act = (silu_gate * up).astype(jnp.bfloat16)
-    grad_act = dot_last(grad_down_all, w_down)
-    grad_w_down = dot_first(act, grad_down_all)
-    grad_gate = grad_act * up * sigma_gate * (1.0 + gate * (1.0 - sigma_gate))
-    grad_up = grad_act * silu_gate
-    grad_w_gate = dot_first(h_all, grad_gate.astype(jnp.bfloat16))
-    grad_w_up = dot_first(h_all, grad_up.astype(jnp.bfloat16))
-    grad_attn_part = jnp.sum(grad_hidden * a_unit, axis=0)
-    grad_branch = norm_back(grad_hidden, a_unit, a_inverse, attn_gain).astype(jnp.bfloat16)
-    grad_branch_all = lax.all_gather(grad_branch, "tensor", axis=0, tiled=True)
-    grad_w_out = dot_first(mixed, grad_branch_all)
-    grad_mixed = dot_last(grad_branch_all, w_out).astype(jnp.bfloat16).reshape(shaped)
-
-    def attend_back(pieces):
-        query_block, key_block, value_block, seg_row, log_block, grad_block = pieces
-        scores = scores_of(query_block, key_block, seg_row)
-        probs = jnp.exp(scores - log_block[..., None])
-        grad_probs = jnp.einsum(
-            "qhd,khd->hqk", grad_block, value_block, preferred_element_type=jnp.float32
-        )
-        grad_scores = (
-            probs * (grad_probs - jnp.sum(probs * grad_probs, axis=-1, keepdims=True))
-        ).astype(jnp.bfloat16)
-        grad_query = (
-            jnp.einsum("hqk,khd->qhd", grad_scores, key_block, preferred_element_type=jnp.float32)
-            * att_scale
-        )
-        grad_key = (
-            jnp.einsum("hqk,qhd->khd", grad_scores, query_block, preferred_element_type=jnp.float32)
-            * att_scale
-        )
-        grad_value = jnp.einsum(
-            "hqk,qhd->khd",
-            probs.astype(jnp.bfloat16),
-            grad_block,
-            preferred_element_type=jnp.float32,
-        )
-        return (grad_query, grad_key, grad_value.astype(jnp.bfloat16))
-
-    grad_query, grad_key, grad_value = lax.map(
-        attend_back, (query_seqs, key_seqs, value_seqs, segment_ids, log_total, grad_mixed)
-    )
-    grad_q_normed = rotate_back(
-        rounded(grad_query.reshape(token_count, heads_here, HD)), cosine, sine
-    ).reshape(token_count, head_cols)
-    grad_k_normed = rotate_back(
-        rounded(grad_key.reshape(token_count, heads_here, HD)), cosine, sine
-    ).reshape(token_count, head_cols)
-    grad_q_gain = jnp.sum(grad_q_normed * q_unit, axis=0)
-    grad_k_gain = jnp.sum(grad_k_normed * k_unit, axis=0)
-    inner_q = grad_q_normed * q_gain
-    inner_k = grad_k_normed * k_gain
-    q_inner_sum, k_inner_sum = lax.psum(
-        (jnp.sum(inner_q * q_unit, axis=1), jnp.sum(inner_k * k_unit, axis=1)), "tensor"
-    )
-    grad_q_raw = q_inverse * (inner_q - q_unit * (q_inner_sum / full_width)[:, None])
-    grad_k_raw = k_inverse * (inner_k - k_unit * (k_inner_sum / full_width)[:, None])
-    grad_qkv = jnp.concatenate(
-        [
-            grad_q_raw.astype(jnp.bfloat16),
-            grad_k_raw.astype(jnp.bfloat16),
-            grad_value.reshape(token_count, head_cols),
-        ],
-        axis=1,
-    )
-    grad_w_qkv = dot_first(whole_x, grad_qkv)
-    grad_tokens = grad_hidden + lax.psum_scatter(
-        dot_last(grad_qkv, w_qkv).astype(jnp.bfloat16), "tensor", scatter_dimension=0, tiled=True
-    ).astype(jnp.float32)
-    grad_w_qkv, grad_w_out = [
-        lax.psum(part.astype(jnp.bfloat16), "dp").astype(jnp.float32)
-        for part in (grad_w_qkv, grad_w_out)
-    ]
-    grad_q_gain, grad_k_gain = lax.psum((grad_q_gain, grad_k_gain), "dp")
-    grad_attn_gain, grad_ffn_gain = lax.psum((grad_attn_part, grad_ffn_part), ("dp", "tensor"))
+    positions = positions_of(segment_ids).reshape(token_count)
+    cosine, sine = rotary_tables(positions)
+    first = (jnp.arange(token_count, dtype=jnp.int32) - positions)[:, None]
+    signed = jnp.where(jnp.arange(HD) < HD // 2, -sine, sine)
+    branch, queries, keys, values, q_unit, k_unit, q_inverse, k_inverse, mixed, x_all = attention(
+        tokens, w_query, w_key, w_value, w_out, q_gain, k_gain, cosine, signed, first
+    )
+    block_out, grad_hidden, grad_branch, gains, act, grad_gate, grad_up, h_all, gd_all = ffn(
+        tokens, branch, cotangent, attn_gain, ffn_gain, w_gate, w_up, w_down
+    )
+    grad_tokens, gains, grad_w_out, grad_qkv, part_gate, part_up, part_down = backward(
+        grad_branch, grad_hidden, (queries, keys, values, mixed, q_unit, k_unit, q_inverse, k_inverse),
+        first, cosine, signed, q_gain, k_gain, (w_query, w_key, w_value, w_out), gains, h_all, gd_all, (w_gate, w_up, w_down),
+    )
+    h_own = h_all[0].reshape(token_count, wide)
+    gd_own = gd_all[0].reshape(token_count, wide)
+    grad_w_gate = part_gate + dot_first(h_own, grad_gate)
+    grad_w_up = part_up + dot_first(h_own, grad_up)
+    grad_w_down = part_down + dot_first(act, gd_own)
+    x_all = x_all.reshape(4 * token_count, wide)
+
+    def over_all(part):
+        return dot_first(x_all, grad_qkv[:, part].reshape(4 * token_count, head_cols))
+
+    lines = wide // HD
+    gain_rows = head_cols // HD
     return (
         block_out,
         grad_tokens,
-        grad_w_qkv[:, :head_cols],
-        grad_w_qkv[:, head_cols : 2 * head_cols],
-        grad_w_qkv[:, 2 * head_cols :],
-        grad_w_out,
+        over_all(0),
+        over_all(1),
+        over_all(2),
+        grad_w_out.reshape(head_cols, wide).astype(jnp.float32),
         grad_w_gate,
         grad_w_up,
         grad_w_down,
-        grad_q_gain,
-        grad_k_gain,
-        grad_attn_gain,
-        grad_ffn_gain,
+        gains[2 * lines : 2 * lines + gain_rows].reshape(head_cols),
+        gains[2 * lines + gain_rows : 2 * lines + 2 * gain_rows].reshape(head_cols),
+        gains[lines : 2 * lines].reshape(wide),
+        gains[:lines].reshape(wide),
     )
 
 

time: 657 us -> 533 us (0.81)
  Pallas kernels: 202 us -> 458 us
  matrix products: 208 us -> 49.4 us
  waiting for transfers between devices: 89.5 us -> 0 us
  blocking collectives: 80 us -> 0 us
  other arithmetic: 27.8 us -> 7 us
  local copies, waits for them, and re-layouts: 25.4 us -> 9.3 us
  between operations: 14.8 us -> 1.08 us
    pallas_call x0 -> x2, Pallas kernels: none -> 251 us  [the longest x1 154 us: backward(): pl.pallas_call(back_kernel, out_shape=(jax.ShapeDtypeStruct((rows, wide),...]
    dot_general x13 -> x0, matrix products: 105 us -> none  [the longest x3 33 us: dot_last(): lax.dot_general(left, right, (((1,), (1,)), ((), ())), preferred_element_...]
    psum x4 -> x0, blocking collectives: 80 us -> none  [the longest x1 38.5 us: on_device_fused(): lax.psum((grad_attn_part, grad_ffn_part), ('dp', 'tensor'))]
    dot_general x5 -> x6, matrix products: 103 us -> 49.4 us  [dot_first(): lax.dot_general(left, right, (((0,), (0,)), ((), ())), preferred_element_...]
    reduce_scatter x2 -> x0, waiting for transfers between devices: 48 us -> none  [the longest x1 48 us: on_device_fused(): lax.psum_scatter(jnp.dot(mixed, w_out, preferred_element_type=jnp.float32...]
    all_gather x2 -> x0, waiting for transfers between devices: 40.7 us -> none  [the longest x1 40.7 us: on_device_fused(): whole_x = lax.all_gather(tokens, 'tensor', axis=0, tiled=True)]
    unnamed x68 -> x36, local copies, waits for them, and re-layouts: 17.3 us -> 2.16 us
    convert_element_type x6 -> x1, other arithmetic: 13.4 us -> 1.63 us  [on_device_fused(): grad_w_out.reshape(head_cols, wide).astype(jnp.float32)]
  transfers between devices with their start and end apart: 5 -> 0, of which waited for: 2 -> 0; matrix products, arithmetic and copies ran while one was open for 30% -> 0% of each run, Pallas kernels for 0% -> 0%
where the time goes in v3:
time: 533 us; the launch traced here: 524 us
  Pallas kernels  458 us (86%)
  matrix products  49.4 us (9%)
  local copies, waits for them, and re-layouts  9.3 us (2%)
  other arithmetic  7 us (1%)
    pallas_call x1, Pallas kernels, ffn(): pl.pallas_call(ffn_kernel, out_shape=(jax.ShapeDtypeStruct((rows, wide),...  207 us
    pallas_call x1, Pallas kernels, backward(): pl.pallas_call(back_kernel, out_shape=(jax.ShapeDtypeStruct((rows, wide),...  154 us
    pallas_call x1, Pallas kernels, attention(): pl.pallas_call(attn_kernel, out_shape=(jax.ShapeDtypeStruct((rows, wide),...  96.8 us
    dot_general x6, matrix products, dot_first(): lax.dot_general(left, right, (((0,), (0,)), ((), ())), preferred_element_...  49.4 us

profile of v3, /device:TPU:0, one launch (start us, length us, event | category | flops | bytes accessed | tf_op | source)
XLA Modules:
  0.0 524.3 jit_solution(14257730727809009609)
XLA Ops:
  0.6 1.3 convert_reduce_fusion
  2.0 1.9 multiply_sine_fusion
  3.9 1.3 negate_select_fusion
  5.2 0.2 copy.28
  5.4 0.9 subtract_subtract_fusion.first_ref
  6.3 96.8 %attn.1 = (f32[128,2048]{1,0:T(8,128)}, bf16[1024,256]{1,0:T(8,128)(2,1)}, bf16[1024,256]{1,0:T(8,128)(2,1)}, bf16[1024,256]{1,0:T(8,128)(2,1)}, f32[1024,256]{1...) custom-call(bf16[128,2048]{1,0:T(8,128)(2,1)} %x_ref.3, ...), custom_call_target="tpu_custom_call" | custom-call | tf_op jit(solution)/shard_map/attn/pallas_call | solution.py:892
  103.1 207.0 %ffn.1 = (bf16[128,2048]{1,0:T(8,128)(2,1)}, f32[128,2048]{1,0:T(8,128)}, bf16[128,2048]{1,0:T(8,128)(2,1)}, f32[32,128]{1,0:T(8,128)}, bf16[1024,1024]{1,0:T(8,...) custom-call(bf16[128,2048]{1,0:T(8,128)(2,1)} %x_ref.3, ...), custom_call_target="tpu_custom_call" | custom-call | tf_op jit(solution)/shard_map/ffn/pallas_call | solution.py:650
  310.1 153.7 %back.1 = (f32[128,2048]{1,0:T(8,128)}, f32[40,128]{1,0:T(8,128)}, bf16[2,128,2048]{2,1,0:T(8,128)(2,1)}, bf16[4,3,1024,256]{3,2,1,0:T(8,128)(2,1)}, f32[2048,10...) custom-call(bf16[128,2048]{1,0:T(8,128)(2,1)} %get-tuple-element.41.gb_ref, ...), custom_call_target="tpu_custom_call" | custom-call | tf_op jit(solution)/shard_map/back/pallas_call | solution.py:1322
  463.9 0.0 copy-start.6
  463.9 0.0 slice-start.8
  463.9 2.7 slice.31
  466.5 0.2 copy-done.6
  466.7 0.0 slice-start.9
  466.7 9.3 %convolution_add_fusion = f32[1024,2048]{1,0:T(8,128)} fusion(f32[1024,2048]{1,0:T(8,128)} %get-tuple-element.62, bf16[1024,1024]{1,0:T(8,128)(2,1)S(1)} %copy-done.6, bf16[1024,2048]{1,0:T(8,128)(2,1)S(1)} %bitcast.39), kind=kOutput, calls=%fused_computation.1 | convolution fusion | flops 4297064448 | bytes 23068672 | tf_op jit(solution)/shard_map/dot_general | solution.py:26
  476.1 0.0 copy-start.5
  476.1 2.7 slice.30
  478.7 0.0 slice-done.8
  478.7 0.0 slice-done.9
  478.8 0.2 copy-done.5
  478.9 6.9 %convolution_add_fusion.1 = f32[2048,1024]{1,0:T(8,128)} fusion(f32[2048,1024]{1,0:T(8,128)S(1)} %bitcast.59, bf16[1024,2048]{1,0:T(8,128)(2,1)S(1)} %bitcast.37, bf16[1024,1024]{1,0:T(8,128)(2,1)S(1)} %copy-done.5), kind=kOutput, calls=%fused_computation.2 | convolution fusion | flops 4297064448 | bytes 23068672 | tf_op jit(solution)/shard_map/dot_general | solution.py:26
  485.8 0.0 slice-done.6
  485.8 0.0 slice-done.7
  485.8 0.0 copy-done.4
  485.9 6.9 %convolution_add_fusion.2 = f32[2048,1024]{1,0:T(8,128)} fusion(f32[2048,1024]{1,0:T(8,128)S(1)} %bitcast.57, bf16[1024,2048]{1,0:T(8,128)(2,1)S(1)} %bitcast.38, bf16[1024,1024]{1,0:T(8,128)(2,1)S(1)} %copy-done.4), kind=kOutput, calls=%fused_computation.3 | convolution fusion | flops 4297064448 | bytes 23068672 | tf_op jit(solution)/shard_map/dot_general | solution.py:26
  492.8 0.0 slice-done
  492.8 0.0 slice-done.1
  492.8 0.4 fusion
  493.2 0.0 slice-start.2
  493.3 0.0 slice-start.3
  493.3 9.9 %fusion.3 = f32[2048,256]{1,0:T(8,128)} fusion(bf16[4096,2048]{1,0:T(8,128)(2,1)} %bitcast.51, bf16[4096,256]{1,0:T(8,128)(2,1)S(1)} %bitcast.42), kind=kOutput, calls=%fused_computation.20 | convolution fusion | flops 4294967296 | bytes 20971520 | tf_op jit(solution)/shard_map/dot_general | solution.py:26
  503.1 10.0 %fusion.2 = f32[2048,256]{1,0:T(8,128)} fusion(bf16[4096,2048]{1,0:T(8,128)(2,1)} %bitcast.52, bf16[4096,256]{1,0:T(8,128)(2,1)S(1)} %bitcast.41), kind=kOutput, calls=%fused_computation.19 | convolution fusion | flops 4294967296 | bytes 20971520 | tf_op jit(solution)/shard_map/dot_general | solution.py:26
  513.2 0.0 slice-done.2
  513.2 0.0 slice-done.3
  513.2 0.0 slice-done.4
  513.2 0.0 slice-done.5
  513.2 0.0 copy-start
  513.2 0.0 copy-start.3
  513.2 0.0 copy-start.2
  513.2 6.3 %fusion.1 = f32[2048,256]{1,0:T(8,128)} fusion(bf16[4096,2048]{1,0:T(8,128)(2,1)S(1)} %bitcast.55, bf16[4096,256]{1,0:T(8,128)(2,1)S(1)} %bitcast.40), kind=kOutput, calls=%fused_computation.18 | convolution fusion | flops 4294967296 | bytes 20971520 | tf_op jit(solution)/shard_map/dot_general | solution.py:26
  519.5 0.0 copy-done
  519.5 1.6 bitcast_convert_fusion
  521.2 0.0 copy-done.3
  521.2 0.6 slice_bitcast_fusion
  521.8 0.6 slice_bitcast_fusion.2
  522.3 0.0 copy-done.2
  522.3 0.8 copy.31
  523.1 0.0 copy-done.1
  523.1 1.0 copy.32
  (15 shorter events, 0.0 us)
Async XLA Ops:
  463.9 2.9 copy-start.6
  463.9 14.9 %slice-start.8 = ((s8[8388608]{0:T(1024)(128)(4,1)}), s8[4194304]{0:T(1024)(128)(4,1)S(1)}, s32[]{:S(2)}) async-start(s8[8388608]{0:T(1024)(128)(4,1)} %bitcast.58), calls=%async_computation.8 | async-start | bytes 8388608
  466.7 12.0 %slice-start.9 = ((s8[8388608]{0:T(1024)(128)(4,1)}), s8[4194304]{0:T(1024)(128)(4,1)S(1)}, s32[]{:S(2)}) async-start(s8[8388608]{0:T(1024)(128)(4,1)} %bitcast.58), calls=%async_computation.9 | async-start | bytes 8388608
  476.1 2.9 copy-start.5
  476.1 9.8 %slice-start.6 = ((s8[8388608]{0:T(1024)(128)(4,1)}), s8[4194304]{0:T(1024)(128)(4,1)S(1)}, s32[]{:S(2)}) async-start(s8[8388608]{0:T(1024)(128)(4,1)} %bitcast.56), calls=%async_computation.6 | async-start | bytes 8388608
  478.9 6.9 %slice-start.7 = ((s8[8388608]{0:T(1024)(128)(4,1)}), s8[4194304]{0:T(1024)(128)(4,1)S(1)}, s32[]{:S(2)}) async-start(s8[8388608]{0:T(1024)(128)(4,1)} %bitcast.56), calls=%async_computation.7 | async-start | bytes 8388608
  478.9 6.9 %copy-start.4 = (bf16[1024,1024]{1,0:T(8,128)(2,1)S(1)}, bf16[1024,1024]{1,0:T(8,128)(2,1)}, u32[]{:S(2)}) copy-start(bf16[1024,1024]{1,0:T(8,128)(2,1)} %get-tuple-element.59) | copy-start | bytes 6291460
  478.9 13.9 %slice-start = ((s8[6291456]{0:T(1024)(128)(4,1)}), s8[4194304]{0:T(1024)(128)(4,1)S(1)}, s32[]{:S(2)}) async-start(s8[6291456]{0:T(1024)(128)(4,1)} %bitcast.35), calls=%async_computation | async-start | bytes 8388608
  485.8 7.0 %slice-start.1 = ((s8[6291456]{0:T(1024)(128)(4,1)}), s8[2097152]{0:T(1024)(128)(4,1)S(1)}, s32[]{:S(2)}) async-start(s8[6291456]{0:T(1024)(128)(4,1)} %bitcast.35), calls=%async_computation.1 | async-start | bytes 4194304
  493.2 19.9 %slice-start.2 = ((s8[16777216]{0:T(1024)(128)(4,1)}), s8[4194304]{0:T(1024)(128)(4,1)S(1)}, s32[]{:S(2)}) async-start(s8[16777216]{0:T(1024)(128)(4,1)} %bitcast.53), calls=%async_computation.2 | async-start | bytes 8388608
  493.3 19.9 %slice-start.3 = ((s8[16777216]{0:T(1024)(128)(4,1)}), s8[4194304]{0:T(1024)(128)(4,1)S(1)}, s32[]{:S(2)}) async-start(s8[16777216]{0:T(1024)(128)(4,1)} %bitcast.53), calls=%async_computation.3 | async-start | bytes 8388608
  503.1 10.0 %slice-start.4 = ((s8[16777216]{0:T(1024)(128)(4,1)}), s8[4194304]{0:T(1024)(128)(4,1)S(1)}, s32[]{:S(2)}) async-start(s8[16777216]{0:T(1024)(128)(4,1)} %bitcast.53), calls=%async_computation.4 | async-start | bytes 8388608
  503.1 10.0 %slice-start.5 = ((s8[16777216]{0:T(1024)(128)(4,1)}), s8[4194304]{0:T(1024)(128)(4,1)S(1)}, s32[]{:S(2)}) async-start(s8[16777216]{0:T(1024)(128)(4,1)} %bitcast.53), calls=%async_computation.5 | async-start | bytes 8388608
  513.2 6.3 %copy-start = (bf16[2,128,2048]{2,1,0:T(8,128)(2,1)S(1)}, bf16[2,128,2048]{2,1,0:T(8,128)(2,1)}, u32[]{:S(2)}) copy-start(bf16[2,128,2048]{2,1,0:T(8,128)(2,1)} %get-tuple-element.57) | copy-start | bytes 3145732
  513.2 8.0 %copy-start.3 = (f32[40,128]{1,0:T(8,128)S(1)}, f32[40,128]{1,0:T(8,128)}, u32[]{:S(2)}) copy-start(f32[40,128]{1,0:T(8,128)} %get-tuple-element.64) | copy-start | bytes 61444
  513.2 9.1 %copy-start.2 = (bf16[128,2048]{1,0:T(8,128)(2,1)S(1)}, bf16[128,2048]{1,0:T(8,128)(2,1)}, u32[]{:S(2)}) copy-start(bf16[128,2048]{1,0:T(8,128)(2,1)} %get-tuple-element.89) | copy-start | bytes 1572868
  519.5 3.6 copy-start.1

commit v4 on v3

--- a/solution.py
+++ b/solution.py
@@ -427,6 +427,12 @@
         self.full, self.whole, self.send, self.recv, self.own_sem = full, whole, send, recv, own_sem
         self.d, self.dx, self.dy, self.zs, self.c, _ = place
         self.t = 2 * self.zs[0] + self.c
+        self.seen = set()
+
+    def ready(self, k, r):
+        other = self.whole.at[1 + k, 2 * self.zs[r] + 1 - self.c]
+        remote(other, other, self.send.at[0], self.recv.at[12 + k * 4 + r], self.d, self.t).wait_recv()
+        self.seen.add((k, r))
 
     def slot(self, g, r):
         return self.whole.at[g, 2 * self.zs[r] + self.c]
@@ -466,8 +472,14 @@
             self.own(r, 1).wait_send()
             self.hop(r).wait_send()
             for k in range(3):
-                self.to_core(r, k).wait()
+                self.to_core(r, k).wait_send()
+                if (k, r) not in self.seen:
+                    self.to_core(r, k).wait_recv()
         self.keep().wait()
+
+
+def dot_tn(left, right):
+    return lax.dot_general(left, right, (((0,), (0,)), ((), ())), preferred_element_type=jnp.float32)
 
 
 def dot_nt(left, right):
@@ -476,9 +488,9 @@
 
 def ffn_kernel(
     x_ref, br_ref, cot_ref, again_ref, gain_ref, wg_ref, wu_ref, wd_ref,
-    bo_ref, gh_ref, gb_ref, gains_ref, act, gg, gu, hall_ref, gdall_ref,
-    hfull, gfull, hid_ref, sums, gate, up, parts, pair, land,
-    ag_send, ag_recv, rs_send, rs_recv, xy_send, xy_recv, own_sem,
+    bo_ref, gh_ref, gb_ref, gains_ref, hall_ref, gdall_ref, og_ref, ou_ref, od_ref, gate_all, up_all,
+    hfull, gfull, hid_ref, sums, gate, up, act, gg, gu, parts, pair, land, hbuf, gbuf, ubuf,
+    ag_send, ag_recv, rs_send, rs_recv, xy_send, xy_recv, own_sem, load_sem, store_sem, out_sem,
 ):
     place = places_of()
     d, dx, dy, zs, c, inner = place
@@ -549,15 +561,95 @@
 
         lax.fori_loop(0, wide // dt, out, 0)
 
+    def own_copies(i, down):
+        slot = pl.ds(pl.multiple_of(lax.rem(i, 4) * 256, 256), 256)
+        at = pl.ds(pl.multiple_of(i * 256, 256), 256)
+        outs = (od_ref.at[at, pl.ds(0, width)], od_ref.at[at, pl.ds(width, width)]) if down else (og_ref.at[at, :], ou_ref.at[at, :])
+        return [
+            pltpu.make_async_copy(buf.at[slot, :], out, out_sem.at[n, lax.rem(i, 4)])
+            for n, (buf, out) in enumerate(zip((gate, up), outs))
+        ]
+
+    def own_in(i, carry):
+        slot = pl.ds(pl.multiple_of(lax.rem(i, 4) * 256, 256), 256)
+        at = pl.ds(pl.multiple_of(i * 256, 256), 256)
+
+        @pl.when(i >= 4)
+        def _():
+            for copy in own_copies(i - 4, False):
+                copy.wait()
+
+        h = hfull[:, :, at].reshape(8 * rows, 256)
+        gate[slot, :] = dot_tn(h, gg[...])
+        up[slot, :] = dot_tn(h, gu[...])
+        for copy in own_copies(i, False):
+            copy.start()
+        return carry
+
+    def own_down(i, carry):
+        at = pl.ds(pl.multiple_of(i * 256, 256), 256)
+        for copy in own_copies(i + 4, False):
+            copy.wait()
+        left = act[:, at]
+        for n, buf in enumerate((gate, up)):
+            buf[at, :] = dot_tn(left, gfull[:, :, n * width : (n + 1) * width].reshape(8 * rows, width))
+        for copy in own_copies(i, True):
+            copy.start()
+        return carry
+
+    done = []
+
+    def fill(chunks):
+        def load(n):
+            k, r = chunks[n]
+            slot = (base + n) % 2
+            return pltpu.make_async_copy(hall_ref.at[1 + k, pl.ds(2 * zs[r], 2)], hbuf.at[slot], load_sem.at[slot])
+
+        base = len(done)
+        for n, (k, r) in enumerate(chunks):
+            slot = len(done) % 2
+            if n == 0:
+                xy_h.ready(k, r)
+                load(0).start()
+            load(n).wait()
+            if n + 1 < len(chunks):
+                xy_h.ready(*chunks[n + 1])
+                load(n + 1).start()
+            if len(done) >= 2:
+                for copy in stores(len(done) - 2):
+                    copy.wait()
+
+            def tile(j, carry):
+                cols = pl.ds(pl.multiple_of(j * ft, ft), ft)
+                block = hbuf[slot].reshape(2 * rows, wide)
+                gbuf[slot, :, cols] = jnp.dot(block, wg_ref[:, cols], preferred_element_type=jnp.float32).astype(jnp.bfloat16)
+                ubuf[slot, :, cols] = jnp.dot(block, wu_ref[:, cols], preferred_element_type=jnp.float32).astype(jnp.bfloat16)
+                return carry
+
+            lax.fori_loop(0, width // ft, tile, 0)
+            done.append((k, r))
+            for copy in stores(len(done) - 1):
+                copy.start()
+
+    def stores(n):
+        k, r = done[n]
+        at = pl.ds(pl.multiple_of(zs[r] * 2 * rows, 2 * rows), 2 * rows)
+        return [
+            pltpu.make_async_copy(buf.at[n % 2], out.at[k, at, :], store_sem.at[m, n % 2])
+            for m, (buf, out) in enumerate(((gbuf, gate_all), (ubuf, up_all)))
+        ]
+
     def phase(p, full, whole, unit):
         ag = Gather(full, ag_send.at[p], ag_recv.at[p], place)
         rs = Scatter(parts, pair.at[p], land.at[p], rs_send.at[p], rs_recv.at[p], place)
-        xy = Spread(full, whole, xy_send.at[p], xy_recv.at[p], own_sem.at[p], place)
+        xy = xy_h if p == 0 else xy_g
         ag.start()
         xy.start(0)
         ag.ready(0)
         unit(zs[0])
         rs.to_core(0).start()
+        if p == 1:
+            fill([(0, 3), (1, 3), (2, 0), (2, 2)])
         ag.start_inner()
         ag.arrive(2)
         xy.start(2)
@@ -585,11 +677,22 @@
         xy.pass_on(0)
         xy.pass_on(2)
         xy.pass_on(1)
+        if p == 0:
+            fill([(0, 0), (1, 0), (0, 2)])
+        else:
+            lax.fori_loop(0, 8, own_in, 0)
         rs.relay()
+        if p == 0:
+            fill([(1, 2), (0, 1), (1, 1)])
+        else:
+            lax.fori_loop(0, 4, own_down, 0)
+            fill([(2, 1), (2, 3)])
         rs.arrived()
-        return ag, rs, xy
-
-    ag, rs, xy_h = phase(0, hfull, hall_ref, unit_forward)
+        return ag, rs
+
+    xy_h = Spread(hfull, hall_ref, xy_send.at[0], xy_recv.at[0], own_sem.at[0], place)
+    xy_g = Spread(gfull, gdall_ref, xy_send.at[1], xy_recv.at[1], own_sem.at[1], place)
+    ag, rs = phase(0, hfull, hall_ref, unit_forward)
     sums[...] = jnp.zeros_like(sums)
 
     def middle(i, carry):
@@ -610,7 +713,7 @@
     xy_h.pass_on(3)
     for r in range(4):
         xy_h.last(r)
-    ag, rs, xy = phase(1, gfull, gdall_ref, unit_backward)
+    ag, rs = phase(1, gfull, gdall_ref, unit_backward)
 
     def ending(i, carry):
         at = pl.ds(pl.multiple_of(i * step_rows, step_rows), step_rows)
@@ -630,11 +733,17 @@
         gains_ref[wide // HD + i : wide // HD + i + 1, :] = sums[1:2, i * HD : (i + 1) * HD]
     ag.finish()
     rs.finish()
-    xy.pass_on(3)
+    xy_g.pass_on(3)
     for r in range(4):
-        xy.last(r)
+        xy_g.last(r)
     xy_h.finish()
-    xy.finish()
+    for i in range(4):
+        for copy in own_copies(i, True):
+            copy.wait()
+    for n in (len(done) - 2, len(done) - 1):
+        for copy in stores(n):
+            copy.wait()
+    xy_g.finish()
 
 
 def ffn(x_own, branch, cot, attn_gain, ffn_gain, w_gate, w_up, w_down):
@@ -645,7 +754,7 @@
     anywhere = pl.BlockSpec(memory_space=pl.ANY)
     bf, f32 = jnp.bfloat16, jnp.float32
     whole = jax.ShapeDtypeStruct((groups, world, rows, wide), bf)
-    units = jax.ShapeDtypeStruct((world * rows, width), bf)
+    others = jax.ShapeDtypeStruct((groups - 1, world * rows, width), bf)
     dma = pltpu.SemaphoreType.DMA
     return pl.pallas_call(
         ffn_kernel,
@@ -654,12 +763,16 @@
             jax.ShapeDtypeStruct((rows, wide), f32),
             jax.ShapeDtypeStruct((rows, wide), bf),
             jax.ShapeDtypeStruct((2 * wide // HD, HD), f32),
-            units, units, units,
             whole,
             whole,
+            jax.ShapeDtypeStruct((wide, width), f32),
+            jax.ShapeDtypeStruct((wide, width), f32),
+            jax.ShapeDtypeStruct((width, wide), f32),
+            others,
+            others,
         ),
         in_specs=[vmem] * 8,
-        out_specs=(vmem,) * 7 + (anywhere, anywhere),
+        out_specs=(vmem,) * 4 + (anywhere,) * 7,
         scratch_shapes=[
             pltpu.VMEM((world, rows, wide), bf),
             pltpu.VMEM((world, rows, wide), bf),
@@ -667,9 +780,15 @@
             pltpu.VMEM((8, wide), f32),
             pltpu.VMEM((world * rows, width), f32),
             pltpu.VMEM((world * rows, width), f32),
+            pltpu.VMEM((world * rows, width), bf),
+            pltpu.VMEM((world * rows, width), bf),
+            pltpu.VMEM((world * rows, width), bf),
             pltpu.VMEM((world, rows, wide), bf),
             pltpu.VMEM((2, 4, rows, wide), bf),
             pltpu.VMEM((2, 4, rows, wide), bf),
+            pltpu.VMEM((2, 2, rows, wide), bf),
+            pltpu.VMEM((2, 2 * rows, width), bf),
+            pltpu.VMEM((2, 2 * rows, width), bf),
             dma((2, 8)),
             dma((2, 8)),
             dma((2, 8)),
@@ -677,6 +796,9 @@
             dma((2, 24)),
             dma((2, 24)),
             dma((2,)),
+            dma((2,)),
+            dma((2, 2)),
+            dma((2, 4)),
         ],
         compiler_params=pltpu.CompilerParams(
             collective_id=2, has_side_effects=True, vmem_limit_bytes=60 * 2**20
@@ -915,52 +1037,58 @@
     )(x_own, w_query, w_key, w_value, w_out, q_gain.reshape(1, -1), k_gain.reshape(1, -1), cosine, sine, first)
 
 
-def dot_tn(left, right):
-    return lax.dot_general(left, right, (((0,), (0,)), ((), ())), preferred_element_type=jnp.float32)
-
-
 class Background:
     tokens, units = 512, 512
 
-    def __init__(self, hall, gdall, weights, outs, hbuf, gbuf, tiles, sums, mids, load_sem, tile_sem, out_sem):
-        self.hall, self.gdall, self.weights, self.outs = hall, gdall, weights, outs
-        self.hbuf, self.gbuf, self.tiles, self.sums, self.mids = hbuf, gbuf, tiles, sums, mids
-        self.load_sem, self.tile_sem, self.out_sem = load_sem, tile_sem, out_sem
+    def __init__(self, hall, gdall, gate_all, up_all, w_down, starts, outs, hbuf, gbuf, gate, up, tile, sums, mids, load_sem, tile_sem, start_sem, out_sem):
+        self.hall, self.gdall, self.gate_all, self.up_all, self.w_down, self.starts, self.outs = hall, gdall, gate_all, up_all, w_down, starts, outs
+        self.hbuf, self.gbuf, self.gate, self.up, self.tile, self.sums, self.mids = hbuf, gbuf, gate, up, tile, sums, mids
+        self.load_sem, self.tile_sem, self.start_sem, self.out_sem = load_sem, tile_sem, start_sem, out_sem
         self.blocks = self.tokens // hall.shape[2]
         self.per_group = hall.shape[1] // self.blocks
         self.per_tile = 3 * self.per_group
-        self.tile_count = weights[0].shape[1] // self.units
+        self.tile_count = w_down.shape[0] // self.units
         self.count = self.tile_count * self.per_tile
 
     def loads(self, n):
         slot, m = n % 2, n % self.per_tile
         group, part = 1 + m // self.per_group, m % self.per_group
         blocks = pl.ds(part * self.blocks, self.blocks)
+        rows = pl.ds(part * self.tokens, self.tokens)
+        units = pl.ds(n // self.per_tile * self.units, self.units)
         return (
             pltpu.make_async_copy(self.hall.at[group, blocks], self.hbuf.at[slot], self.load_sem.at[0, slot]),
             pltpu.make_async_copy(self.gdall.at[group, blocks], self.gbuf.at[slot], self.load_sem.at[1, slot]),
+            pltpu.make_async_copy(self.gate_all.at[group - 1, rows, units], self.gate.at[slot], self.load_sem.at[2, slot]),
+            pltpu.make_async_copy(self.up_all.at[group - 1, rows, units], self.up.at[slot], self.load_sem.at[3, slot]),
         )
 
-    def tile_loads(self, tile):
+    def tile_load(self, tile):
+        return pltpu.make_async_copy(self.w_down.at[pl.ds(tile * self.units, self.units), :], self.tile, self.tile_sem)
+
+    def moves(self, tile, refs, sem, inward):
         at = pl.ds(tile * self.units, self.units)
-        wg, wu, wd = self.weights
-        return (
-            pltpu.make_async_copy(wg.at[:, at], self.tiles[0], self.tile_sem.at[0]),
-            pltpu.make_async_copy(wu.at[:, at], self.tiles[1], self.tile_sem.at[1]),
-            pltpu.make_async_copy(wd.at[at, :], self.tiles[2], self.tile_sem.at[2]),
-        )
+        g, u, d = refs
+        pairs = zip(self.sums, (g.at[:, at], u.at[:, at], d.at[at, :]))
+        return [
+            pltpu.make_async_copy(far, near, sem.at[n]) if inward else pltpu.make_async_copy(near, far, sem.at[n])
+            for n, (near, far) in enumerate(pairs)
+        ]
 
     def stores(self, tile):
-        at = pl.ds(tile * self.units, self.units)
-        og, ou, od = self.outs
-        return (
-            pltpu.make_async_copy(self.sums[0], og.at[:, at], self.out_sem.at[0]),
-            pltpu.make_async_copy(self.sums[1], ou.at[:, at], self.out_sem.at[1]),
-            pltpu.make_async_copy(self.sums[2], od.at[at, :], self.out_sem.at[2]),
-        )
+        return self.moves(tile, self.outs, self.out_sem, False)
+
+    def sums_in(self, tile):
+        return self.moves(tile, self.starts, self.start_sem, True)
 
     def begin(self):
-        for copy in self.tile_loads(0) + self.loads(0):
+        for copy in self.loads(0) + (self.tile_load(0),) + tuple(self.sums_in(0)):
+            copy.start()
+
+    def turn(self, tile):
+        for copy in self.stores(tile):
+            copy.wait()
+        for copy in self.sums_in(tile + 1):
             copy.start()
 
     def step(self, n):
@@ -969,15 +1097,13 @@
             for copy in self.loads(n + 1):
                 copy.start()
         if m == 0:
-            for copy in self.tile_loads(tile):
+            self.tile_load(tile).wait()
+            for copy in self.sums_in(tile):
                 copy.wait()
-            if tile:
-                for copy in self.stores(tile - 1):
-                    copy.wait()
         for copy in self.loads(n):
             copy.wait()
-        hbuf, gbuf = self.hbuf.at[slot], self.gbuf.at[slot]
-        wg, wu, wd = self.tiles
+        hbuf, gbuf, gate, up = self.hbuf.at[slot], self.gbuf.at[slot], self.gate.at[slot], self.up.at[slot]
+        wd = self.tile
         act, gg, gu = self.mids
         rows, wide = hbuf.shape[1:]
         half = self.tokens // 2
@@ -985,9 +1111,7 @@
         def mid(i, carry):
             blocks = pl.ds(i * (self.blocks // 2), self.blocks // 2)
             at = pl.ds(pl.multiple_of(i * half, half), half)
-            h = hbuf[blocks].reshape(half, wide)
-            g = jnp.dot(h, wg[...], preferred_element_type=jnp.float32)
-            u = jnp.dot(h, wu[...], preferred_element_type=jnp.float32)
+            g, u = gate[at, :].astype(jnp.float32), up[at, :].astype(jnp.float32)
             ga = dot_nt(gbuf[blocks].reshape(half, wide), wd[...])
             s = jax.nn.sigmoid(g)
             gs = g * s
@@ -1005,12 +1129,9 @@
             pg = dot_tn(h, gg[...])
             pu = dot_tn(h, gu[...])
             pd = dot_tn(act[...], gbuf[:, :, at].reshape(self.tokens, span))
-            if m == 0:
-                self.sums[0][at, :], self.sums[1][at, :], self.sums[2][:, at] = pg, pu, pd
-            else:
-                self.sums[0][at, :] += pg
-                self.sums[1][at, :] += pu
-                self.sums[2][:, at] += pd
+            self.sums[0][at, :] += pg
+            self.sums[1][at, :] += pu
+            self.sums[2][:, at] += pd
             return carry
 
         lax.fori_loop(0, wide // span, into, 0)
@@ -1018,8 +1139,7 @@
             for copy in self.stores(tile):
                 copy.start()
             if tile + 1 < self.tile_count:
-                for copy in self.tile_loads(tile + 1):
-                    copy.start()
+                self.tile_load(tile + 1).start()
 
     def finish(self):
         for copy in self.stores(self.tile_count - 1):
@@ -1100,12 +1220,12 @@
 
 def back_kernel(
     gb_ref, gh_ref, q_ref, k_ref, v_ref, mixed_ref, qu_ref, ku_ref, rq_ref, rk_ref, first_ref, cos_ref, sin_ref,
-    qg_ref, kg_ref, wq_ref, wk_ref, wv_ref, wo_ref, gains_ref, hall, gdall, wg, wu, wd,
+    qg_ref, kg_ref, wq_ref, wk_ref, wv_ref, wo_ref, gains_ref, hall, gdall, gate_all, up_all, w_down, own_g, own_u, own_d,
     gt_ref, gains_out, dwo_ref, gall_ref, dwg, dwu, dwd,
     full, pair, land, gm, dq, dk, dv, own, wo_once, wo_twice, stat, stats, gland, block, blocks, gacc,
-    hbuf, gbuf, tg, tu, td, sg, su, sd, act, gg, gu,
+    hbuf, gbuf, gbf, ubf, td, sg, su, sd, act, gg, gu,
     ag_send, ag_recv, rs_send, rs_recv, st_send, st_recv, ga_send, ga_recv, gr_send, gr_recv,
-    co_send, co_recv, wo_send, wo_recv, own_sem, load_sem, tile_sem, out_sem,
+    co_send, co_recv, wo_send, wo_recv, own_sem, load_sem, tile_sem, start_sem, out_sem,
 ):
     place = places_of()
     d, dx, dy, zs, c, inner = place
@@ -1129,7 +1249,10 @@
     groups = ExchangeGroups(block, blocks, gr_send, gr_recv, place)
     cols_all = SpreadColumns(own, gall_ref, co_send, co_recv, own_sem, place)
     wo_sum = SumHalves(dwo_ref, wo_once, wo_twice, wo_send, wo_recv, place)
-    work = Background(hall, gdall, (wg, wu, wd), (dwg, dwu, dwd), hbuf, gbuf, (tg, tu, td), (sg, su, sd), (act, gg, gu), load_sem, tile_sem, out_sem)
+    work = Background(
+        hall, gdall, gate_all, up_all, w_down, (own_g, own_u, own_d), (dwg, dwu, dwd), hbuf, gbuf, gbf, ubf, td, (sg, su, sd), (act, gg, gu),
+        load_sem, tile_sem, start_sem, out_sem,
+    )
 
     def at_of(zz):
         return pl.ds(pl.multiple_of(zz * span, span), span)
@@ -1193,11 +1316,13 @@
             dv[keys_at, cols] += dot_tn(probs.astype(jnp.bfloat16), grad)
         return carry
 
-    lax.fori_loop(0, 4, attend_back, 0)
+    lax.fori_loop(0, 2, attend_back, 0)
+    wo_sum.add(0)
+    wo_sum.start(1)
+    work.turn(0)
+    lax.fori_loop(2, 4, attend_back, 0)
     own[2] = dv[...].astype(jnp.bfloat16)
     cols_all.start(2)
-    wo_sum.add(0)
-    wo_sum.start(1)
     gacc[...] = jnp.zeros_like(gacc)
 
     def unrope(i, carry):
@@ -1306,13 +1431,13 @@
     work.finish()
 
 
-def backward(grad_branch, grad_hidden, kept, first, cosine, signed, q_gain, k_gain, weights, gains, h_all, gd_all, ffn_weights):
+def backward(grad_branch, grad_hidden, kept, first, cosine, signed, q_gain, k_gain, weights, gains, h_all, gd_all, gate_all, up_all, w_down, own_parts):
     queries, keys, values, mixed, q_unit, k_unit, q_inverse, k_inverse = kept
     rows, wide = grad_branch.shape
     count, head_cols = queries.shape
     heads = head_cols // HD
     world = 8
-    width = ffn_weights[0].shape[1]
+    width = w_down.shape[0]
     lines = gains.shape[0]
     vmem = pl.BlockSpec(memory_space=pltpu.VMEM)
     anywhere = pl.BlockSpec(memory_space=pl.ANY)
@@ -1330,7 +1455,7 @@
             jax.ShapeDtypeStruct((wide, width), f32),
             jax.ShapeDtypeStruct((width, wide), f32),
         ),
-        in_specs=[vmem] * 20 + [anywhere] * 5,
+        in_specs=[vmem] * 20 + [anywhere] * 8,
         out_specs=(vmem, vmem, vmem) + (anywhere,) * 4,
         scratch_shapes=[
             pltpu.VMEM((world, rows, wide), bf),
@@ -1351,8 +1476,8 @@
             pltpu.VMEM((8, HD), f32),
             pltpu.VMEM((2, tok // rows, rows, wide), bf),
             pltpu.VMEM((2, tok // rows, rows, wide), bf),
-            pltpu.VMEM((wide, unit), bf),
-            pltpu.VMEM((wide, unit), bf),
+            pltpu.VMEM((2, tok, unit), bf),
+            pltpu.VMEM((2, tok, unit), bf),
             pltpu.VMEM((unit, wide), bf),
             pltpu.VMEM((wide, unit), f32),
             pltpu.VMEM((wide, unit), f32),
@@ -1361,7 +1486,7 @@
             pltpu.VMEM((tok, unit), bf),
             pltpu.VMEM((tok, unit), bf),
             dma((8,)), dma((8,)), dma((8,)), dma((8,)), dma((8,)), dma((8,)), dma((8,)), dma((8,)), dma((3,)), dma((3,)),
-            dma((12,)), dma((12,)), dma((4,)), dma((4,)), pltpu.SemaphoreType.DMA, dma((2, 2)), dma((3,)), dma((3,)),
+            dma((12,)), dma((12,)), dma((4,)), dma((4,)), pltpu.SemaphoreType.DMA, dma((4, 2)), pltpu.SemaphoreType.DMA, dma((3,)), dma((3,)),
         ],
         compiler_params=pltpu.CompilerParams(
             collective_id=3, has_side_effects=True, vmem_limit_bytes=62 * 2**20
@@ -1369,8 +1494,52 @@
         name="back",
     )(
         grad_branch, grad_hidden, queries, keys, values, mixed, q_unit, k_unit, q_inverse, k_inverse, first, cosine, signed,
-        q_gain.reshape(1, -1), k_gain.reshape(1, -1), *weights, gains, h_all, gd_all, *ffn_weights,
-    )
+        q_gain.reshape(1, -1), k_gain.reshape(1, -1), *weights, gains, h_all, gd_all, gate_all, up_all, w_down, *own_parts,
+    )
+
+
+def tail_kernel(pg_ref, pu_ref, pd_ref, x_ref, g_ref, og_ref, ou_ref, od_ref, oq_ref, ok_ref, ov_ref):
+    count, cols = g_ref.shape[2], x_ref.shape[-1]
+    og_ref[...] = pg_ref[...]
+    ou_ref[...] = pu_ref[...]
+    od_ref[...] = pd_ref[...]
+    for p, out in enumerate((oq_ref, ok_ref, ov_ref)):
+        total = jnp.zeros(out.shape, jnp.float32)
+        for g in range(4):
+            total = total + dot_tn(x_ref[g].reshape(count, cols), g_ref[g, p])
+        out[...] = total
+
+
+def weight_tail(parts, x_all, grad_qkv):
+    groups, world, rows, wide = x_all.shape
+    count, width = world * rows, parts[0].shape[1]
+    head_cols = grad_qkv.shape[-1]
+    cols = 256
+    f32 = jnp.float32
+    down = pl.BlockSpec((cols, width), lambda i: (i, 0))
+    across = pl.BlockSpec((width, cols), lambda i: (0, i))
+    heads = pl.BlockSpec((cols, head_cols), lambda i: (i, 0))
+    return pl.pallas_call(
+        tail_kernel,
+        grid=(wide // cols,),
+        in_specs=[
+            down, down, across,
+            pl.BlockSpec((groups, world, rows, cols), lambda i: (0, 0, 0, i)),
+            pl.BlockSpec(grad_qkv.shape, lambda i: (0, 0, 0, 0)),
+        ],
+        out_specs=(down, down, across, heads, heads, heads),
+        out_shape=(
+            jax.ShapeDtypeStruct((wide, width), f32),
+            jax.ShapeDtypeStruct((wide, width), f32),
+            jax.ShapeDtypeStruct((width, wide), f32),
+        )
+        + (jax.ShapeDtypeStruct((wide, head_cols), f32),) * 3,
+        compiler_params=pltpu.CompilerParams(vmem_limit_bytes=60 * 2**20),
+        cost_estimate=pl.CostEstimate(
+            flops=2 * count * wide * 3 * groups * head_cols, bytes_accessed=100 * 2**20, transcendentals=0
+        ),
+        name="tail",
+    )(*parts, x_all, grad_qkv)
 
 
 def on_device_fused(
@@ -1399,31 +1568,25 @@
     branch, queries, keys, values, q_unit, k_unit, q_inverse, k_inverse, mixed, x_all = attention(
         tokens, w_query, w_key, w_value, w_out, q_gain, k_gain, cosine, signed, first
     )
-    block_out, grad_hidden, grad_branch, gains, act, grad_gate, grad_up, h_all, gd_all = ffn(
+    block_out, grad_hidden, grad_branch, gains, h_all, gd_all, own_gate, own_up, own_down, gate_all, up_all = ffn(
         tokens, branch, cotangent, attn_gain, ffn_gain, w_gate, w_up, w_down
     )
     grad_tokens, gains, grad_w_out, grad_qkv, part_gate, part_up, part_down = backward(
         grad_branch, grad_hidden, (queries, keys, values, mixed, q_unit, k_unit, q_inverse, k_inverse),
-        first, cosine, signed, q_gain, k_gain, (w_query, w_key, w_value, w_out), gains, h_all, gd_all, (w_gate, w_up, w_down),
-    )
-    h_own = h_all[0].reshape(token_count, wide)
-    gd_own = gd_all[0].reshape(token_count, wide)
-    grad_w_gate = part_gate + dot_first(h_own, grad_gate)
-    grad_w_up = part_up + dot_first(h_own, grad_up)
-    grad_w_down = part_down + dot_first(act, gd_own)
-    x_all = x_all.reshape(4 * token_count, wide)
-
-    def over_all(part):
-        return dot_first(x_all, grad_qkv[:, part].reshape(4 * token_count, head_cols))
-
+        first, cosine, signed, q_gain, k_gain, (w_query, w_key, w_value, w_out), gains, h_all, gd_all, gate_all, up_all, w_down,
+        (own_gate, own_up, own_down),
+    )
+    grad_w_gate, grad_w_up, grad_w_down, grad_w_query, grad_w_key, grad_w_value = weight_tail(
+        (part_gate, part_up, part_down), x_all, grad_qkv
+    )
     lines = wide // HD
     gain_rows = head_cols // HD
     return (
         block_out,
         grad_tokens,
-        over_all(0),
-        over_all(1),
-        over_all(2),
+        grad_w_query,
+        grad_w_key,
+        grad_w_value,
         grad_w_out.reshape(head_cols, wide).astype(jnp.float32),
         grad_w_gate,
         grad_w_up,

time: 533 us -> 497 us (0.932)
  matrix products: 49.4 us -> 0 us
  Pallas kernels: 458 us -> 474 us
    dot_general x6 -> x0, matrix products: 49.4 us -> none  [dot_first(): lax.dot_general(left, right, (((0,), (0,)), ((), ())), preferred_element_...]
    pallas_call x0 -> x1, Pallas kernels: none -> 32 us  [weight_tail(): pl.pallas_call(tail_kernel, grid=(wide // cols,), in_specs=[down, down, a...]
    pallas_call x1, Pallas kernels: 154 us -> 140 us  [backward(): pl.pallas_call(back_kernel, out_shape=(jax.ShapeDtypeStruct((rows, wide),...]
    slice x3 -> x0, local copies, waits for them, and re-layouts: 5.74 us -> none  [the longest x1 2.65 us: on_device_fused(): gd_own = gd_all[0].reshape(token_count, wide)]
where the time goes in v4:
time: 497 us; the launch traced here: 488 us
  Pallas kernels  474 us (95%)
  other arithmetic  8.15 us (2%)
    pallas_call x1, Pallas kernels, ffn(): pl.pallas_call(ffn_kernel, out_shape=(jax.ShapeDtypeStruct((rows, wide),...  205 us
    pallas_call x1, Pallas kernels, backward(): pl.pallas_call(back_kernel, out_shape=(jax.ShapeDtypeStruct((rows, wide),...  140 us
    pallas_call x1, Pallas kernels, attention(): pl.pallas_call(attn_kernel, out_shape=(jax.ShapeDtypeStruct((rows, wide),...  96.8 us
    pallas_call x1, Pallas kernels, weight_tail(): pl.pallas_call(tail_kernel, grid=(wide // cols,), in_specs=[down, down, a...  32 us

profile of v4, /device:TPU:0, one launch (start us, length us, event | category | flops | bytes accessed | tf_op | source)
XLA Modules:
  0.0 488.3 jit_solution(1693381856249544572)
XLA Ops:
  0.7 1.3 convert_reduce_fusion
  2.0 0.2 copy.28
  2.2 0.9 subtract_subtract_fusion.first_ref
  3.1 1.9 multiply_sine_fusion
  5.0 1.3 negate_select_fusion
  6.3 96.8 %attn.1 = (f32[128,2048]{1,0:T(8,128)}, bf16[1024,256]{1,0:T(8,128)(2,1)}, bf16[1024,256]{1,0:T(8,128)(2,1)}, bf16[1024,256]{1,0:T(8,128)(2,1)}, f32[1024,256]{1...) custom-call(bf16[128,2048]{1,0:T(8,128)(2,1)} %x_ref.3, ...), custom_call_target="tpu_custom_call" | custom-call | tf_op jit(solution)/shard_map/attn/pallas_call | solution.py:1014
  103.1 205.1 %ffn.1 = (bf16[128,2048]{1,0:T(8,128)(2,1)}, f32[128,2048]{1,0:T(8,128)}, bf16[128,2048]{1,0:T(8,128)(2,1)}, f32[32,128]{1,0:T(8,128)}, bf16[4,8,128,2048]{3,2,1...) custom-call(bf16[128,2048]{1,0:T(8,128)(2,1)} %x_ref.3, ...), custom_call_target="tpu_custom_call" | custom-call | tf_op jit(solution)/shard_map/ffn/pallas_call | solution.py:759
  308.2 140.4 %back.1 = (f32[128,2048]{1,0:T(8,128)}, f32[40,128]{1,0:T(8,128)}, bf16[2,128,2048]{2,1,0:T(8,128)(2,1)}, bf16[4,3,1024,256]{3,2,1,0:T(8,128)(2,1)}, f32[2048,10...) custom-call(bf16[128,2048]{1,0:T(8,128)(2,1)} %get-tuple-element.49.gb_ref, ...), custom_call_target="tpu_custom_call" | custom-call | tf_op jit(solution)/shard_map/back/pallas_call | solution.py:1447
  448.6 1.3 slice_bitcast_fusion.2
  450.0 1.3 slice_bitcast_fusion
  451.3 2.8 bitcast_convert_fusion
  454.1 0.0 copy-start.1
  454.1 0.0 copy-start
  454.1 32.0 %tail.1 = (f32[2048,1024]{1,0:T(8,128)}, f32[2048,1024]{1,0:T(8,128)}, f32[1024,2048]{1,0:T(8,128)}, f32[2048,256]{1,0:T(8,128)}, f32[2048,256]{1,0:T(8,128)}, /*index=5*/f32[2048,256]{1,0:T(8,128)}) custom-call(f32[2048,1024]{1,0:T(8,128)} %get-tuple-element.68.pg_ref, f32[2048,1024]{1,0:T(8,128)} %get-tuple-element.69.pu_ref, ...), custom_call_target="tpu_custom_call" | custom-call | flops 12884901888 | bytes 104857600 | tf_op jit(solution)/shard_map/tail/pallas_call | solution.py:1522
  486.1 0.0 copy-done.1
  486.1 0.8 copy.31
  486.9 0.0 copy-done
  486.9 1.0 copy.32
  (3 shorter events, 0.0 us)
Async XLA Ops:
  454.1 32.0 %copy-start.1 = (bf16[128,2048]{1,0:T(8,128)(2,1)S(1)}, bf16[128,2048]{1,0:T(8,128)(2,1)}, u32[]{:S(2)}) copy-start(bf16[128,2048]{1,0:T(8,128)(2,1)} %get-tuple-element.102) | copy-start | bytes 1572868
  454.1 32.8 %copy-start = (f32[128,2048]{1,0:T(8,128)S(1)}, f32[128,2048]{1,0:T(8,128)}, u32[]{:S(2)}) copy-start(f32[128,2048]{1,0:T(8,128)} %get-tuple-element.103) | copy-start | bytes 3145732

commit v5 on v4

--- a/solution.py
+++ b/solution.py
@@ -350,65 +350,97 @@
         self.parts, self.pair, self.land, self.send, self.recv = parts, pair, land, send, recv
         self.d, _, _, self.zs, self.c, self.inner = place
         self.t = 2 * self.zs[0] + self.c
-
-    def mine(self, r):
-        return self.parts.at[2 * self.zs[r] + self.c]
-
-    def to_core(self, r):
-        src = self.parts.at[2 * self.zs[r] + 1 - self.c]
-        return remote(src, self.pair.at[r], self.send.at[r], self.recv.at[r], self.d, 2 * self.zs[0] + 1 - self.c)
-
-    def to_z(self, r, k, via):
-        return remote(self.mine(r), self.land.at[k], self.send.at[4 + r], self.recv.at[4 + k], self.d, 2 * self.zs[via] + self.c)
-
-    def add_pair(self, r):
-        self.to_core(r).wait_recv()
-        add_into(self.mine(r), self.pair.at[r])
-
-    def pass_on(self, r):
+        self.half = parts.shape[2] // 2
+
+    def cut(self, ref, at, r, h):
+        if h is None:
+            return ref.at[at]
+        return ref.at[at, :, pl.ds(h * self.half, self.half)]
+
+    def mine(self, r, h=None):
+        return self.cut(self.parts, 2 * self.zs[r] + self.c, r, h)
+
+    def to_core(self, r, h=None):
+        src = self.cut(self.parts, 2 * self.zs[r] + 1 - self.c, r, h)
+        at = 8 if h == 1 else r
+        return remote(src, self.cut(self.pair, r, r, h), self.send.at[at], self.recv.at[at], self.d, 2 * self.zs[0] + 1 - self.c)
+
+    def start_core(self, r):
+        for h in (0, 1) if r == 3 else (None,):
+            self.to_core(r, h).start()
+
+    def to_z(self, r, k, via, h=None):
+        return remote(
+            self.mine(r, h), self.cut(self.land, k, r, h), self.send.at[SENT[r, h]], self.recv.at[LANDED[k, h]], self.d,
+            2 * self.zs[via] + self.c,
+        )
+
+    def add_pair(self, r, h=None):
+        halves = (0, 1) if r == 3 and h is None else (h,)
+        for h in halves:
+            self.to_core(r, h).wait_recv()
+            add_into(self.mine(r, h), self.cut(self.pair, r, r, h))
+
+    def pass_on(self, r, h=None):
         if r == 1:
             self.to_z(1, 1, 1).start()
         if r == 2:
             @pl.when(jnp.logical_not(self.inner))
             def _():
-                self.to_z(2, 2, 2).start()
+                for h in range(2):
+                    self.to_z(2, 2, 2, h).start()
         if r == 3:
+            halves = (0, 1) if h is None else (h,)
+
             @pl.when(self.inner)
             def _():
-                self.to_z(3, 3, 3).start()
+                for h in halves:
+                    self.to_z(3, 3, 3, h).start()
 
             @pl.when(jnp.logical_not(self.inner))
             def _():
-                self.to_z(3, 0, 1).start()
+                for h in halves:
+                    self.to_z(3, 0, 1, h).start()
 
     def relay(self):
         @pl.when(self.inner)
         def _():
-            self.to_z(3, 0, 1).wait_recv()
-            add_into(self.mine(2), self.land.at[0])
-            self.to_z(2, 2, 2).start()
+            for h in range(2):
+                self.to_z(3, 0, 1, h).wait_recv()
+                add_into(self.mine(2, h), self.cut(self.land, 0, 0, h))
+                self.to_z(2, 2, 2, h).start()
 
     def arrived(self):
         self.to_z(1, 1, 1).wait_recv()
-        self.to_z(2, 2, 2).wait_recv()
 
         @pl.when(self.inner)
         def _():
-            self.to_z(3, 3, 3).wait_recv()
+            for h in range(2):
+                self.to_z(3, 3, 3, h).wait_recv()
 
         @pl.when(jnp.logical_not(self.inner))
         def _():
             self.land[3] = jnp.zeros(self.land.shape[1:], self.land.dtype)
 
+        for h in range(2):
+            self.to_z(2, 2, 2, h).wait_recv()
+
     def total(self, rows):
         own = self.parts[2 * self.zs[0] + self.c, rows, :].astype(jnp.float32)
         return own + self.land[1, rows, :].astype(jnp.float32) + self.land[2, rows, :].astype(jnp.float32) + self.land[3, rows, :].astype(jnp.float32)
 
     def finish(self):
-        for r in range(4):
+        for r in range(3):
             self.to_core(r).wait_send()
-        for r in (1, 2, 3):
-            self.to_z(r, 1, 1).wait_send()
+        self.to_z(1, 1, 1).wait_send()
+        for h in range(2):
+            self.to_core(3, h).wait_send()
+            self.to_z(2, 2, 2, h).wait_send()
+            self.to_z(3, 3, 3, h).wait_send()
+
+
+SENT = {(1, None): 5, (2, 0): 6, (2, 1): 9, (3, 0): 7, (3, 1): 10}
+LANDED = {(1, None): 5, (2, 0): 6, (2, 1): 9, (3, 0): 7, (3, 1): 10, (0, 0): 4, (0, 1): 11}
 
 
 def add_into(into, other):
@@ -420,6 +452,19 @@
         return carry
 
     lax.fori_loop(0, rows // 32, step, 0)
+
+
+class Loads:
+    def __init__(self, pairs, sem):
+        self.copies = [pltpu.make_async_copy(far, near, sem.at[n]) for n, (far, near) in enumerate(pairs)]
+
+    def start(self):
+        for copy in self.copies:
+            copy.start()
+
+    def wait(self, *which):
+        for n in which:
+            self.copies[n].wait()
 
 
 class Spread:
@@ -487,14 +532,16 @@
 
 
 def ffn_kernel(
-    x_ref, br_ref, cot_ref, again_ref, gain_ref, wg_ref, wu_ref, wd_ref,
+    x_ref, br_ref, cot_ref, again_ref, gain_ref, wg_hbm, wu_hbm, wd_hbm,
     bo_ref, gh_ref, gb_ref, gains_ref, hall_ref, gdall_ref, og_ref, ou_ref, od_ref, gate_all, up_all,
-    hfull, gfull, hid_ref, sums, gate, up, act, gg, gu, parts, pair, land, hbuf, gbuf, ubuf,
-    ag_send, ag_recv, rs_send, rs_recv, xy_send, xy_recv, own_sem, load_sem, store_sem, out_sem,
+    hfull, gfull, hid_ref, sums, gate, up, act, gg, gu, parts, pair, land, hbuf, gbuf, ubuf, wg_ref, wu_ref, wd_ref,
+    ag_send, ag_recv, rs_send, rs_recv, xy_send, xy_recv, own_sem, load_sem, store_sem, out_sem, weight_sem,
 ):
     place = places_of()
     d, dx, dy, zs, c, inner = place
     t = 2 * zs[0] + c
+    weights = Loads(((wg_hbm, wg_ref), (wu_hbm, wu_ref), (wd_hbm, wd_ref)), weight_sem)
+    weights.start()
     width = wg_ref.shape[1]
     rows, wide = x_ref.shape
     ft, dt = 512, 1024
@@ -513,7 +560,7 @@
     lax.fori_loop(0, rows // step_rows, opening, 0)
     enter(d, zs, c, dx, dy)
 
-    def unit_forward(zz):
+    def unit_forward(zz, after=None):
         both = pl.ds(2 * zz, 2)
         at = pl.ds(pl.multiple_of(zz * 2 * rows, 2 * rows), 2 * rows)
 
@@ -535,9 +582,14 @@
             parts[both, :, cols] = p.astype(jnp.bfloat16).reshape(2, rows, dt)
             return carry
 
-        lax.fori_loop(0, wide // dt, out, 0)
-
-    def unit_backward(zz):
+        if after is None:
+            lax.fori_loop(0, wide // dt, out, 0)
+        else:
+            for j in range(wide // dt):
+                out(j, 0)
+                after(j)
+
+    def unit_backward(zz, after=None):
         both = pl.ds(2 * zz, 2)
         at = pl.ds(pl.multiple_of(zz * 2 * rows, 2 * rows), 2 * rows)
 
@@ -559,7 +611,12 @@
             parts[both, :, cols] = p.astype(jnp.bfloat16).reshape(2, rows, dt)
             return carry
 
-        lax.fori_loop(0, wide // dt, out, 0)
+        if after is None:
+            lax.fori_loop(0, wide // dt, out, 0)
+        else:
+            for j in range(wide // dt):
+                out(j, 0)
+                after(j)
 
     def own_copies(i, down):
         slot = pl.ds(pl.multiple_of(lax.rem(i, 4) * 256, 256), 256)
@@ -646,10 +703,13 @@
         ag.start()
         xy.start(0)
         ag.ready(0)
+        if p == 0:
+            weights.wait(0, 1, 2)
         unit(zs[0])
-        rs.to_core(0).start()
+        rs.start_core(0)
         if p == 1:
             fill([(0, 3), (1, 3), (2, 0), (2, 2)])
+        xy.pass_on(0)
         ag.start_inner()
         ag.arrive(2)
         xy.start(2)
@@ -657,10 +717,10 @@
         xy.start(1)
         ag.ready(2)
         unit(zs[2])
-        rs.to_core(2).start()
+        rs.start_core(2)
         ag.ready(1)
         unit(zs[1])
-        rs.to_core(1).start()
+        rs.start_core(1)
         rs.add_pair(2)
         rs.pass_on(2)
         rs.add_pair(1)
@@ -668,24 +728,27 @@
         ag.arrive(3)
         xy.start(3)
         ag.ready(3)
-        unit(zs[3])
-        rs.to_core(3).start()
+        unit(zs[3], lambda j: rs.to_core(3, j).start())
+        for h in range(2):
+            rs.add_pair(3, h)
+            rs.pass_on(3, h)
         xy.keep().start()
-        rs.add_pair(3)
-        rs.pass_on(3)
         rs.add_pair(0)
-        xy.pass_on(0)
-        xy.pass_on(2)
-        xy.pass_on(1)
         if p == 0:
-            fill([(0, 0), (1, 0), (0, 2)])
+            fill([(0, 0), (1, 0)])
+            xy.pass_on(2)
+            xy.pass_on(1)
+            fill([(0, 2)])
         else:
             lax.fori_loop(0, 8, own_in, 0)
+            xy.pass_on(2)
+            xy.pass_on(1)
         rs.relay()
         if p == 0:
             fill([(1, 2), (0, 1), (1, 1)])
         else:
             lax.fori_loop(0, 4, own_down, 0)
+            xy.pass_on(3)
             fill([(2, 1), (2, 3)])
         rs.arrived()
         return ag, rs
@@ -733,7 +796,6 @@
         gains_ref[wide // HD + i : wide // HD + i + 1, :] = sums[1:2, i * HD : (i + 1) * HD]
     ag.finish()
     rs.finish()
-    xy_g.pass_on(3)
     for r in range(4):
         xy_g.last(r)
     xy_h.finish()
@@ -771,7 +833,7 @@
             others,
             others,
         ),
-        in_specs=[vmem] * 8,
+        in_specs=[vmem] * 5 + [anywhere] * 3,
         out_specs=(vmem,) * 4 + (anywhere,) * 7,
         scratch_shapes=[
             pltpu.VMEM((world, rows, wide), bf),
@@ -789,16 +851,20 @@
             pltpu.VMEM((2, 2, rows, wide), bf),
             pltpu.VMEM((2, 2 * rows, width), bf),
             pltpu.VMEM((2, 2 * rows, width), bf),
+            pltpu.VMEM((wide, width), bf),
+            pltpu.VMEM((wide, width), bf),
+            pltpu.VMEM((width, wide), bf),
             dma((2, 8)),
             dma((2, 8)),
-            dma((2, 8)),
-            dma((2, 8)),
+            dma((2, 12)),
+            dma((2, 12)),
             dma((2, 24)),
             dma((2, 24)),
             dma((2,)),
             dma((2,)),
             dma((2, 2)),
             dma((2, 4)),
+            dma((3,)),
         ],
         compiler_params=pltpu.CompilerParams(
             collective_id=2, has_side_effects=True, vmem_limit_bytes=60 * 2**20
@@ -860,16 +926,18 @@
 
 
 def attn_kernel(
-    x_ref, wq_ref, wk_ref, wv_ref, wo_ref, qg_ref, kg_ref, cos_ref, sin_ref, first_ref,
+    x_ref, wq_hbm, wk_hbm, wv_hbm, wo_hbm, qg_ref, kg_ref, cos_ref, sin_ref, first_ref,
     br_ref, q_out, k_out, v_out, qu_out, ku_out, rq_out, rk_out, mixed_out, xall_ref,
-    xfull, parts, pair, land, stat, stats,
-    ag_send, ag_recv, rs_send, rs_recv, xy_send, xy_recv, st_send, st_recv, own_sem,
+    xfull, parts, pair, land, stat, stats, wq_ref, wk_ref, wv_ref, wo_ref,
+    ag_send, ag_recv, rs_send, rs_recv, xy_send, xy_recv, st_send, st_recv, own_sem, weight_sem,
 ):
     place = places_of()
     d, dx, dy, zs, c, inner = place
     t = 2 * zs[0] + c
     rows, wide = x_ref.shape
     span = 2 * rows
+    weights = Loads(((wq_hbm, wq_ref), (wk_hbm, wk_ref), (wv_hbm, wv_ref), (wo_hbm, wo_ref)), weight_sem)
+    weights.start()
     heads = wq_ref.shape[1] // HD
     xfull[t] = x_ref[...]
     enter_all(d, zs, c, dx, dy)
@@ -895,8 +963,10 @@
     ag.start()
     xy.start(0)
     ag.ready(0)
+    weights.wait(0, 1, 2, 3)
     project_qk(zs[0])
     project_v(zs[0])
+    xy.pass_on(0)
     ag.start_inner()
     ag.arrive(2)
     xy.start(2)
@@ -966,21 +1036,20 @@
         lax.fori_loop(0, wide // dt, out, 0)
 
     attend(zs[3])
-    rs.to_core(3).start()
+    rs.start_core(3)
     attend(zs[2])
-    rs.to_core(2).start()
+    rs.start_core(2)
     rs.add_pair(3)
     rs.pass_on(3)
     attend(zs[1])
-    rs.to_core(1).start()
+    rs.start_core(1)
     rs.add_pair(2)
     rs.pass_on(2)
     rs.add_pair(1)
     rs.pass_on(1)
     attend(zs[0])
-    rs.to_core(0).start()
+    rs.start_core(0)
     rs.add_pair(0)
-    xy.pass_on(0)
     xy.pass_on(2)
     xy.pass_on(1)
     rs.relay()
@@ -1006,6 +1075,7 @@
     groups, world = 4, 8
     count = world * rows
     vmem = pl.BlockSpec(memory_space=pltpu.VMEM)
+    anywhere = pl.BlockSpec(memory_space=pl.ANY)
     bf, f32 = jnp.bfloat16, jnp.float32
     dma = pltpu.SemaphoreType.DMA
     cols = jax.ShapeDtypeStruct((count, head_cols), bf)
@@ -1018,7 +1088,7 @@
             cols, cols, cols, wide_cols, wide_cols, line, line, cols,
             jax.ShapeDtypeStruct((groups, world, rows, wide), bf),
         ),
-        in_specs=[vmem] * 10,
+        in_specs=[vmem] + [anywhere] * 4 + [vmem] * 5,
         out_specs=(vmem,) * 9 + (pl.BlockSpec(memory_space=pl.ANY),),
         scratch_shapes=[
             pltpu.VMEM((world, rows, wide), bf),
@@ -1027,8 +1097,12 @@
             pltpu.VMEM((4, rows, wide), bf),
             pltpu.VMEM((16, HD), f32),
             pltpu.VMEM((world, 16, HD), f32),
-            dma((8,)), dma((8,)), dma((8,)), dma((8,)), dma((24,)), dma((24,)), dma((8,)), dma((8,)),
-            pltpu.SemaphoreType.DMA,
+            pltpu.VMEM((wide, head_cols), bf),
+            pltpu.VMEM((wide, head_cols), bf),
+            pltpu.VMEM((wide, head_cols), bf),
+            pltpu.VMEM((head_cols, wide), bf),
+            dma((8,)), dma((8,)), dma((12,)), dma((12,)), dma((24,)), dma((24,)), dma((8,)), dma((8,)),
+            pltpu.SemaphoreType.DMA, dma((4,)),
         ],
         compiler_params=pltpu.CompilerParams(
             collective_id=1, has_side_effects=True, vmem_limit_bytes=60 * 2**20
@@ -1219,13 +1293,14 @@
 
 
 def back_kernel(
-    gb_ref, gh_ref, q_ref, k_ref, v_ref, mixed_ref, qu_ref, ku_ref, rq_ref, rk_ref, first_ref, cos_ref, sin_ref,
-    qg_ref, kg_ref, wq_ref, wk_ref, wv_ref, wo_ref, gains_ref, hall, gdall, gate_all, up_all, w_down, own_g, own_u, own_d,
+    gb_ref, gh_ref, q_hbm, k_hbm, v_hbm, mixed_hbm, qu_hbm, ku_hbm, rq_ref, rk_ref, first_ref, cos_ref, sin_ref,
+    qg_ref, kg_ref, wq_hbm, wk_hbm, wv_hbm, wo_hbm, gains_ref, hall, gdall, gate_all, up_all, w_down, own_g, own_u, own_d,
     gt_ref, gains_out, dwo_ref, gall_ref, dwg, dwu, dwd,
     full, pair, land, gm, dq, dk, dv, own, wo_once, wo_twice, stat, stats, gland, block, blocks, gacc,
     hbuf, gbuf, gbf, ubf, td, sg, su, sd, act, gg, gu,
+    q_ref, k_ref, v_ref, mixed_ref, qu_ref, ku_ref, wq_ref, wk_ref, wv_ref, wo_ref,
     ag_send, ag_recv, rs_send, rs_recv, st_send, st_recv, ga_send, ga_recv, gr_send, gr_recv,
-    co_send, co_recv, wo_send, wo_recv, own_sem, load_sem, tile_sem, start_sem, out_sem,
+    co_send, co_recv, wo_send, wo_recv, own_sem, load_sem, tile_sem, start_sem, out_sem, input_sem,
 ):
     place = places_of()
     d, dx, dy, zs, c, inner = place
@@ -1235,6 +1310,13 @@
     heads = wq_ref.shape[1] // HD
     count = q_ref.shape[0]
     scale = HD**-0.5
+    inputs = Loads(
+        (
+            (wo_hbm, wo_ref), (mixed_hbm, mixed_ref), (q_hbm, q_ref), (k_hbm, k_ref), (v_hbm, v_ref), (qu_hbm, qu_ref), (ku_hbm, ku_ref),
+            (wq_hbm, wq_ref), (wk_hbm, wk_ref), (wv_hbm, wv_ref),
+        ),
+        input_sem,
+    )
     full[t] = gb_ref[...]
     barrier = pltpu.get_barrier_semaphore()
     peers = [(d, 2 * zs[r] + c) for r in (1, 2, 3)] + [(d, 2 * zs[r] + 1 - c) for r in range(4)]
@@ -1260,6 +1342,7 @@
     ag.start()
     gains.start()
     work.begin()
+    inputs.start()
     work.step(0)
     work.step(1)
     ag.ready(0)
@@ -1274,6 +1357,8 @@
     work.step(4)
     work.step(5)
     ag.ready(3)
+
+    inputs.wait(*range(10))
 
     def mixed_back(zz, carry):
         part = full[pl.ds(2 * zz, 2)].reshape(span, wide)
@@ -1392,19 +1477,19 @@
         lax.fori_loop(0, wide // dt, out, 0)
 
     tokens_back(zs[3])
-    rs.to_core(3).start()
+    rs.start_core(3)
     tokens_back(zs[2])
-    rs.to_core(2).start()
+    rs.start_core(2)
     rs.add_pair(3)
     rs.pass_on(3)
     tokens_back(zs[1])
-    rs.to_core(1).start()
+    rs.start_core(1)
     rs.add_pair(2)
     rs.pass_on(2)
     rs.add_pair(1)
     rs.pass_on(1)
     tokens_back(zs[0])
-    rs.to_core(0).start()
+    rs.start_core(0)
     rs.add_pair(0)
     cols_all.pass_on(2)
     wo_sum.add(1)
@@ -1455,7 +1540,7 @@
             jax.ShapeDtypeStruct((wide, width), f32),
             jax.ShapeDtypeStruct((width, wide), f32),
         ),
-        in_specs=[vmem] * 20 + [anywhere] * 8,
+        in_specs=[vmem] * 2 + [anywhere] * 6 + [vmem] * 7 + [anywhere] * 4 + [vmem] + [anywhere] * 8,
         out_specs=(vmem, vmem, vmem) + (anywhere,) * 4,
         scratch_shapes=[
             pltpu.VMEM((world, rows, wide), bf),
@@ -1485,8 +1570,18 @@
             pltpu.VMEM((tok, unit), bf),
             pltpu.VMEM((tok, unit), bf),
             pltpu.VMEM((tok, unit), bf),
-            dma((8,)), dma((8,)), dma((8,)), dma((8,)), dma((8,)), dma((8,)), dma((8,)), dma((8,)), dma((3,)), dma((3,)),
-            dma((12,)), dma((12,)), dma((4,)), dma((4,)), pltpu.SemaphoreType.DMA, dma((4, 2)), pltpu.SemaphoreType.DMA, dma((3,)), dma((3,)),
+            pltpu.VMEM((count, head_cols), bf),
+            pltpu.VMEM((count, head_cols), bf),
+            pltpu.VMEM((count, head_cols), bf),
+            pltpu.VMEM((count, head_cols), bf),
+            pltpu.VMEM((count, head_cols), f32),
+            pltpu.VMEM((count, head_cols), f32),
+            pltpu.VMEM((wide, head_cols), bf),
+            pltpu.VMEM((wide, head_cols), bf),
+            pltpu.VMEM((wide, head_cols), bf),
+            pltpu.VMEM((head_cols, wide), bf),
+            dma((8,)), dma((8,)), dma((12,)), dma((12,)), dma((8,)), dma((8,)), dma((8,)), dma((8,)), dma((3,)), dma((3,)),
+            dma((12,)), dma((12,)), dma((4,)), dma((4,)), pltpu.SemaphoreType.DMA, dma((4, 2)), pltpu.SemaphoreType.DMA, dma((3,)), dma((3,)), dma((10,)),
         ],
         compiler_params=pltpu.CompilerParams(
             collective_id=3, has_side_effects=True, vmem_limit_bytes=62 * 2**20
@@ -1498,11 +1593,18 @@
     )
 
 
-def tail_kernel(pg_ref, pu_ref, pd_ref, x_ref, g_ref, og_ref, ou_ref, od_ref, oq_ref, ok_ref, ov_ref):
+def tail_kernel(
+    pg_ref, pu_ref, pd_ref, x_ref, g_ref, wo_ref, gains_ref, og_ref, ou_ref, od_ref, oq_ref, ok_ref, ov_ref, oo_ref, *gain_refs
+):
     count, cols = g_ref.shape[2], x_ref.shape[-1]
     og_ref[...] = pg_ref[...]
     ou_ref[...] = pu_ref[...]
     od_ref[...] = pd_ref[...]
+    oo_ref[...] = wo_ref[...].reshape(oo_ref.shape).astype(jnp.float32)
+    row = 0
+    for out in gain_refs:
+        out[...] = gains_ref[row : row + out.shape[0], :]
+        row += out.shape[0]
     for p, out in enumerate((oq_ref, ok_ref, ov_ref)):
         total = jnp.zeros(out.shape, jnp.float32)
         for g in range(4):
@@ -1510,7 +1612,7 @@
         out[...] = total
 
 
-def weight_tail(parts, x_all, grad_qkv):
+def weight_tail(parts, x_all, grad_qkv, grad_out, gains):
     groups, world, rows, wide = x_all.shape
     count, width = world * rows, parts[0].shape[1]
     head_cols = grad_qkv.shape[-1]
@@ -1519,6 +1621,7 @@
     down = pl.BlockSpec((cols, width), lambda i: (i, 0))
     across = pl.BlockSpec((width, cols), lambda i: (0, i))
     heads = pl.BlockSpec((cols, head_cols), lambda i: (i, 0))
+    lines = [(wide // HD, HD)] * 2 + [(head_cols // HD, HD)] * 2
     return pl.pallas_call(
         tail_kernel,
         grid=(wide // cols,),
@@ -1526,20 +1629,25 @@
             down, down, across,
             pl.BlockSpec((groups, world, rows, cols), lambda i: (0, 0, 0, i)),
             pl.BlockSpec(grad_qkv.shape, lambda i: (0, 0, 0, 0)),
+            pl.BlockSpec((2, head_cols // 2, cols), lambda i: (0, 0, i)),
+            pl.BlockSpec(gains.shape, lambda i: (0, 0)),
         ],
-        out_specs=(down, down, across, heads, heads, heads),
+        out_specs=(down, down, across, heads, heads, heads, pl.BlockSpec((head_cols, cols), lambda i: (0, i)))
+        + tuple(pl.BlockSpec(shape, lambda i: (0, 0)) for shape in lines),
         out_shape=(
             jax.ShapeDtypeStruct((wide, width), f32),
             jax.ShapeDtypeStruct((wide, width), f32),
             jax.ShapeDtypeStruct((width, wide), f32),
         )
-        + (jax.ShapeDtypeStruct((wide, head_cols), f32),) * 3,
+        + (jax.ShapeDtypeStruct((wide, head_cols), f32),) * 3
+        + (jax.ShapeDtypeStruct((head_cols, wide), f32),)
+        + tuple(jax.ShapeDtypeStruct(shape, f32) for shape in lines),
         compiler_params=pltpu.CompilerParams(vmem_limit_bytes=60 * 2**20),
         cost_estimate=pl.CostEstimate(
             flops=2 * count * wide * 3 * groups * head_cols, bytes_accessed=100 * 2**20, transcendentals=0
         ),
         name="tail",
-    )(*parts, x_all, grad_qkv)
+    )(*parts, x_all, grad_qkv, grad_out, gains)
 
 
 def on_device_fused(
@@ -1576,25 +1684,24 @@
         first, cosine, signed, q_gain, k_gain, (w_query, w_key, w_value, w_out), gains, h_all, gd_all, gate_all, up_all, w_down,
         (own_gate, own_up, own_down),
     )
-    grad_w_gate, grad_w_up, grad_w_down, grad_w_query, grad_w_key, grad_w_value = weight_tail(
-        (part_gate, part_up, part_down), x_all, grad_qkv
-    )
-    lines = wide // HD
-    gain_rows = head_cols // HD
+    *grad_weights, grad_ffn_gain, grad_attn_gain, grad_q_gain, grad_k_gain = weight_tail(
+        (part_gate, part_up, part_down), x_all, grad_qkv, grad_w_out, gains
+    )
+    grad_w_gate, grad_w_up, grad_w_down, grad_w_query, grad_w_key, grad_w_value, grad_w_out = grad_weights
     return (
         block_out,
         grad_tokens,
         grad_w_query,
         grad_w_key,
         grad_w_value,
-        grad_w_out.reshape(head_cols, wide).astype(jnp.float32),
+        grad_w_out,
         grad_w_gate,
         grad_w_up,
         grad_w_down,
-        gains[2 * lines : 2 * lines + gain_rows].reshape(head_cols),
-        gains[2 * lines + gain_rows : 2 * lines + 2 * gain_rows].reshape(head_cols),
-        gains[lines : 2 * lines].reshape(wide),
-        gains[:lines].reshape(wide),
+        grad_q_gain.reshape(head_cols),
+        grad_k_gain.reshape(head_cols),
+        grad_attn_gain.reshape(wide),
+        grad_ffn_gain.reshape(wide),
     )
 
 

time: 497 us -> 476 us (0.958)
  Pallas kernels: 474 us -> 459 us
    pallas_call x1, Pallas kernels: 205 us -> 187 us  [ffn(): pl.pallas_call(ffn_kernel, out_shape=(jax.ShapeDtypeStruct((rows, wide),...]
where the time goes in v5:
time: 476 us; the launch traced here: 467 us
  Pallas kernels  459 us (96%)
  other arithmetic  5.36 us (1%)
    pallas_call x1, Pallas kernels, ffn(): pl.pallas_call(ffn_kernel, out_shape=(jax.ShapeDtypeStruct((rows, wide),...  187 us
    pallas_call x1, Pallas kernels, backward(): pl.pallas_call(back_kernel, out_shape=(jax.ShapeDtypeStruct((rows, wide),...  143 us
    pallas_call x1, Pallas kernels, attention(): pl.pallas_call(attn_kernel, out_shape=(jax.ShapeDtypeStruct((rows, wide),...  95.7 us
    pallas_call x1, Pallas kernels, weight_tail(): pl.pallas_call(tail_kernel, grid=(wide // cols,), in_specs=[down, down, a...  32.8 us

profile of v5, /device:TPU:0, one launch (start us, length us, event | category | flops | bytes accessed | tf_op | source)
XLA Modules:
  0.0 467.3 jit_solution(8466705464669964969)
XLA Ops:
  0.7 1.3 convert_reduce_fusion
  2.0 0.2 copy.28
  2.2 0.9 subtract_subtract_fusion.first_ref
  3.1 1.9 multiply_sine_fusion
  5.0 1.3 negate_select_fusion
  6.3 95.7 %attn.1 = (f32[128,2048]{1,0:T(8,128)}, bf16[1024,256]{1,0:T(8,128)(2,1)}, bf16[1024,256]{1,0:T(8,128)(2,1)}, bf16[1024,256]{1,0:T(8,128)(2,1)}, f32[1024,256]{1...) custom-call(bf16[128,2048]{1,0:T(8,128)(2,1)} %x_ref.3, ...), custom_call_target="tpu_custom_call" | custom-call | tf_op jit(solution)/shard_map/attn/pallas_call | solution.py:1084
  101.9 187.0 %ffn.1 = (bf16[128,2048]{1,0:T(8,128)(2,1)}, f32[128,2048]{1,0:T(8,128)}, bf16[128,2048]{1,0:T(8,128)(2,1)}, f32[32,128]{1,0:T(8,128)}, bf16[4,8,128,2048]{3,2,1...) custom-call(bf16[128,2048]{1,0:T(8,128)(2,1)} %x_ref.3, ...), custom_call_target="tpu_custom_call" | custom-call | tf_op jit(solution)/shard_map/ffn/pallas_call | solution.py:821
  288.9 143.3 %back.1 = (f32[128,2048]{1,0:T(8,128)}, f32[40,128]{1,0:T(8,128)}, bf16[2,128,2048]{2,1,0:T(8,128)(2,1)}, bf16[4,3,1024,256]{3,2,1,0:T(8,128)(2,1)}, f32[2048,10...) custom-call(bf16[128,2048]{1,0:T(8,128)(2,1)} %get-tuple-element.54.gb_ref, ...), custom_call_target="tpu_custom_call" | custom-call | tf_op jit(solution)/shard_map/back/pallas_call | solution.py:1532
  432.3 0.0 copy-start.1
  432.3 0.0 copy-start
  432.3 32.8 %tail.1 = (f32[2048,1024]{1,0:T(8,128)}, f32[2048,1024]{1,0:T(8,128)}, f32[1024,2048]{1,0:T(8,128)}, f32[2048,256]{1,0:T(8,128)}, f32[2048,256]{1,0:T(8,128)}, /...) custom-call(f32[2048,1024]{1,0:T(8,128)} %get-tuple-element.73.pg_re, ...), custom_call_target="tpu_custom_call" | custom-call | flops 12884901888 | bytes 104857600 | tf_op jit(solution)/shard_map/tail/pallas_call | solution.py:1625
  465.1 0.0 copy-done.1
  465.1 0.8 copy.31
  465.9 0.0 copy-done
  465.9 1.0 copy.32
  (3 shorter events, 0.0 us)
Async XLA Ops:
  432.3 32.8 %copy-start.1 = (bf16[128,2048]{1,0:T(8,128)(2,1)S(1)}, bf16[128,2048]{1,0:T(8,128)(2,1)}, u32[]{:S(2)}) copy-start(bf16[128,2048]{1,0:T(8,128)(2,1)} %get-tuple-element.108) | copy-start | bytes 1572868
  432.3 33.6 %copy-start = (f32[128,2048]{1,0:T(8,128)S(1)}, f32[128,2048]{1,0:T(8,128)}, u32[]{:S(2)}) copy-start(f32[128,2048]{1,0:T(8,128)} %get-tuple-element.109) | copy-start | bytes 3145732

commit v6 on v5

--- a/solution.py
+++ b/solution.py
@@ -740,16 +740,19 @@
             xy.pass_on(1)
             fill([(0, 2)])
         else:
-            lax.fori_loop(0, 8, own_in, 0)
             xy.pass_on(2)
             xy.pass_on(1)
+            lax.fori_loop(0, 8, own_in, 0)
         rs.relay()
         if p == 0:
             fill([(1, 2), (0, 1), (1, 1)])
         else:
+            xy.pass_on(3)
             lax.fori_loop(0, 4, own_down, 0)
-            xy.pass_on(3)
+            xy.last(0)
             fill([(2, 1), (2, 3)])
+            xy.last(2)
+            xy.last(1)
         rs.arrived()
         return ag, rs
 
@@ -796,8 +799,7 @@
         gains_ref[wide // HD + i : wide // HD + i + 1, :] = sums[1:2, i * HD : (i + 1) * HD]
     ag.finish()
     rs.finish()
-    for r in range(4):
-        xy_g.last(r)
+    xy_g.last(3)
     xy_h.finish()
     for i in range(4):
         for copy in own_copies(i, True):
@@ -1180,22 +1182,14 @@
         wd = self.tile
         act, gg, gu = self.mids
         rows, wide = hbuf.shape[1:]
-        half = self.tokens // 2
-
-        def mid(i, carry):
-            blocks = pl.ds(i * (self.blocks // 2), self.blocks // 2)
-            at = pl.ds(pl.multiple_of(i * half, half), half)
-            g, u = gate[at, :].astype(jnp.float32), up[at, :].astype(jnp.float32)
-            ga = dot_nt(gbuf[blocks].reshape(half, wide), wd[...])
-            s = jax.nn.sigmoid(g)
-            gs = g * s
-            act[at, :] = (gs * u).astype(jnp.bfloat16)
-            gg[at, :] = (ga * u * s * (1.0 + g * (1.0 - s))).astype(jnp.bfloat16)
-            gu[at, :] = (ga * gs).astype(jnp.bfloat16)
-            return carry
-
-        lax.fori_loop(0, 2, mid, 0)
-        span = 512
+        g, u = gate[...].astype(jnp.float32), up[...].astype(jnp.float32)
+        ga = dot_nt(gbuf[...].reshape(self.tokens, wide), wd[...])
+        s = jax.nn.sigmoid(g)
+        gs = g * s
+        act[...] = (gs * u).astype(jnp.bfloat16)
+        gg[...] = (ga * u * s * (1.0 + g * (1.0 - s))).astype(jnp.bfloat16)
+        gu[...] = (ga * gs).astype(jnp.bfloat16)
+        span = 1024
 
         def into(i, carry):
             at = pl.ds(pl.multiple_of(i * span, span), span)
@@ -1317,6 +1311,12 @@
         ),
         input_sem,
     )
+    work = Background(
+        hall, gdall, gate_all, up_all, w_down, (own_g, own_u, own_d), (dwg, dwu, dwd), hbuf, gbuf, gbf, ubf, td, (sg, su, sd), (act, gg, gu),
+        load_sem, tile_sem, start_sem, out_sem,
+    )
+    work.begin()
+    inputs.start()
     full[t] = gb_ref[...]
     barrier = pltpu.get_barrier_semaphore()
     peers = [(d, 2 * zs[r] + c) for r in (1, 2, 3)] + [(d, 2 * zs[r] + 1 - c) for r in range(4)]
@@ -1331,56 +1331,20 @@
     groups = ExchangeGroups(block, blocks, gr_send, gr_recv, place)
     cols_all = SpreadColumns(own, gall_ref, co_send, co_recv, own_sem, place)
     wo_sum = SumHalves(dwo_ref, wo_once, wo_twice, wo_send, wo_recv, place)
-    work = Background(
-        hall, gdall, gate_all, up_all, w_down, (own_g, own_u, own_d), (dwg, dwu, dwd), hbuf, gbuf, gbf, ubf, td, (sg, su, sd), (act, gg, gu),
-        load_sem, tile_sem, start_sem, out_sem,
-    )
-
     def at_of(zz):
         return pl.ds(pl.multiple_of(zz * span, span), span)
 
     ag.start()
     gains.start()
-    work.begin()
-    inputs.start()
-    work.step(0)
-    work.step(1)
-    ag.ready(0)
-    ag.start_inner()
-    ag.arrive(2)
-    ag.arrive(1)
-    work.step(2)
-    work.step(3)
-    ag.ready(2)
-    ag.ready(1)
-    ag.arrive(3)
-    work.step(4)
-    work.step(5)
-    ag.ready(3)
-
-    inputs.wait(*range(10))
-
-    def mixed_back(zz, carry):
-        part = full[pl.ds(2 * zz, 2)].reshape(span, wide)
-        gm[at_of(zz), :] = dot_nt(part, wo_ref[...]).astype(jnp.bfloat16)
-        return carry
-
-    lax.fori_loop(0, 4, mixed_back, 0)
-
     def out_back(j, carry):
         to = pl.ds(pl.multiple_of(j * 512, 512), 512)
         p = dot_tn(mixed_ref[...], full[:, :, to].reshape(count, 512))
         dwo_ref[:, :, to] = p.astype(jnp.bfloat16).reshape(2, p.shape[0] // 2, 512)
         return carry
 
-    lax.fori_loop(0, wide // 512, out_back, 0)
-    wo_sum.start(0)
-    ag.finish()
-    dk[...] = jnp.zeros_like(dk)
-    dv[...] = jnp.zeros_like(dv)
-
-    def attend_back(zz, carry):
+    def attend_back(zz):
         at = at_of(zz)
+        gm[at, :] = dot_nt(full[pl.ds(2 * zz, 2)].reshape(span, wide), wo_ref[...]).astype(jnp.bfloat16)
         low = jnp.maximum(zz - (WINDOW - 1), 0) * span
         keys_at = pl.ds(pl.multiple_of(low, span), WINDOW * span)
         key_place = low + lax.broadcasted_iota(jnp.int32, (span, WINDOW * span), 1)
@@ -1399,13 +1363,27 @@
             dq[at, cols] = jnp.dot(gs, k_ref[keys_at, cols], preferred_element_type=jnp.float32) * scale
             dk[keys_at, cols] += dot_tn(gs, q_ref[at, cols]) * scale
             dv[keys_at, cols] += dot_tn(probs.astype(jnp.bfloat16), grad)
-        return carry
-
-    lax.fori_loop(0, 2, attend_back, 0)
-    wo_sum.add(0)
-    wo_sum.start(1)
-    work.turn(0)
-    lax.fori_loop(2, 4, attend_back, 0)
+
+    dk[...] = jnp.zeros_like(dk)
+    dv[...] = jnp.zeros_like(dv)
+    work.step(0)
+    ag.ready(0)
+    inputs.wait(*range(10))
+    attend_back(zs[0])
+    work.step(1)
+    work.step(2)
+    ag.start_inner()
+    ag.arrive(2)
+    ag.arrive(1)
+    work.step(3)
+    ag.ready(2)
+    attend_back(zs[2])
+    ag.ready(1)
+    attend_back(zs[1])
+    ag.arrive(3)
+    work.step(4)
+    ag.ready(3)
+    attend_back(zs[3])
     own[2] = dv[...].astype(jnp.bfloat16)
     cols_all.start(2)
     gacc[...] = jnp.zeros_like(gacc)
@@ -1440,7 +1418,10 @@
     block[:lines, :] = total
     block[lines:, :] = gacc[...]
     groups.start()
-    work.step(6)
+    lax.fori_loop(0, wide // 512, out_back, 0)
+    wo_sum.start(0)
+    ag.finish()
+    work.step(5)
     ex.wait()
     total = stat[...]
     for r in range(4):
@@ -1478,6 +1459,7 @@
 
     tokens_back(zs[3])
     rs.start_core(3)
+    work.turn(0)
     tokens_back(zs[2])
     rs.start_core(2)
     rs.add_pair(3)
@@ -1492,15 +1474,18 @@
     rs.start_core(0)
     rs.add_pair(0)
     cols_all.pass_on(2)
-    wo_sum.add(1)
+    work.step(6)
+    rs.relay()
     work.step(7)
-    rs.relay()
+    wo_sum.add(0)
+    wo_sum.start(1)
     work.step(8)
     work.step(9)
     cols_all.pass_on(0)
+    work.step(10)
     cols_all.pass_on(1)
-    work.step(10)
     work.step(11)
+    wo_sum.add(1)
     rs.arrived()
 
     def ending(i, carry):
@@ -1616,7 +1601,7 @@
     groups, world, rows, wide = x_all.shape
     count, width = world * rows, parts[0].shape[1]
     head_cols = grad_qkv.shape[-1]
-    cols = 256
+    cols = 512
     f32 = jnp.float32
     down = pl.BlockSpec((cols, width), lambda i: (i, 0))
     across = pl.BlockSpec((width, cols), lambda i: (0, i))

time: 476 us -> 463 us (0.973)
  Pallas kernels: 459 us -> 445 us
    pallas_call x1, Pallas kernels: 143 us -> 131 us  [backward(): pl.pallas_call(back_kernel, out_shape=(jax.ShapeDtypeStruct((rows, wide),...]
where the time goes in v6:
time: 463 us; the launch traced here: 454 us
  Pallas kernels  445 us (96%)
  other arithmetic  5.36 us (1%)
    pallas_call x1, Pallas kernels, ffn(): pl.pallas_call(ffn_kernel, out_shape=(jax.ShapeDtypeStruct((rows, wide),...  187 us
    pallas_call x1, Pallas kernels, backward(): pl.pallas_call(back_kernel, out_shape=(jax.ShapeDtypeStruct((rows, wide),...  131 us
    pallas_call x1, Pallas kernels, attention(): pl.pallas_call(attn_kernel, out_shape=(jax.ShapeDtypeStruct((rows, wide),...  95.7 us
    pallas_call x1, Pallas kernels, weight_tail(): pl.pallas_call(tail_kernel, grid=(wide // cols,), in_specs=[down, down, a...  32.1 us

profile of v6, /device:TPU:0, one launch (start us, length us, event | category | flops | bytes accessed | tf_op | source)
XLA Modules:
  0.0 454.0 jit_solution(9236074193653036863)
XLA Ops:
  0.7 1.3 convert_reduce_fusion
  2.0 0.2 copy.28
  2.2 0.9 subtract_subtract_fusion.first_ref
  3.1 1.9 multiply_sine_fusion
  5.0 1.3 negate_select_fusion
  6.3 95.7 %attn.1 = (f32[128,2048]{1,0:T(8,128)}, bf16[1024,256]{1,0:T(8,128)(2,1)}, bf16[1024,256]{1,0:T(8,128)(2,1)}, bf16[1024,256]{1,0:T(8,128)(2,1)}, f32[1024,256]{1...) custom-call(bf16[128,2048]{1,0:T(8,128)(2,1)} %x_ref.3, ...), custom_call_target="tpu_custom_call" | custom-call | tf_op jit(solution)/shard_map/attn/pallas_call | solution.py:1086
  101.9 186.6 %ffn.1 = (bf16[128,2048]{1,0:T(8,128)(2,1)}, f32[128,2048]{1,0:T(8,128)}, bf16[128,2048]{1,0:T(8,128)(2,1)}, f32[32,128]{1,0:T(8,128)}, bf16[4,8,128,2048]{3,2,1...) custom-call(bf16[128,2048]{1,0:T(8,128)(2,1)} %x_ref.3, ...), custom_call_target="tpu_custom_call" | custom-call | tf_op jit(solution)/shard_map/ffn/pallas_call | solution.py:823
  288.6 131.1 %back.1 = (f32[128,2048]{1,0:T(8,128)}, f32[40,128]{1,0:T(8,128)}, bf16[2,128,2048]{2,1,0:T(8,128)(2,1)}, bf16[4,3,1024,256]{3,2,1,0:T(8,128)(2,1)}, f32[2048,10...) custom-call(bf16[128,2048]{1,0:T(8,128)(2,1)} %get-tuple-element.54.gb_ref, ...), custom_call_target="tpu_custom_call" | custom-call | tf_op jit(solution)/shard_map/back/pallas_call | solution.py:1517
  419.6 0.0 copy-start.1
  419.6 0.0 copy-start
  419.6 32.1 %tail.1 = (f32[2048,1024]{1,0:T(8,128)}, f32[2048,1024]{1,0:T(8,128)}, f32[1024,2048]{1,0:T(8,128)}, f32[2048,256]{1,0:T(8,128)}, f32[2048,256]{1,0:T(8,128)}, /...) custom-call(f32[2048,1024]{1,0:T(8,128)} %get-tuple-element.73.pg_re, ...), custom_call_target="tpu_custom_call" | custom-call | flops 12884901888 | bytes 104857600 | tf_op jit(solution)/shard_map/tail/pallas_call | solution.py:1610
  451.7 0.0 copy-done.1
  451.8 0.8 copy.31
  452.6 0.0 copy-done
  452.6 1.0 copy.32
  (3 shorter events, 0.0 us)
Async XLA Ops:
  419.6 32.1 %copy-start.1 = (bf16[128,2048]{1,0:T(8,128)(2,1)S(1)}, bf16[128,2048]{1,0:T(8,128)(2,1)}, u32[]{:S(2)}) copy-start(bf16[128,2048]{1,0:T(8,128)(2,1)} %get-tuple-element.108) | copy-start | bytes 1572868
  419.6 32.9 %copy-start = (f32[128,2048]{1,0:T(8,128)S(1)}, f32[128,2048]{1,0:T(8,128)}, u32[]{:S(2)}) copy-start(f32[128,2048]{1,0:T(8,128)} %get-tuple-element.109) | copy-start | bytes 3145732

commit v7 on v6

--- a/solution.py
+++ b/solution.py
@@ -1654,10 +1654,11 @@
     wide = tokens.shape[1]
     token_count = segment_ids.shape[0] * segment_ids.shape[1]
     head_cols = w_query.shape[1]
-    positions = positions_of(segment_ids).reshape(token_count)
-    cosine, sine = rotary_tables(positions)
-    first = (jnp.arange(token_count, dtype=jnp.int32) - positions)[:, None]
-    signed = jnp.where(jnp.arange(HD) < HD // 2, -sine, sine)
+    first = jnp.sum((segment_ids[:, None, :] < segment_ids[:, :, None]).astype(jnp.int32), axis=2).reshape(token_count, 1)
+    half = HD // 2
+    freq = THETA ** (-(jnp.arange(half, dtype=jnp.float32) * 2.0 / HD))
+    angle = (jnp.arange(token_count, dtype=jnp.int32)[:, None] - first).astype(jnp.float32) * jnp.concatenate([-freq, freq])[None, :]
+    cosine, signed = jnp.cos(angle), jnp.sin(angle)
     branch, queries, keys, values, q_unit, k_unit, q_inverse, k_inverse, mixed, x_all = attention(
         tokens, w_query, w_key, w_value, w_out, q_gain, k_gain, cosine, signed, first
     )

time: 463 us -> 462 us (level)
  no operation moved by 1% of the time
where the time goes in v7:
time: 462 us; the launch traced here: 454 us
  Pallas kernels  445 us (96%)
    pallas_call x1, Pallas kernels, ffn(): pl.pallas_call(ffn_kernel, out_shape=(jax.ShapeDtypeStruct((rows, wide),...  187 us
    pallas_call x1, Pallas kernels, backward(): pl.pallas_call(back_kernel, out_shape=(jax.ShapeDtypeStruct((rows, wide),...  131 us
    pallas_call x1, Pallas kernels, attention(): pl.pallas_call(attn_kernel, out_shape=(jax.ShapeDtypeStruct((rows, wide),...  95.7 us
    pallas_call x1, Pallas kernels, weight_tail(): pl.pallas_call(tail_kernel, grid=(wide // cols,), in_specs=[down, down, a...  32.1 us

profile of v7, /device:TPU:0, one launch (start us, length us, event | category | flops | bytes accessed | tf_op | source)
XLA Modules:
  0.0 453.8 jit_solution(12276963660015614640)
XLA Ops:
  0.7 0.1 pad_maximum_fusion
  0.7 1.3 convert_reduce_fusion
  2.1 1.0 copy.29.first_ref
  3.1 3.0 multiply_sine_fusion
  6.1 95.7 %attn.1 = (f32[128,2048]{1,0:T(8,128)}, bf16[1024,256]{1,0:T(8,128)(2,1)}, bf16[1024,256]{1,0:T(8,128)(2,1)}, bf16[1024,256]{1,0:T(8,128)(2,1)}, f32[1024,256]{1...) custom-call(bf16[128,2048]{1,0:T(8,128)(2,1)} %x_ref.3, ...), custom_call_target="tpu_custom_call" | custom-call | tf_op jit(solution)/shard_map/attn/pallas_call | solution.py:1086
  101.8 186.6 %ffn.1 = (bf16[128,2048]{1,0:T(8,128)(2,1)}, f32[128,2048]{1,0:T(8,128)}, bf16[128,2048]{1,0:T(8,128)(2,1)}, f32[32,128]{1,0:T(8,128)}, bf16[4,8,128,2048]{3,2,1...) custom-call(bf16[128,2048]{1,0:T(8,128)(2,1)} %x_ref.3, ...), custom_call_target="tpu_custom_call" | custom-call | tf_op jit(solution)/shard_map/ffn/pallas_call | solution.py:823
  288.4 131.0 %back.1 = (f32[128,2048]{1,0:T(8,128)}, f32[40,128]{1,0:T(8,128)}, bf16[2,128,2048]{2,1,0:T(8,128)(2,1)}, bf16[4,3,1024,256]{3,2,1,0:T(8,128)(2,1)}, f32[2048,10...) custom-call(bf16[128,2048]{1,0:T(8,128)(2,1)} %get-tuple-element.54.gb_ref, ...), custom_call_target="tpu_custom_call" | custom-call | tf_op jit(solution)/shard_map/back/pallas_call | solution.py:1517
  419.4 0.0 copy-start.1
  419.5 0.0 copy-start
  419.5 32.1 %tail.1 = (f32[2048,1024]{1,0:T(8,128)}, f32[2048,1024]{1,0:T(8,128)}, f32[1024,2048]{1,0:T(8,128)}, f32[2048,256]{1,0:T(8,128)}, f32[2048,256]{1,0:T(8,128)}, /...) custom-call(f32[2048,1024]{1,0:T(8,128)} %get-tuple-element.73.pg_re, ...), custom_call_target="tpu_custom_call" | custom-call | flops 12884901888 | bytes 104857600 | tf_op jit(solution)/shard_map/tail/pallas_call | solution.py:1610
  451.6 0.0 copy-done.1
  451.6 0.8 copy.33
  452.4 0.0 copy-done
  452.4 1.0 copy.34
  (2 shorter events, 0.0 us)
Async XLA Ops:
  419.4 32.1 %copy-start.1 = (bf16[128,2048]{1,0:T(8,128)(2,1)S(1)}, bf16[128,2048]{1,0:T(8,128)(2,1)}, u32[]{:S(2)}) copy-start(bf16[128,2048]{1,0:T(8,128)(2,1)} %get-tuple-element.108) | copy-start | bytes 1572868
  419.5 32.9 %copy-start = (f32[128,2048]{1,0:T(8,128)S(1)}, f32[128,2048]{1,0:T(8,128)}, u32[]{:S(2)}) copy-start(f32[128,2048]{1,0:T(8,128)} %get-tuple-element.109) | copy-start | bytes 3145732
